TPU v7x, 32 devices: a whole 2x2x4 slice. The times are simulated.
32 devices in a mesh: seq: 8 (over z, y), head: 4 (over x, core).
Axes of the slice: x: 2, y: 2, z: 4, core: 2. Of those that a mesh axis runs over, the one named last changes fastest.
Arguments:
- block_input: bfloat16 [3072, 1024], P('seq'), may hold values from -6 to 6
- cotangent: bfloat16 [3072, 1024], P('seq'), may hold values from -6 to 6
- segment_ids: int32 [3072], P('seq'), may hold values from 0 to 98, as said below
- norm_gain: float32 [1024], replicated, may hold values from 0.5 to 1.5
- w_query: bfloat16 [1024, 1024], P(None, 'head'), may hold values from -0.1875 to 0.1875
- w_key: bfloat16 [1024, 1024], P(None, 'head'), may hold values from -0.1875 to 0.1875
- w_value: bfloat16 [1024, 1024], P(None, 'head'), may hold values from -0.1875 to 0.1875
- w_gate: bfloat16 [1024, 1024], P(None, 'head'), may hold values from -0.1875 to 0.1875
- w_beta: bfloat16 [1024, 8], P(None, 'head'), may hold values from -0.1875 to 0.1875
- beta_bias: float32 [8], P('head'), may hold values from -8 to 2
- conv_weight: float32 [3, 4, 1024], P(None, None, 'head'), may hold values from -3 to 3
- head_gain: float32 [128], replicated, may hold values from 0.5 to 1.5
- w_out: bfloat16 [1024, 1024], P('head'), may hold values from -0.375 to 0.375
- ffn_gain: float32 [1024], replicated, may hold values from 0.5 to 1.5
- w_ffn_gate: bfloat16 [1024, 2816], P(None, 'head'), may hold values from -0.1875 to 0.1875
- w_ffn_up: bfloat16 [1024, 2816], P(None, 'head'), may hold values from -0.1875 to 0.1875
- w_ffn_down: bfloat16 [2816, 1024], P('head'), may hold values from -0.21875 to 0.21875
Outputs:
- block_output: bfloat16 [3072, 1024], P('seq')
- input_grad: float32 [3072, 1024], P('seq')
- norm_gain_grad: float32 [1024], replicated
- w_query_grad: float32 [1024, 1024], P('seq', 'head')
- w_key_grad: float32 [1024, 1024], P('seq', 'head')
- w_value_grad: float32 [1024, 1024], P('seq', 'head')
- w_gate_grad: float32 [1024, 1024], P('seq', 'head')
- w_beta_grad: float32 [1024, 8], P('seq', 'head')
- beta_bias_grad: float32 [8], P('head')
- conv_weight_grad: float32 [3, 4, 1024], P(None, None, 'head')
- head_gain_grad: float32 [128], replicated
- w_out_grad: float32 [1024, 1024], P('head', 'seq')
- ffn_gain_grad: float32 [1024], replicated
- w_ffn_gate_grad: float32 [1024, 2816], P('seq', 'head')
- w_ffn_up_grad: float32 [1024, 2816], P('seq', 'head')
- w_ffn_down_grad: float32 [2816, 1024], P('head', 'seq')
Inputs may be any that keep to these rules, and one draw needn't show every extreme that they name: `segment_ids`: segment ids start at 0, never fall and rise by at most one from a token to the next; one document starts within the first 384 tokens and reaches into the last 384 tokens; the others have very unequal lengths.
All inputs are finite; a program needn't handle non-finite values.
Results may differ from a plain program's by a relative error of at most 0.04.
Values may be sent and summed in bfloat16 or wider, within the bound.
No kernel may reach another device: no remote copies, remote signals or barrier semaphores. Data moves between devices by JAX's collectives and lax.ppermute only.
A program may use at most 128 MiB of HBM per device.

v0:
```python
import jax
import jax.numpy as jnp
from jax import lax
from jax.sharding import PartitionSpec as P

HEAD_DIM = 128
SPAN = 64


top_precision = lax.Precision.HIGHEST


def passed_along(value, axis, steps):
    count = lax.axis_size(axis)
    initial, last = (max(0, -steps), min(count, count - steps))
    return lax.ppermute(value, axis, [(source, source + steps) for source in range(initial, last)])


def rms_scale(row_vals, gain_vec):
    return (
        row_vals
        * lax.rsqrt(jnp.mean(row_vals * row_vals, axis=-1, keepdims=True) + 1e-06)
        * gain_vec
    )


def head_scale(mix_out, gate_raw, gain_vec):
    gate_heads = gate_raw.reshape(mix_out.shape)
    scaled = (
        mix_out
        * lax.rsqrt(jnp.mean(mix_out * mix_out, axis=-1, keepdims=True) + 1e-05)
        * gain_vec
        * jax.nn.silu(gate_heads)
    )
    return scaled.reshape(mix_out.shape[0], mix_out.shape[1] * mix_out.shape[2])


def gated_unit(gate_vals, up_vals):
    return jax.nn.silu(gate_vals) * up_vals


def unit_inverse(matrix):
    size_rows = matrix.shape[0]
    row_ids = lax.broadcasted_iota(jnp.int32, (size_rows, size_rows), 0)
    col_ids = lax.broadcasted_iota(jnp.int32, (size_rows, size_rows), 1)
    inverse = jnp.eye(size_rows, dtype=jnp.float32)
    block_width = 1
    while block_width < size_rows:
        within = (row_ids // (2 * block_width) == col_ids // (2 * block_width)) & (
            row_ids // block_width != col_ids // block_width
        )
        coupling = jnp.where(within, matrix, 0.0)
        inverse = inverse - jnp.dot(
            jnp.dot(inverse, coupling, precision=top_precision), inverse, precision=top_precision
        )
        block_width = block_width * 2
    return inverse


def span_step(state, query_rows, key_rows, value_rows, beta_vals, seg_rows, prev_seg):
    size_rows = query_rows.shape[0]
    row_ids = lax.broadcasted_iota(jnp.int32, (size_rows, size_rows), 0)
    col_ids = lax.broadcasted_iota(jnp.int32, (size_rows, size_rows), 1)
    same_doc = (seg_rows[:, None] == seg_rows[None, :]).astype(jnp.float32)
    opened = (seg_rows == prev_seg).astype(jnp.float32)
    closing = (seg_rows == seg_rows[size_rows - 1]).astype(jnp.float32)
    kept_flag = opened[size_rows - 1]
    key_inner = jnp.dot(key_rows, key_rows.T, precision=top_precision) * same_doc
    system = jnp.eye(size_rows, dtype=jnp.float32) + jnp.where(
        row_ids > col_ids, key_inner * beta_vals[:, None], 0.0
    )
    inverse = unit_inverse(system)
    w_rows = jnp.dot(inverse, beta_vals[:, None] * key_rows, precision=top_precision)
    u_rows = jnp.dot(inverse, beta_vals[:, None] * value_rows, precision=top_precision)
    fresh = u_rows - opened[:, None] * jnp.dot(w_rows, state, precision=top_precision)
    scores = jnp.where(
        row_ids >= col_ids, jnp.dot(query_rows, key_rows.T, precision=top_precision) * same_doc, 0.0
    )
    output = opened[:, None] * jnp.dot(query_rows, state, precision=top_precision) + jnp.dot(
        scores, fresh, precision=top_precision
    )
    new_state = kept_flag * state + jnp.dot(
        (closing[:, None] * key_rows).T, fresh, precision=top_precision
    )
    return (new_state, output)


def scan_blocks(queries, key_rows, value_rows, beta_vals, segment_ids, first_prev, start_state):
    block_count = queries.shape[0] // SPAN
    tails = segment_ids[SPAN - 1 :: SPAN]
    prev_ids = jnp.concatenate([jnp.reshape(first_prev, (1,)), tails[: block_count - 1]])

    def blocked(array):
        return array.reshape((block_count, SPAN) + array.shape[1:])

    stepper = jax.vmap(span_step, in_axes=(0, 1, 1, 1, 1, None, None), out_axes=(0, 1))

    def advance(state, inputs):
        q_block, k_block, v_block, b_block, s_block, p_block = inputs
        return stepper(state, q_block, k_block, v_block, b_block, s_block, p_block)

    final_state, outputs = lax.scan(
        jax.checkpoint(advance),
        start_state,
        (
            blocked(queries),
            blocked(key_rows),
            blocked(value_rows),
            blocked(beta_vals),
            blocked(segment_ids),
            prev_ids,
        ),
    )
    return (outputs.reshape(queries.shape), final_state)


def conv_mix(pre_vals, halo_rows, tap_rows, segment_ids, halo_ids):
    row_count = pre_vals.shape[0]
    lag_rows = halo_rows.shape[0]
    joined = jnp.concatenate([halo_rows, pre_vals], axis=0)
    joined_ids = jnp.concatenate([halo_ids, segment_ids], axis=0)
    mixed_sum = jnp.zeros_like(pre_vals)
    for lag_step in range(lag_rows + 1):
        offset = lag_rows - lag_step
        match_doc = (joined_ids[offset : offset + row_count] == segment_ids).astype(jnp.float32)
        mixed_sum = (
            mixed_sum
            + tap_rows[lag_rows - lag_step]
            * joined[offset : offset + row_count]
            * match_doc[:, None]
        )
    return jax.nn.silu(mixed_sum)


def unit_heads(mixed_act, heads_here):
    row_count = mixed_act.shape[0]
    part_width = mixed_act.shape[1] // 3
    query_raw = mixed_act[:, :part_width].reshape(row_count, heads_here, HEAD_DIM)
    key_raw = mixed_act[:, part_width : 2 * part_width].reshape(row_count, heads_here, HEAD_DIM)
    value_rows = mixed_act[:, 2 * part_width :].reshape(row_count, heads_here, HEAD_DIM)
    queries = (
        query_raw
        * lax.rsqrt(jnp.sum(query_raw * query_raw, axis=-1, keepdims=True) + 1e-06)
        * HEAD_DIM ** (-0.5)
    )
    key_rows = key_raw * lax.rsqrt(jnp.sum(key_raw * key_raw, axis=-1, keepdims=True) + 1e-06)
    return (queries, key_rows, value_rows)


def apply_map(matrix, state):
    return jnp.einsum("hij,hjk->hik", matrix, state, precision=top_precision)


def body(
    block_input,
    cotangent,
    segment_ids,
    norm_gain,
    w_query,
    w_key,
    w_value,
    w_gate,
    w_beta,
    beta_bias,
    conv_weight,
    head_gain,
    w_out,
    ffn_gain,
    w_ffn_gate,
    w_ffn_up,
    w_ffn_down,
):
    row_count = block_input.shape[0]
    heads_here = w_beta.shape[1]
    head_width = w_query.shape[1]
    ffn_width = w_ffn_gate.shape[1]
    lag_rows = conv_weight.shape[1] - 1
    inputs = block_input.astype(jnp.float32)
    normed_one, norm_one_back = jax.vjp(rms_scale, inputs, norm_gain)
    normed_one_low = normed_one.astype(jnp.bfloat16)
    w_project = jnp.concatenate([w_query, w_key, w_value, w_gate], axis=1)
    projected = jnp.dot(normed_one_low, w_project, preferred_element_type=jnp.float32)
    pre_low = lax.optimization_barrier(projected[:, : 3 * head_width].astype(jnp.bfloat16))
    pre_vals = pre_low.astype(jnp.float32)
    gate_raw = projected[:, 3 * head_width :]
    beta_vals = jax.nn.sigmoid(
        jnp.dot(normed_one_low, w_beta, preferred_element_type=jnp.float32) + beta_bias
    )
    halo_rows, halo_marks = passed_along(
        (pre_vals[row_count - lag_rows :], segment_ids[row_count - lag_rows :].astype(jnp.float32)),
        "seq",
        1,
    )
    halo_ids = halo_marks.astype(jnp.int32)
    tap_rows = jnp.transpose(conv_weight, (1, 0, 2)).reshape(lag_rows + 1, 3 * head_width)

    def conv_heads(pre_in, halo_in, taps_in):
        return unit_heads(conv_mix(pre_in, halo_in, taps_in, segment_ids, halo_ids), heads_here)

    (queries, key_rows, value_rows), conv_back = jax.vjp(conv_heads, pre_vals, halo_rows, tap_rows)
    first_prev = halo_ids[lag_rows - 1]

    def local_run(query_in, key_in, value_in, beta_in, start_in):
        return scan_blocks(query_in, key_in, value_in, beta_in, segment_ids, first_prev, start_in)

    zero_state = jnp.zeros((heads_here, HEAD_DIM, HEAD_DIM), jnp.float32)
    unit_state = jnp.broadcast_to(jnp.eye(HEAD_DIM, dtype=jnp.float32), zero_state.shape)
    carry_mult = local_run(queries, key_rows, jnp.zeros_like(value_rows), beta_vals, unit_state)[1]
    carry_add = local_run(queries, key_rows, value_rows, beta_vals, zero_state)[1]

    def relay_fwd(turn_index, carry_pair):
        incoming = passed_along(carry_pair[1].astype(jnp.bfloat16), "seq", 1).astype(jnp.float32)
        return (incoming, apply_map(carry_mult, incoming) + carry_add)

    state_in = lax.fori_loop(0, lax.axis_size("seq") - 1, relay_fwd, (zero_state, carry_add))[0]
    (mix_out, state_out), delta_back = jax.vjp(
        local_run, queries, key_rows, value_rows, beta_vals, state_in
    )
    head_mixed, head_back = jax.vjp(head_scale, mix_out, gate_raw, head_gain)
    head_low = head_mixed.astype(jnp.bfloat16)
    attention = lax.psum(
        jnp.dot(head_low, w_out, preferred_element_type=jnp.float32).astype(jnp.bfloat16), "head"
    ).astype(jnp.float32)
    residual = inputs + attention
    normed_two, norm_two_back = jax.vjp(rms_scale, residual, ffn_gain)
    normed_two_low = normed_two.astype(jnp.bfloat16)
    w_ffn = jnp.concatenate([w_ffn_gate, w_ffn_up], axis=1)
    gate_up = jnp.dot(normed_two_low, w_ffn, preferred_element_type=jnp.float32)
    hidden, gated_back = jax.vjp(gated_unit, gate_up[:, :ffn_width], gate_up[:, ffn_width:])
    hidden_low = hidden.astype(jnp.bfloat16)
    ffn_out = lax.psum(
        jnp.dot(hidden_low, w_ffn_down, preferred_element_type=jnp.float32).astype(jnp.bfloat16),
        "head",
    ).astype(jnp.float32)
    block_output = (residual + ffn_out).astype(jnp.bfloat16)
    grad_down = jnp.einsum("tf,td->fd", hidden_low, cotangent, preferred_element_type=jnp.float32)
    grad_hidden = jnp.einsum("td,fd->tf", cotangent, w_ffn_down, preferred_element_type=jnp.float32)
    grad_gate, grad_up = gated_back(grad_hidden)
    grad_gu_low = jnp.concatenate([grad_gate, grad_up], axis=1).astype(jnp.bfloat16)
    grad_w_ffn = jnp.einsum(
        "td,tf->df", normed_two_low, grad_gu_low, preferred_element_type=jnp.float32
    )
    grad_two_part = jnp.einsum("tf,df->td", grad_gu_low, w_ffn, preferred_element_type=jnp.float32)
    grad_normed_two = lax.psum(grad_two_part.astype(jnp.bfloat16), "head").astype(jnp.float32)
    grad_resid_norm, grad_ffn_gain = norm_two_back(grad_normed_two)
    grad_resid = cotangent.astype(jnp.float32) + grad_resid_norm
    grad_attn_low = grad_resid.astype(jnp.bfloat16)
    grad_w_out = jnp.einsum(
        "tw,td->wd", head_low, grad_attn_low, preferred_element_type=jnp.float32
    )
    grad_head = jnp.einsum("td,wd->tw", grad_attn_low, w_out, preferred_element_type=jnp.float32)
    grad_mix_out, grad_gate_raw, grad_head_gain = head_back(grad_head)
    local_pull = delta_back((grad_mix_out, zero_state))[4]
    pull_mult = jnp.transpose(carry_mult, (0, 2, 1))

    def relay_back(turn_index, carry_pair):
        incoming = passed_along(carry_pair[1].astype(jnp.bfloat16), "seq", -1).astype(jnp.float32)
        return (incoming, apply_map(pull_mult, incoming) + local_pull)

    state_grad = lax.fori_loop(0, lax.axis_size("seq") - 1, relay_back, (zero_state, local_pull))[0]
    grad_query, grad_key, grad_value, grad_beta, grad_start = delta_back((grad_mix_out, state_grad))
    grad_pre, grad_halo, grad_taps = conv_back((grad_query, grad_key, grad_value))
    from_next = passed_along(grad_halo, "seq", -1)
    grad_pre = grad_pre + jnp.pad(from_next, ((row_count - lag_rows, 0), (0, 0)))
    grad_beta_raw = grad_beta * beta_vals * (1.0 - beta_vals)
    grad_bias_local = jnp.sum(grad_beta_raw, axis=0)
    grad_beta_low = grad_beta_raw.astype(jnp.bfloat16)
    grad_proj_low = jnp.concatenate([grad_pre, grad_gate_raw], axis=1).astype(jnp.bfloat16)
    grad_w_project = jnp.einsum(
        "td,tp->dp", normed_one_low, grad_proj_low, preferred_element_type=jnp.float32
    )
    grad_w_beta = jnp.einsum(
        "td,th->dh", normed_one_low, grad_beta_low, preferred_element_type=jnp.float32
    )
    grad_one_part = jnp.einsum(
        "tp,dp->td", grad_proj_low, w_project, preferred_element_type=jnp.float32
    )
    grad_one_part = grad_one_part + jnp.einsum(
        "th,dh->td", grad_beta_low, w_beta, preferred_element_type=jnp.float32
    )
    grad_normed_one, grad_head_gain_all = (
        lax.psum(grad_one_part.astype(jnp.bfloat16), "head").astype(jnp.float32),
        lax.psum(grad_head_gain.astype(jnp.bfloat16), "head").astype(jnp.float32),
    )
    grad_inputs_norm, grad_norm_gain = norm_one_back(grad_normed_one)
    input_grad = grad_resid + grad_inputs_norm
    project_share, beta_share, out_share, ffn_share, down_share = (
        lax.psum_scatter(
            grad_w_project.astype(jnp.bfloat16), "seq", scatter_dimension=0, tiled=True
        ).astype(jnp.float32),
        lax.psum_scatter(
            grad_w_beta.astype(jnp.bfloat16), "seq", scatter_dimension=0, tiled=True
        ).astype(jnp.float32),
        lax.psum_scatter(
            grad_w_out.astype(jnp.bfloat16), "seq", scatter_dimension=1, tiled=True
        ).astype(jnp.float32),
        lax.psum_scatter(
            grad_w_ffn.astype(jnp.bfloat16), "seq", scatter_dimension=0, tiled=True
        ).astype(jnp.float32),
        lax.psum_scatter(
            grad_down.astype(jnp.bfloat16), "seq", scatter_dimension=1, tiled=True
        ).astype(jnp.float32),
    )
    grad_conv = jnp.transpose(grad_taps.reshape(lag_rows + 1, 3, head_width), (1, 0, 2))
    conv_total, norm_total, ffn_gain_total, head_gain_total, bias_total = lax.psum(
        (grad_conv, grad_norm_gain, grad_ffn_gain, grad_head_gain_all, grad_bias_local), "seq"
    )
    return (
        block_output,
        input_grad,
        norm_total,
        project_share[:, :head_width],
        project_share[:, head_width : 2 * head_width],
        project_share[:, 2 * head_width : 3 * head_width],
        project_share[:, 3 * head_width :],
        beta_share,
        bias_total,
        conv_total,
        head_gain_total,
        out_share,
        ffn_gain_total,
        ffn_share[:, :ffn_width],
        ffn_share[:, ffn_width:],
        down_share,
    )


def solution(mesh):
    return jax.shard_map(
        body,
        mesh=mesh,
        in_specs=(
            P("seq", None),
            P("seq", None),
            P("seq"),
            P(),
            P(None, "head"),
            P(None, "head"),
            P(None, "head"),
            P(None, "head"),
            P(None, "head"),
            P("head"),
            P(None, None, "head"),
            P(),
            P("head", None),
            P(),
            P(None, "head"),
            P(None, "head"),
            P("head", None),
        ),
        out_specs=(
            P("seq", None),
            P("seq", None),
            P(),
            P("seq", "head"),
            P("seq", "head"),
            P("seq", "head"),
            P("seq", "head"),
            P("seq", "head"),
            P("head"),
            P(None, None, "head"),
            P(),
            P("head", "seq"),
            P(),
            P("seq", "head"),
            P("seq", "head"),
            P("head", "seq"),
        ),
        check_vma=False,
    )
```

profile of v0, /device:TPU:0, one launch (start us, length us, event | category | flops | bytes accessed | tf_op | source)
XLA Modules:
  0.0 1092.4 jit_solution(16224338973624770034)
XLA Ops:
  8.7 5.5 collective-permute-start.2
  42.6 56.4 %while.113 = (s32[]{:T(128)}, f32[2,128,128]{2,1,0:T(8,128)S(1)}, s32[6,64]{1,0:T(8,128)}, s32[6]{0:T(128)}, f32[6,64,2,128]{3,1,2,0:T(8,128)S(1)}, /*index=5*/f...) while((s32[]{:T(128)}, f32[2,128,128]{2,1,0:T(8,128)S(1)}, ...), condition=%wide.region_3.4_spmd.clone, body=%wide.region_2.3_spmd.clone.sunk | while | flops 164076416 | bytes 2582700 | solution.py:102
  99.7 56.0 %while.108 = (s32[]{:T(128)}, f32[2,128,128]{2,1,0:T(8,128)S(1)}, s32[6,64]{1,0:T(8,128)}, s32[6]{0:T(128)}, f32[6,64,2,128]{3,1,2,0:T(8,128)S(1)}, /*index=5*/f32[6,64,2]{1,2,0:T(2,128)S(1)}, s32[]{:T(128)}) while((s32[]{:T(128)}, f32[2,128,128]{2,1,0:T(8,128)S(1)}, s32[6,64]{1,0:T(8,128)}, s32[6]{0:T(128)}, f32[6,64,2,128]{3,1,2,0:T(8,128)S(1)}, ...), condition=%wide.region_5.6_spmd, body=%wide.region_4.5_spmd.sunk | while | flops 163994624 | bytes 2484365 | solution.py:102
  160.0 52.4 %while.109 = (s32[]{:T(128)}, f32[2,128,128]{2,1,0:T(8,128)}, bf16[2,128,128]{2,1,0:T(8,128)(2,1)S(1)}, f32[2,128,128]{2,1,0:T(8,128)S(1)}, f32[2,128,128]{2,1,0:T(8,128)S(1)}, /*index=5*/s32[]{:T(128)}) while((s32[]{:T(128)}, f32[2,128,128]{2,1,0:T(8,128)}, bf16[2,128,128]{2,1,0:T(8,128)(2,1)S(1)}, f32[2,128,128]{2,1,0:T(8,128)S(1)}, ...), condition=%wide.region_7.8_spmd, body=%wide.region_6.7_spmd.sunk | while | flops 50429952 | bytes 852077 | solution.py:215
  196.3 5.3 collective-permute-start
  212.5 85.2 %while.112 = (s32[]{:T(128)}, f32[2,128,128]{2,1,0:T(8,128)}, f32[6,64,2,128]{3,1,2,0:T(8,128)S(1)}, f32[6,2,128,128]{3,2,1,0:T(8,128)}, s32[6,64]{1,0:T(8,128)}...) while((s32[]{:T(128)}, f32[2,128,128]{2,1,0:T(8,128)}, ...), condition=%wide.region_10.11_spmd.clone.clone, body=%wide.region_9.10_spmd.clone.clone.sunk | while | flops 214270208 | bytes 4555061 | solution.py:102
  307.8 33.4 %all-reduce.18.cloned.1.call-done = bf16[384,1024]{1,0:T(8,128)(2,1)} async-done(((bf16[384,1024]{1,0:T(8,128)(2,1)}), bf16[384,1024]{1,0:T(8,128)(2,1)}) %all-reduce.18.cloned.1.call-update) | async-done | bytes 786448 | tf_op jit(solution)/shard_map/psum | solution.py:221
  357.1 31.1 %all-reduce.20.cloned.1.call-done = bf16[384,1024]{1,0:T(8,128)(2,1)} async-done(((bf16[384,1024]{1,0:T(8,128)(2,1)}), bf16[384,1024]{1,0:T(8,128)(2,1)}) %all-reduce.20.cloned.1.call-update) | async-done | bytes 786448 | tf_op jit(solution)/shard_map/psum | solution.py:244
  401.6 70.3 %while.114 = (s32[]{:T(128)}, f32[2,128,128]{2,1,0:T(8,128)S(1)}, f32[6,64,2,128]{3,1,2,0:T(8,128)}, f32[6,64,2,128]{3,1,2,0:T(8,128)S(1)}, f32[6,64,2]{1,2,0:T(...) while((s32[]{:T(128)}, f32[2,128,128]{2,1,0:T(8,128)S(1)}, ...), condition=%wide.region_19.20_spmd.clone, body=%wide.region_18.19_spmd.clone.sunk | while | flops 201862016 | bytes 3648707 | solution.py:102
  472.5 54.7 %while.110 = (s32[]{:T(128)}, f32[2,128,128]{2,1,0:T(8,128)}, bf16[2,128,128]{2,1,0:T(8,128)(2,1)S(1)}, f32[2,128,128]{2,1,0:T(8,128)S(1)}, f32[2,128,128]{2,1,0:T(8,128)S(1)}, /*index=5*/s32[]{:T(128)}) while((s32[]{:T(128)}, f32[2,128,128]{2,1,0:T(8,128)}, bf16[2,128,128]{2,1,0:T(8,128)(2,1)S(1)}, f32[2,128,128]{2,1,0:T(8,128)S(1)}, ...), condition=%wide.region_21.22_spmd, body=%wide.region_20.21_spmd.sunk | while | flops 50429952 | bytes 852077 | solution.py:260
  488.3 5.8 collective-permute-done.1
  496.2 5.8 collective-permute-done.1
  504.1 6.0 collective-permute-done.1
  512.4 6.1 collective-permute-done.1
  520.7 5.6 collective-permute-done.1
  528.9 149.7 %while.111 = (s32[]{:T(128)}, f32[2,128,128]{2,1,0:T(8,128)}, f32[6,64,2,128]{3,1,2,0:T(8,128)S(1)}, f32[6,64,2,128]{3,1,2,0:T(8,128)}, f32[6,64,2,128]{3,2,1,0:...) while((s32[]{:T(128)}, f32[2,128,128]{2,1,0:T(8,128)}, ...), condition=%wide.region_26.27_spmd, body=%wide.region_22.26_spmd.sunk | while | flops 567454464 | bytes 10477849 | solution.py:102
  719.0 6.1 psum.77
  725.1 34.7 %reduce-scatter.16.cloned.1.call-done = bf16[128,2]{1,0:T(8,128)(2,1)} async-done(((bf16[1024,2]{1,0:T(8,128)(2,1)}), bf16[128,2]{1,0:T(8,128)(2,1)}) %reduce-scatter.16.cloned.1.call-update) | async-done | bytes 528
  761.2 43.5 %all-reduce.22.cloned.1.call-done = (bf16[384,1024]{1,0:T(8,128)(2,1)}, bf16[384,1024]{1,0:T(8,128)(2,1)}) async-done(((bf16[384,1024]{1,0:T(8,128)(2,1)}, bf16[384,1024]{1,0:T(8,128)(2,1)}), (bf16[384,1024]{1,0:T(8,128)(2,1)}, bf16[384,1024]{1,0:T(8,128)(2,1)})) %all-reduce.22.cloned.1.call-update) | async-done | bytes 1572880 | tf_op jit(solution)/shard_map/psum | solution.py:231
  806.5 37.8 %all-reduce.12 = (f32[1024]{0:T(1024)}, f32[2]{0:T(128)}, f32[3,4,256]{2,1,0:T(4,128)}, f32[128]{0:T(128)}, f32[1024]{0:T(1024)}) all-reduce(f32[1024]{0:T(1024)S(1)} %get-tuple-element.1665, f32[2]{0:T(128)S(1)} %get-tuple-element.1816, f32[3,4,256]{2,1,0:T(4,128)S(1)} %bitcast.1099, ...), channel_id=1, replica_groups=mesh['seq'=8,'head'=4] {'seq'}, use_global_device_ids=true, to_apply=%region_32.33 | all-reduce | flops 5250 | bytes 41744 | tf_op jit(solution)/shard_map/psum | solution.py:305
  848.0 22.0 %reduce-scatter.18.cloned.1.call-done = bf16[128,256]{1,0:T(8,128)(2,1)} async-done(((bf16[1024,256]{1,0:T(8,128)(2,1)}), bf16[128,256]{1,0:T(8,128)(2,1)}) %reduce-scatter.18.cloned.1.call-update) | async-done | bytes 65552
  871.6 65.9 %reduce-scatter.20.cloned.1.call-done = bf16[128,704]{1,0:T(8,128)(2,1)} async-done(((bf16[1024,704]{1,0:T(8,128)(2,1)}), bf16[128,704]{1,0:T(8,128)(2,1)}) %reduce-scatter.20.cloned.1.call-update) | async-done | bytes 180240
  939.4 68.3 %reduce-scatter.12.cloned.1.call-done = bf16[128,1024]{1,0:T(8,128)(2,1)} async-done(((bf16[1024,1024]{1,0:T(8,128)(2,1)}), bf16[128,1024]{1,0:T(8,128)(2,1)}) %reduce-scatter.12.cloned.1.call-update) | async-done | bytes 262160 | tf_op jit(solution)/shard_map/reduce_scatter | solution.py:288
  1009.6 72.6 %reduce-scatter.14.cloned.1.call-done = bf16[128,1408]{1,0:T(8,128)(2,1)} async-done(((bf16[1024,1408]{1,0:T(8,128)(2,1)}), bf16[128,1408]{1,0:T(8,128)(2,1)}) %reduce-scatter.14.cloned.1.call-update) | async-done | bytes 360464 | tf_op jit(solution)/shard_map/reduce_scatter | solution.py:297
  (1786 shorter events, 610.6 us)
Async XLA Ops:
  7.2 333.9 %all-reduce.18.cloned.1.call-start = ((), (), s32[]{:S(2)}) async-start(), calls=%async_computation.5 | async-start | bytes 1572864 | tf_op jit(solution)/shard_map/psum | solution.py:221
  8.7 17.0 %collective-permute-start.2 = (f32[3]{0:T(128)}, f32[3]{0:T(128)}, u32[]{:S(2)}, u32[]{:S(2)}) collective-permute-start(f32[3]{0:T(128)} %slice_convert_fusion.1), channel_id=1, source_target_pairs={{0,4},{4,8},{8,12},{12,16},{16,20},{20,24},{24,28},{1,5},{5,9},{9,... | collective-permute-start | bytes 44 | tf_op jit(solution)/shard_map/ppermute | solution.py:16
  19.1 9.1 collective-permute-start.3
  166.2 6.2 collective-permute-start
  173.3 6.2 collective-permute-start
  180.4 7.1 collective-permute-start
  188.3 7.1 collective-permute-start
  196.3 7.4 collective-permute-start
  204.5 7.0 collective-permute-start
  303.6 84.6 %all-reduce.20.cloned.1.call-start = ((), (), s32[]{:S(2)}) async-start(), calls=%async_computation.6 | async-start | bytes 1572864 | tf_op jit(solution)/shard_map/psum | solution.py:244
  353.4 406.5 %reduce-scatter.16.cloned.1.call-start = ((), (), s32[]{:S(2)}) async-start(), calls=%async_computation.9 | async-start | bytes 294912
  472.5 6.1 collective-permute-start.1
  479.5 6.5 collective-permute-start.1
  487.0 7.1 collective-permute-start.1
  494.9 7.1 collective-permute-start.1
  502.9 7.3 collective-permute-start.1
  511.1 7.4 collective-permute-start.1
  519.4 6.9 collective-permute-start.1
  689.2 6.7 collective-permute-start.4
  695.9 108.9 %all-reduce.22.cloned.1.call-start = ((), (), s32[]{:S(2)}) async-start(), calls=%async_computation.12 | async-start | bytes 3145728 | tf_op jit(solution)/shard_map/psum | solution.py:231
  701.6 168.4 %reduce-scatter.18.cloned.1.call-start = ((), (), s32[]{:S(2)}) async-start(), calls=%async_computation.10 | async-start | bytes 589824
  703.3 234.2 %reduce-scatter.20.cloned.1.call-start = ((), (), s32[]{:S(2)}) async-start(), calls=%async_computation.11 | async-start | bytes 1769472
  709.3 298.4 %reduce-scatter.12.cloned.1.call-start = ((), (), s32[]{:S(2)}) async-start(), calls=%async_computation.7 | async-start | bytes 2359296 | tf_op jit(solution)/shard_map/reduce_scatter | solution.py:288
  713.1 369.0 %reduce-scatter.14.cloned.1.call-start = ((), (), s32[]{:S(2)}) async-start(), calls=%async_computation.8 | async-start | bytes 3244032 | tf_op jit(solution)/shard_map/reduce_scatter | solution.py:297
  (108 other events, 931.1 us)
Sparse Core Ops, SparseCore 0:
  303.7 37.3 all-reduce.17
  353.5 34.6 all-reduce.19
  696.0 63.7 reduce-scatter.15
  762.6 42.0 all-reduce.21
  807.9 62.0 reduce-scatter.17
  873.7 63.8 reduce-scatter.19
  941.1 66.6 reduce-scatter.11
  1011.3 70.8 reduce-scatter.13
where the time goes:
time: 1100 us; the launch traced here: 1090 us
  waiting for transfers between devices  424 us (39%)
  matrix products  262 us (24%)
  local copies, waits for them, and re-layouts  173 us (16%)
  other arithmetic  111 us (10%)
  starting transfers between devices  52 us (5%)
  blocking collectives  43.9 us (4%)
  between operations  16.1 us (1%)
    unnamed x11, waiting for transfers between devices  123 us
    reduce_scatter x1, waiting for transfers between devices, body(): lax.psum_scatter(grad_w_ffn.astype(jnp.bfloat16), 'seq', scatter_dimensio...  72.6 us
    reduce_scatter x1, waiting for transfers between devices, body(): lax.psum_scatter(grad_w_project.astype(jnp.bfloat16), 'seq', scatter_dime...  68.3 us
    ppermute x17, waiting for transfers between devices, passed_along(): lax.ppermute(value, axis, [(source, source + steps) for source in range(i...  52.7 us
    dot_general x246, matrix products, unit_inverse(): jnp.dot(inverse, coupling, precision=top_precision)  52.2 us
    ppermute x17, starting transfers between devices, passed_along(): lax.ppermute(value, axis, [(source, source + steps) for source in range(i...  51.5 us
    dot_general x246, matrix products, unit_inverse(): jnp.dot(jnp.dot(inverse, coupling, precision=top_precision), inverse, pre...  51.5 us
    psum x1, waiting for transfers between devices, body(): lax.psum(jnp.dot(hidden_low, w_ffn_down, preferred_element_type=jnp.float...  43.5 us
  transfers between devices with their start and end apart: 25, of which 22 were waited for; matrix products, arithmetic and copies ran while one was open for 5% of the time, Pallas kernels for 0%

commit v1 on v0

v1 whole, which is shorter than its diff:
```python
import functools

import jax
import jax.numpy as jnp
from jax import lax
from jax.experimental import pallas as pl
from jax.experimental.pallas import tpu as pltpu
from jax.sharding import PartitionSpec as P

HEAD_DIM = 128
CHUNK = 128
LANES = 128
SUB = 8
Q_SCALE = HEAD_DIM ** (-0.5)
VMEM_BYTES = 56 * 1024 * 1024

bf16 = jnp.bfloat16
f32 = jnp.float32


def mm(left, right, left_dim=1, right_dim=0):
    return lax.dot_general(
        left.astype(bf16),
        right.astype(bf16),
        (((left_dim,), (right_dim,)), ((), ())),
        preferred_element_type=f32,
    )


def sigmoid(value):
    return 1.0 / (1.0 + jnp.exp(-value))


def kernel_call(body, out_shapes, *args, scratch=(), name, flops=0):
    vmem = pl.BlockSpec(memory_space=pltpu.VMEM)
    smem = pl.BlockSpec(memory_space=pltpu.SMEM)
    moved = sum(a.size * a.dtype.itemsize for a in args)
    moved += sum(o.size * o.dtype.itemsize for o in out_shapes)
    return pl.pallas_call(
        body,
        out_shape=tuple(out_shapes),
        in_specs=[smem] + [vmem] * (len(args) - 1),
        out_specs=tuple([vmem] * len(out_shapes)),
        scratch_shapes=list(scratch),
        compiler_params=pltpu.CompilerParams(vmem_limit_bytes=VMEM_BYTES),
        cost_estimate=pl.CostEstimate(flops=int(flops), bytes_accessed=int(moved), transcendentals=0),
        name=name,
    )(*args)


def shaped(shape, dtype):
    return jax.ShapeDtypeStruct(tuple(shape), dtype)


def swap(value, axis, bit):
    count = lax.axis_size(axis)
    return lax.ppermute(value, axis, [(s, s ^ bit) for s in range(count)])


def shift(value, axis, step):
    count = lax.axis_size(axis)
    return lax.ppermute(
        value, axis, [(s, s + step) for s in range(count) if 0 <= s + step < count]
    )


def bit_of(place_ref, which, bit):
    return lax.rem(lax.shift_right_logical(place_ref[which], bit), 2)


def chosen(flag, when_one, when_zero):
    return jnp.where(flag == 1, when_one, when_zero)


def tri_masks():
    rows = lax.broadcasted_iota(jnp.int32, (CHUNK, CHUNK), 0)
    cols = lax.broadcasted_iota(jnp.int32, (CHUNK, CHUNK), 1)
    return rows, cols


def unit_inverses(lowers):
    rows, cols = tri_masks()
    eye = jnp.where(rows == cols, 1.0, 0.0).astype(f32)
    width = 1
    inverses = None
    while width < CHUNK:
        shift_bits = width.bit_length() - 1
        row_block = lax.shift_right_logical(rows, shift_bits)
        col_block = lax.shift_right_logical(cols, shift_bits)
        within = (
            lax.shift_right_logical(row_block, 1) == lax.shift_right_logical(col_block, 1)
        ) & (row_block != col_block)
        couplings = [jnp.where(within, low, 0.0) for low in lowers]
        if inverses is None:
            inverses = [eye - coupling for coupling in couplings]
        else:
            halves = [mm(inv, coupling) for inv, coupling in zip(inverses, couplings)]
            inverses = [inv - mm(half, inv) for inv, half in zip(inverses, halves)]
        width *= 2
    return inverses


def project_kernel(
    place, x_ref, gain_ref, wq_ref, wk_ref, wv_ref, wg_ref, wb_ref, bias_ref, seg_ref,
    a_ref, p_ref, gate_ref, beta_ref, segc_ref, tail_ref,
):
    rows = x_ref.shape[0]
    head_width = wq_ref.shape[1]
    x = x_ref[...].astype(f32)
    scale = lax.rsqrt(jnp.mean(x * x, axis=-1, keepdims=True) + 1e-06)
    a = (x * scale * gain_ref[...]).astype(bf16)
    a_ref[...] = a
    for part, w_ref in enumerate((wq_ref, wk_ref, wv_ref)):
        value = mm(a, w_ref[...])
        cols = slice(part * head_width, (part + 1) * head_width)
        low = value.astype(bf16)
        p_ref[:, cols] = low
        tail_ref[:, cols] = low.astype(f32)[rows - SUB :, :]
    gate_ref[...] = mm(a, wg_ref[...])
    logits = mm(a, wb_ref[...])
    for head in range(head_width // LANES):
        column = logits[:, head : head + 1] + bias_ref[:, head : head + 1]
        beta_ref[:, head * LANES : (head + 1) * LANES] = sigmoid(
            jnp.broadcast_to(column, (rows, LANES))
        )
    for chunk in range(rows // CHUNK):
        ids = jnp.broadcast_to(seg_ref[chunk : chunk + 1, :], (CHUNK, LANES))
        turned = ids.T
        segc_ref[chunk * CHUNK : (chunk + 1) * CHUNK, :] = turned
        if chunk == rows // CHUNK - 1:
            tail_ref[:, 3 * head_width :] = turned[CHUNK - SUB :, :]


def fill_joined(p_ref, tail_ref, segc_ref, joined, joined_ids):
    width = p_ref.shape[1]
    rows = p_ref.shape[0]
    joined[0:SUB, :] = tail_ref[:, :width]
    joined[SUB : SUB + rows, :] = p_ref[...].astype(f32)
    joined_ids[0:SUB, :] = tail_ref[:, width:]
    joined_ids[SUB : SUB + rows, :] = segc_ref[...]


def lag_masks(joined_ids, segc_ref, lags):
    rows = segc_ref.shape[0]
    ids = segc_ref[...]
    return [None] + [
        jnp.where(joined_ids[SUB - lag : SUB - lag + rows, :] == ids, 1.0, 0.0)
        for lag in range(1, lags + 1)
    ]


def conv_sum(joined, taps_ref, masks, part, head, head_width, rows):
    lags = taps_ref.shape[1] - 1
    col = part * head_width + head * LANES
    tap_cols = slice(head * LANES, (head + 1) * LANES)
    total = taps_ref[part, lags : lags + 1, tap_cols] * joined[SUB : SUB + rows, col : col + LANES]
    for lag in range(1, lags + 1):
        tap = taps_ref[part, lags - lag : lags - lag + 1, tap_cols]
        total = total + tap * joined[SUB - lag : SUB - lag + rows, col : col + LANES] * masks[lag]
    return total


def chunk_flags(joined_ids, segc_ref, seg_ref, chunk):
    start = chunk * CHUNK
    ids = segc_ref[start : start + CHUNK, :]
    same = jnp.where(ids == seg_ref[chunk : chunk + 1, :], 1.0, 0.0)
    before = joined_ids[SUB + start - 1 : SUB + start, :]
    final = joined_ids[SUB + start + CHUNK - 1 : SUB + start + CHUNK, :]
    opened = jnp.where(ids == before, 1.0, 0.0)
    closing = jnp.where(ids == final, 1.0, 0.0)
    kept = jnp.where(final == before, 1.0, 0.0)
    return same, opened, closing, kept


def delta_kernel(
    place, p_ref, tail_ref, taps_ref, seg_ref, segc_ref, beta_ref,
    qkv_ref, w_ref, u_ref, qe_ref, pu_ref, r_ref, s_ref, d_ref, ku_ref, maps_ref,
    joined, joined_ids,
):
    rows, width = p_ref.shape
    head_width = width // 3
    heads = head_width // LANES
    chunks = rows // CHUNK
    fill_joined(p_ref, tail_ref, segc_ref, joined, joined_ids)
    masks = lag_masks(joined_ids, segc_ref, taps_ref.shape[1] - 1)
    for part in range(3):
        for head in range(heads):
            total = conv_sum(joined, taps_ref, masks, part, head, head_width, rows)
            z = total * sigmoid(total)
            if part < 2:
                z = z * lax.rsqrt(jnp.sum(z * z, axis=-1, keepdims=True) + 1e-06)
                if part == 0:
                    z = z * Q_SCALE
            col = part * head_width + head * LANES
            qkv_ref[:, col : col + LANES] = z.astype(bf16)
    row_ids, col_ids = tri_masks()
    flags = [chunk_flags(joined_ids, segc_ref, seg_ref, chunk) for chunk in range(chunks)]
    sets = [(head, chunk) for head in range(heads) for chunk in range(chunks)]

    def tile(ref, head, chunk, part=0):
        col = part * head_width + head * LANES
        return ref[chunk * CHUNK : (chunk + 1) * CHUNK, col : col + LANES]

    lowers = []
    for head, chunk in sets:
        same = flags[chunk][0]
        q, k = tile(qkv_ref, head, chunk, 0), tile(qkv_ref, head, chunk, 1)
        inner = mm(jnp.concatenate([q, k], axis=0), k, 1, 1)
        scores = jnp.where(row_ids >= col_ids, inner[:CHUNK] * same, 0.0)
        s_ref[chunk * CHUNK : (chunk + 1) * CHUNK, head * LANES : (head + 1) * LANES] = (
            scores.astype(bf16)
        )
        lowers.append(
            jnp.where(row_ids > col_ids, inner[CHUNK:] * same * tile(beta_ref, head, chunk), 0.0)
        )
    inverses = unit_inverses(lowers)
    eye = jnp.where(row_ids == col_ids, 1.0, 0.0).astype(f32)
    maps = [
        jnp.concatenate([eye, jnp.zeros((HEAD_DIM, HEAD_DIM), f32)], axis=1) for _ in range(heads)
    ]
    products = []
    for (head, chunk), inverse in zip(sets, inverses):
        beta = tile(beta_ref, head, chunk)
        k = tile(qkv_ref, head, chunk, 1).astype(f32)
        v = tile(qkv_ref, head, chunk, 2).astype(f32)
        both = jnp.concatenate([beta * k, beta * v], axis=1)
        products.append(mm(inverse, both))
    steps = {}
    for (head, chunk), inverse, product in zip(sets, inverses, products):
        same, opened, closing, kept = flags[chunk]
        at = (slice(chunk * CHUNK, (chunk + 1) * CHUNK), slice(head * LANES, (head + 1) * LANES))
        w_rows, u_rows = product[:, :HEAD_DIM], product[:, HEAD_DIM:]
        r_ref[at] = inverse.astype(bf16)
        w_ref[at] = w_rows.astype(bf16)
        u_ref[at] = u_rows.astype(bf16)
        both = jnp.concatenate([opened * w_rows, u_rows], axis=1)
        k = tile(qkv_ref, head, chunk, 1).astype(f32)
        q = tile(qkv_ref, head, chunk, 0).astype(f32)
        step = mm(closing * k, both, 0, 0)
        through = mm(s_ref[at], both)
        qe_ref[at] = (opened * q - through[:, :HEAD_DIM]).astype(bf16)
        pu_ref[at] = through[:, HEAD_DIM:].astype(bf16)
        d_ref[at] = step[:, :HEAD_DIM].astype(bf16)
        ku_ref[at] = step[:, HEAD_DIM:].astype(bf16)
        steps[head, chunk] = step
    for chunk in range(chunks):
        kept = flags[chunk][3]
        kept_wide = jnp.concatenate([kept, kept], axis=1)
        for head in range(heads):
            step = steps[head, chunk]
            pushed = kept_wide * maps[head] - mm(step[:, :HEAD_DIM], maps[head])
            maps[head] = jnp.concatenate(
                [pushed[:, :HEAD_DIM], pushed[:, HEAD_DIM:] + step[:, HEAD_DIM:]], axis=1
            )
    for head in range(heads):
        maps_ref[head * HEAD_DIM : (head + 1) * HEAD_DIM, :] = maps[head][:, :HEAD_DIM].astype(bf16)
        base = (heads + head) * HEAD_DIM
        maps_ref[base : base + HEAD_DIM, :] = maps[head][:, HEAD_DIM:].astype(bf16)


def scan_round_kernel(
    bit, first, place, own_ref, other_ref, prefix_ref, suffix_ref, total_ref, prefix_out, suffix_out
):
    upper = bit_of(place, 0, bit)
    heads = own_ref.shape[0] // (2 * HEAD_DIM)
    for head in range(heads):
        m_at = slice(head * HEAD_DIM, (head + 1) * HEAD_DIM)
        a_at = slice((heads + head) * HEAD_DIM, (heads + head + 1) * HEAD_DIM)
        own_m, own_a = own_ref[m_at, :].astype(f32), own_ref[a_at, :].astype(f32)
        other_m, other_a = other_ref[m_at, :].astype(f32), other_ref[a_at, :].astype(f32)
        high_m, high_a = chosen(upper, own_m, other_m), chosen(upper, own_a, other_a)
        low_m, low_a = chosen(upper, other_m, own_m), chosen(upper, other_a, own_a)
        total = mm(high_m, jnp.concatenate([low_m, low_a], axis=1))
        total_ref[m_at, :] = total[:, :HEAD_DIM].astype(bf16)
        total_ref[a_at, :] = (total[:, HEAD_DIM:] + high_a).astype(bf16)
        if first:
            rows, cols = tri_masks()
            eye = jnp.where(rows == cols, 1.0, 0.0).astype(f32)
            prefix_out[m_at, :] = chosen(upper, other_m, eye).astype(bf16)
            prefix_out[a_at, :] = chosen(upper, other_a, jnp.zeros_like(other_a)).astype(bf16)
            suffix_out[m_at, :] = chosen(upper, eye, other_m.T).astype(bf16)
        else:
            before_m, before_a = prefix_ref[m_at, :].astype(f32), prefix_ref[a_at, :].astype(f32)
            after_m = suffix_ref[m_at, :].astype(f32)
            joint = mm(before_m, jnp.concatenate([other_m, other_a], axis=1))
            prefix_out[m_at, :] = chosen(upper, joint[:, :HEAD_DIM], before_m).astype(bf16)
            prefix_out[a_at, :] = chosen(
                upper, joint[:, HEAD_DIM:] + before_a, before_a
            ).astype(bf16)
            suffix_out[m_at, :] = chosen(upper, after_m, mm(after_m, other_m, 1, 1)).astype(bf16)


def back_round_kernel(
    bit, first, place, own_maps, other_maps, suffix_m, own_ref, other_ref, after_ref,
    total_ref, after_out,
):
    upper = bit_of(place, 0, bit)
    heads = own_ref.shape[0] // HEAD_DIM
    for head in range(heads):
        at = slice(head * HEAD_DIM, (head + 1) * HEAD_DIM)
        own, other = own_ref[at, :].astype(f32), other_ref[at, :].astype(f32)
        low_m = chosen(upper, other_maps[at, :].astype(f32), own_maps[at, :].astype(f32))
        high, low = chosen(upper, own, other), chosen(upper, other, own)
        total_ref[at, :] = (mm(low_m, high, 0, 0) + low).astype(bf16)
        if first:
            after_out[at, :] = chosen(upper, jnp.zeros_like(other), other).astype(bf16)
        else:
            after = after_ref[at, :].astype(f32)
            after_out[at, :] = chosen(upper, after, mm(suffix_m[at, :], other) + after).astype(bf16)


def mixer_kernel(
    last_bit, place, seg_ref, segc_ref, tail_ref, prefix_ref, other_a_ref,
    qe_ref, pu_ref, d_ref, ku_ref, gate_ref, hgain_ref,
    y_ref, o_ref, state_ref, joined_ids,
):
    rows, head_width = qe_ref.shape
    heads = head_width // LANES
    width = tail_ref.shape[1] - LANES
    joined_ids[0:SUB, :] = tail_ref[:, width:]
    joined_ids[SUB : SUB + rows, :] = segc_ref[...]
    upper = bit_of(place, 0, last_bit)
    for head in range(heads):
        m_at = slice(head * HEAD_DIM, (head + 1) * HEAD_DIM)
        a_at = slice((heads + head) * HEAD_DIM, (heads + head + 1) * HEAD_DIM)
        before_m, before_a = prefix_ref[m_at, :], prefix_ref[a_at, :].astype(f32)
        state = chosen(upper, mm(before_m, other_a_ref[m_at, :]) + before_a, before_a)
        cols = slice(head * LANES, (head + 1) * LANES)
        for chunk in range(rows // CHUNK):
            at = (slice(chunk * CHUNK, (chunk + 1) * CHUNK), cols)
            kept = chunk_flags(joined_ids, segc_ref, seg_ref, chunk)[3]
            low = state.astype(bf16)
            state_ref[at] = low
            out = mm(qe_ref[at], low) + pu_ref[at].astype(f32)
            o_ref[at] = out
            state = kept * state - mm(d_ref[at], low) + ku_ref[at].astype(f32)
            gate = gate_ref[at]
            scale = lax.rsqrt(jnp.mean(out * out, axis=-1, keepdims=True) + 1e-05)
            y_ref[at] = (out * scale * hgain_ref[...] * (gate * sigmoid(gate))).astype(bf16)


def ffn_kernel(
    place, x_ref, g_ref, fgain_ref, wg_ref, wu_ref, wd_ref, *rest,
):
    *parts, h_ref, b_ref, hid_ref, dgate_ref, dup_ref, keep_ref, send_ref, whole = rest
    y_refs, wo_refs = parts[: len(parts) // 2], parts[len(parts) // 2 :]
    att = None
    for y_ref, wo_ref in zip(y_refs, wo_refs):
        for piece in range(y_ref.shape[0]):
            part = mm(y_ref[piece], wo_ref[piece])
            att = part if att is None else att + part
    h = x_ref[...].astype(f32) + att
    h_ref[...] = h
    scale = lax.rsqrt(jnp.mean(h * h, axis=-1, keepdims=True) + 1e-06)
    b = (h * scale * fgain_ref[...]).astype(bf16)
    b_ref[...] = b
    gate = mm(b, wg_ref[...])
    up = mm(b, wu_ref[...])
    sg = sigmoid(gate)
    act = gate * sg
    hid_ref[...] = (act * up).astype(bf16)
    dhid = mm(g_ref[...], wd_ref[...], 1, 1)
    dgate = (dhid * up * (sg * (1.0 + gate * (1.0 - sg)))).astype(bf16)
    dup = (dhid * act).astype(bf16)
    dgate_ref[...] = dgate
    dup_ref[...] = dup
    whole[...] = mm(dgate, wg_ref[...], 1, 1) + mm(dup, wu_ref[...], 1, 1)
    split_rows(place, whole, keep_ref, send_ref)


def split_rows(place, whole, keep_ref, send_ref):
    half = keep_ref.shape[0]
    core = bit_of(place, 1, 0)
    keep_ref[...] = whole[pl.ds(pl.multiple_of(core * half, half), half), :].astype(bf16)
    send_ref[...] = whole[pl.ds(pl.multiple_of((1 - core) * half, half), half), :].astype(bf16)


def join_rows(place, mine, theirs, whole):
    half = mine.shape[0]
    core = bit_of(place, 1, 0)
    whole[pl.ds(pl.multiple_of(core * half, half), half), :] = mine
    whole[pl.ds(pl.multiple_of((1 - core) * half, half), half), :] = theirs


def ffn_grads_kernel(place, b_ref, hid_ref, dgate_ref, dup_ref, g_ref, wd_ref,
                     ggate_ref, gup_ref, gdown_ref, keep_ref, send_ref, whole):
    whole[...] = mm(hid_ref[...], wd_ref[...])
    split_rows(place, whole, keep_ref, send_ref)
    ggate_ref[...] = mm(b_ref[...], dgate_ref[...], 0, 0).astype(bf16)
    gup_ref[...] = mm(b_ref[...], dup_ref[...], 0, 0).astype(bf16)
    gdown_ref[...] = mm(g_ref[...], hid_ref[...], 0, 0).astype(bf16)


def residual_back_kernel(
    place, mine_a, mine_b, theirs_a, theirs_b, h_ref, g_ref, fgain_ref, wo_ref, y_ref, o_ref,
    gate_ref, hgain_ref, seg_ref, segc_ref, tail_ref, qe_ref, d_ref,
    dh_ref, gh_ref, do_ref, dgr_ref, pull_ref, sums_ref, whole, joined_ids,
):
    rows, head_width = o_ref.shape
    heads = head_width // LANES
    width = tail_ref.shape[1] - LANES
    joined_ids[0:SUB, :] = tail_ref[:, width:]
    joined_ids[SUB : SUB + rows, :] = segc_ref[...]
    join_rows(
        place,
        mine_a[...].astype(f32) + mine_b[...].astype(f32),
        theirs_a[...].astype(f32) + theirs_b[...].astype(f32),
        whole,
    )
    h = h_ref[...]
    db = whole[...]
    scale = lax.rsqrt(jnp.mean(h * h, axis=-1, keepdims=True) + 1e-06)
    hat = h * scale
    prod = db * hat
    sums_ref[0:1, :] = jnp.sum(prod, axis=0, keepdims=True)
    inner = jnp.mean(prod * fgain_ref[...], axis=-1, keepdims=True)
    dh = g_ref[...].astype(f32) + scale * (db * fgain_ref[...] - hat * inner)
    dh_ref[...] = dh
    gh = dh.astype(bf16)
    gh_ref[...] = gh
    dy_all = mm(gh, wo_ref[...], 1, 1)
    hg_sum = jnp.zeros((1, LANES), f32)
    for head in range(heads):
        cols = slice(head * LANES, (head + 1) * LANES)
        out, gate, dy = o_ref[:, cols], gate_ref[:, cols], dy_all[:, cols]
        norm = lax.rsqrt(jnp.mean(out * out, axis=-1, keepdims=True) + 1e-05)
        hat_o = out * norm
        sg = sigmoid(gate)
        act = gate * sg
        hg_sum = hg_sum + jnp.sum(dy * hat_o * act, axis=0, keepdims=True)
        dgain = dy * hgain_ref[...]
        dgr_ref[:, cols] = (dgain * hat_o * (sg * (1.0 + gate * (1.0 - sg)))).astype(bf16)
        e = dgain * act
        do_ref[:, cols] = (norm * (e - hat_o * jnp.mean(e * hat_o, axis=-1, keepdims=True))).astype(bf16)
    sums_ref[1:2, :] = jnp.concatenate(
        [hg_sum, jnp.zeros((1, sums_ref.shape[1] - LANES), f32)], axis=1
    )
    chunks = rows // CHUNK
    pulls = [None] * heads
    for chunk in range(chunks - 1, -1, -1):
        kept = chunk_flags(joined_ids, segc_ref, seg_ref, chunk)[3]
        for head in range(heads):
            at = (slice(chunk * CHUNK, (chunk + 1) * CHUNK), slice(head * LANES, (head + 1) * LANES))
            local = mm(qe_ref[at], do_ref[at], 0, 0)
            if pulls[head] is not None:
                local = local + kept * pulls[head] - mm(d_ref[at], pulls[head], 0, 0)
            pulls[head] = local
    for head in range(heads):
        pull_ref[head * HEAD_DIM : (head + 1) * HEAD_DIM, :] = pulls[head].astype(bf16)


def delta_back_kernel(
    last_bit, place, p_ref, tail_ref, taps_ref, seg_ref, segc_ref, beta_ref,
    qkv_ref, w_ref, u_ref, r_ref, s_ref, d_ref, qe_ref, state_ref, do_ref,
    suffix_m, after_ref, other_ref,
    gp_ref, last_ref, halo_ref, gb_ref, gtaps_ref, gbias_ref,
    joined, joined_ids, dq_s, du_s, mask_s,
):
    rows, width = p_ref.shape
    head_width = width // 3
    heads = head_width // LANES
    chunks = rows // CHUNK
    lags = taps_ref.shape[1] - 1
    fill_joined(p_ref, tail_ref, segc_ref, joined, joined_ids)
    masks = lag_masks(joined_ids, segc_ref, lags)
    row_ids, col_ids = tri_masks()
    flags = [chunk_flags(joined_ids, segc_ref, seg_ref, chunk) for chunk in range(chunks)]
    upper = bit_of(place, 0, last_bit)
    sets = [(head, chunk) for head in range(heads) for chunk in range(chunks)]

    def at_of(head, chunk, part=0):
        col = part * head_width + head * LANES
        return (slice(chunk * CHUNK, (chunk + 1) * CHUNK), slice(col, col + LANES))

    state_grads = {}
    for head in range(heads):
        at = slice(head * HEAD_DIM, (head + 1) * HEAD_DIM)
        after = after_ref[at, :].astype(f32)
        grad = chosen(upper, after, mm(suffix_m[at, :], other_ref[at, :]) + after)
        for chunk in range(chunks - 1, -1, -1):
            state_grads[head, chunk] = grad
            if chunk:
                tile = at_of(head, chunk)
                low = grad.astype(bf16)
                grad = (
                    flags[chunk][3] * grad
                    - mm(d_ref[tile], low, 0, 0)
                    + mm(qe_ref[tile], do_ref[tile], 0, 0)
                )
    lane_ids = lax.broadcasted_iota(jnp.int32, (CHUNK, LANES), 1)
    gb_cols = [jnp.zeros((CHUNK, LANES), f32) for _ in range(chunks)]
    for head, chunk in sets:
        same, opened, closing, kept = flags[chunk]
        at = at_of(head, chunk)
        q, k, v = (qkv_ref[at_of(head, chunk, part)] for part in range(3))
        kf, vf = k.astype(f32), v.astype(f32)
        beta = beta_ref[at]
        state, do = state_ref[at], do_ref[at]
        scores, w_rows, u_rows, inverse = s_ref[at], w_ref[at], u_ref[at], r_ref[at]
        sgrad = state_grads[head, chunk].astype(bf16)
        fresh = (u_rows.astype(f32) - opened * mm(w_rows, state)).astype(bf16)
        dfresh = mm(scores, do, 0, 0) + mm(closing * kf, sgrad)
        dscore = jnp.where(row_ids >= col_ids, mm(do, fresh, 1, 1) * same, 0.0).astype(bf16)
        dw = -(opened * mm(dfresh, state, 1, 1))
        dx = mm(inverse, jnp.concatenate([dfresh, dw], axis=1), 0, 0)
        dxv, dxk = dx[:, :HEAD_DIM], dx[:, HEAD_DIM:]
        dlow = mm(dx, jnp.concatenate([u_rows, w_rows], axis=1), 1, 1)
        dlow = jnp.where(row_ids > col_ids, -dlow * same, 0.0)
        inner = mm(k, k, 1, 1)
        dbeta = jnp.sum(dxv * vf + dxk * kf + dlow * inner, axis=-1, keepdims=True)
        glow = (dlow * beta).astype(bf16)
        dq_s[at_of(head, chunk, 0)] = opened * mm(do, state, 1, 1) + mm(dscore, k)
        dq_s[at_of(head, chunk, 1)] = (
            beta * dxk
            + mm(dscore, q, 0, 0)
            + closing * mm(fresh, sgrad, 1, 1)
            + mm(glow, k)
            + mm(glow, k, 0, 0)
        )
        dq_s[at_of(head, chunk, 2)] = beta * dxv
        raw = jnp.broadcast_to(dbeta, (CHUNK, LANES)) * beta * (1.0 - beta)
        gb_cols[chunk] = jnp.where(lane_ids == head, raw, gb_cols[chunk])
    bias_sum = jnp.zeros((1, LANES), f32)
    for chunk in range(chunks):
        gb_ref[chunk * CHUNK : (chunk + 1) * CHUNK, :] = gb_cols[chunk].astype(bf16)
        bias_sum = bias_sum + jnp.sum(gb_cols[chunk], axis=0, keepdims=True)
    gbias_ref[...] = bias_sum
    du_s[0:SUB, :] = jnp.zeros((SUB, LANES), f32)
    du_s[SUB + rows :, :] = jnp.zeros((SUB, LANES), f32)
    for lag in range(1, lags + 1):
        mask_s[lag - 1, 0:SUB, :] = jnp.zeros((SUB, LANES), f32)
        mask_s[lag - 1, SUB : SUB + rows, :] = masks[lag]
        mask_s[lag - 1, SUB + rows :, :] = jnp.zeros((SUB, LANES), f32)
    for part in range(3):
        for head in range(heads):
            col = part * head_width + head * LANES
            cols = slice(col, col + LANES)
            tap_cols = slice(head * LANES, (head + 1) * LANES)
            total = conv_sum(joined, taps_ref, masks, part, head, head_width, rows)
            sg = sigmoid(total)
            grad = dq_s[:, cols]
            if part < 2:
                z = total * sg
                norm = lax.rsqrt(jnp.sum(z * z, axis=-1, keepdims=True) + 1e-06)
                hat = z * norm
                grad = norm * (grad - hat * jnp.sum(grad * hat, axis=-1, keepdims=True))
                if part == 0:
                    grad = grad * Q_SCALE
            grad = grad * (sg * (1.0 + total * (1.0 - sg)))
            du_s[SUB : SUB + rows, :] = grad
            dp = taps_ref[part, lags : lags + 1, tap_cols] * grad
            halo = jnp.zeros((SUB, LANES), f32)
            gtaps_ref[part, lags : lags + 1, tap_cols] = jnp.sum(
                grad * joined[SUB : SUB + rows, cols], axis=0, keepdims=True
            )
            for lag in range(1, lags + 1):
                tap = taps_ref[part, lags - lag : lags - lag + 1, tap_cols]
                gtaps_ref[part, lags - lag : lags - lag + 1, tap_cols] = jnp.sum(
                    grad * joined[SUB - lag : SUB - lag + rows, cols] * masks[lag],
                    axis=0,
                    keepdims=True,
                )
                moved = du_s[SUB + lag : SUB + lag + rows, :]
                dp = dp + tap * moved * mask_s[lag - 1, SUB + lag : SUB + lag + rows, :]
                halo = halo + tap * du_s[lag : lag + SUB, :] * mask_s[lag - 1, lag : lag + SUB, :]
            gp_ref[:, cols] = dp.astype(bf16)
            last_ref[:, cols] = dp[rows - 2 * SUB :, :]
            halo_ref[:, cols] = halo


def input_back_kernel(
    place, gp_ref, last_ref, next_ref, dgr_ref, gb_ref, wq_ref, wk_ref, wv_ref, wg_ref, wb_ref,
    x_ref, keep_ref, send_ref, gpf_ref, sums_ref, whole,
):
    rows, width = gp_ref.shape
    head_width = width // 3
    gpf_ref[...] = gp_ref[...]
    last = last_ref[...]
    gpf_ref[rows - 2 * SUB :, :] = jnp.concatenate(
        [last[:SUB], last[SUB:] + next_ref[...]], axis=0
    ).astype(bf16)
    total = mm(dgr_ref[...], wg_ref[...], 1, 1) + mm(gb_ref[...], wb_ref[...], 1, 1)
    for part, w_ref in enumerate((wq_ref, wk_ref, wv_ref)):
        total = total + mm(gpf_ref[:, part * head_width : (part + 1) * head_width], w_ref[...], 1, 1)
    whole[...] = total
    split_rows(place, whole, keep_ref, send_ref)
    x = x_ref[...].astype(f32)
    scale = lax.rsqrt(jnp.mean(x * x, axis=-1, keepdims=True) + 1e-06)
    sums_ref[...] = jnp.sum(total * (x * scale), axis=0, keepdims=True)


def project_grads_kernel(order, place, a_ref, gp_ref, dgr_ref, gb_ref, keep_ref, send_ref, gwb_ref, whole):
    width = gp_ref.shape[1]
    a = a_ref[...]
    whole[:, :width] = mm(a, gp_ref[...], 0, 0).astype(bf16)
    whole[:, width:] = mm(a, dgr_ref[...], 0, 0).astype(bf16)
    gwb_ref[...] = mm(gb_ref[...], a, 0, 0)[: gwb_ref.shape[0]]
    block = whole.shape[0] // (2 * len(order))
    for index, relative in enumerate(order):
        for ref, low_bit in ((keep_ref, 0), (send_ref, 1)):
            owner = lax.bitwise_xor(place[0], jnp.int32(relative | low_bit))
            ref[index * block : (index + 1) * block, :] = whole[
                pl.ds(pl.multiple_of(owner * block, block), block), :
            ]


def input_grad_kernel(place, mine_a, mine_b, theirs_a, theirs_b, x_ref, gain_ref, dh_ref, out_ref, whole):
    join_rows(
        place,
        mine_a[...].astype(f32) + mine_b[...].astype(f32),
        theirs_a[...].astype(f32) + theirs_b[...].astype(f32),
        whole,
    )
    x = x_ref[...].astype(f32)
    scale = lax.rsqrt(jnp.mean(x * x, axis=-1, keepdims=True) + 1e-06)
    hat = x * scale
    grad = whole[...] * gain_ref[...]
    inner = jnp.mean(grad * hat, axis=-1, keepdims=True)
    out_ref[...] = dh_ref[...] + scale * (grad - hat * inner)


def output_kernel(place, mine_a, mine_b, theirs_a, theirs_b, h_ref, out_ref, whole):
    join_rows(
        place,
        mine_a[...].astype(f32) + mine_b[...].astype(f32),
        theirs_a[...].astype(f32) + theirs_b[...].astype(f32),
        whole,
    )
    out_ref[...] = (h_ref[...] + whole[...]).astype(bf16)


def head_sum(keep, send):
    count = lax.axis_size("head")
    mine = keep + swap(send, "head", 1)
    bit = 2
    if bit >= count:
        zero = jnp.zeros_like(mine)
        return mine, zero, swap(mine, "head", 1), zero
    while bit * 2 < count:
        mine = mine + swap(mine, "head", bit)
        bit *= 2
    far = swap(mine, "head", bit)
    return mine, far, swap(mine, "head", 1), swap(far, "head", 1)


def gathered(value):
    count = lax.axis_size("head")
    blocks = value[None]
    bits = []
    bit = 2
    while bit < count:
        bits.append(bit)
        bit *= 2
    bits.append(1)
    for bit in bits:
        blocks = jnp.concatenate([blocks, swap(blocks, "head", bit)], axis=0)
    return blocks


def body(
    block_input, cotangent, segment_ids, norm_gain, w_query, w_key, w_value, w_gate, w_beta,
    beta_bias, conv_weight, head_gain, w_out, ffn_gain, w_ffn_gate, w_ffn_up, w_ffn_down,
):
    rows, model = block_input.shape
    heads = w_beta.shape[1]
    head_width = w_query.shape[1]
    ffn_width = w_ffn_gate.shape[1]
    taps = conv_weight.shape[1]
    seq_count = lax.axis_size("seq")
    rounds = seq_count.bit_length() - 1
    width = 3 * head_width
    chunks = rows // CHUNK

    place = jnp.stack([lax.axis_index("seq"), lax.axis_index("head")]).astype(jnp.int32)
    seg_rows = segment_ids.reshape(chunks, LANES).astype(f32)
    gain_row, fgain_row, hgain_row = norm_gain[None], ffn_gain[None], head_gain[None]
    w_beta_wide = jnp.pad(w_beta, ((0, 0), (0, LANES - heads)))
    bias_row = jnp.pad(beta_bias, (0, LANES - heads))[None]

    w_out_all = gathered(w_out)

    a, p, gate_raw, beta, seg_cols, tail = kernel_call(
        project_kernel,
        (
            shaped((rows, model), bf16),
            shaped((rows, width), bf16),
            shaped((rows, head_width), f32),
            shaped((rows, head_width), f32),
            shaped((rows, LANES), f32),
            shaped((SUB, width + LANES), f32),
        ),
        place, block_input, gain_row, w_query, w_key, w_value, w_gate, w_beta_wide, bias_row, seg_rows,
        name="project",
        flops=2 * rows * model * (4 * head_width + LANES),
    )
    halo = shift(tail, "seq", 1)
    square = (rows, head_width)
    joined = pltpu.VMEM((rows + SUB, width), f32)
    joined_ids = pltpu.VMEM((rows + SUB, LANES), f32)
    qkv, w_rows, u_rows, q_eff, p_u, inverse, scores, d_map, k_u, maps = kernel_call(
        delta_kernel,
        (shaped((rows, width), bf16),)
        + (shaped(square, bf16),) * 8
        + (shaped((2 * heads * HEAD_DIM, HEAD_DIM), bf16),),
        place, p, halo, conv_weight, seg_rows, seg_cols, beta,
        scratch=(joined, joined_ids),
        name="delta",
        flops=2 * heads * chunks * 128**3 * 30,
    )
    half_maps = heads * HEAD_DIM
    prefix = suffix = maps
    round_maps = []
    suffixes = [None]
    for bit in range(rounds - 1):
        other = swap(maps, "seq", 1 << bit)
        round_maps.append((maps, other))
        maps, prefix, suffix = kernel_call(
            functools.partial(scan_round_kernel, bit, bit == 0),
            (shaped(maps.shape, bf16), shaped(maps.shape, bf16), shaped((half_maps, HEAD_DIM), bf16)),
            place, maps, other, prefix, suffix,
            name="scan_round",
            flops=2 * heads * 128**3 * 5,
        )
        suffixes.append(suffix)
    other_a = swap(maps[half_maps:], "seq", 1 << (rounds - 1))
    y, mixed, states = kernel_call(
        functools.partial(mixer_kernel, rounds - 1),
        (shaped(square, bf16), shaped(square, f32), shaped(square, bf16)),
        place, seg_rows, seg_cols, halo, prefix, other_a, q_eff, p_u, d_map, k_u, gate_raw, hgain_row,
        scratch=(joined_ids,),
        name="mixer",
        flops=2 * heads * chunks * 128**3 * 2,
    )
    y_all = gathered(y)
    half = (rows // 2, model)
    h, b, hidden, dgate, dup, db_keep, db_send = kernel_call(
        ffn_kernel,
        (
            shaped((rows, model), f32),
            shaped((rows, model), bf16),
            shaped((rows, ffn_width), bf16),
            shaped((rows, ffn_width), bf16),
            shaped((rows, ffn_width), bf16),
            shaped(half, bf16),
            shaped(half, bf16),
        ),
        place, block_input, cotangent, fgain_row, w_ffn_gate, w_ffn_up, w_ffn_down, y_all, w_out_all,
        scratch=(pltpu.VMEM((rows, model), f32),),
        name="ffn",
        flops=2 * rows * model * (model + 5 * ffn_width),
    )
    db_parts = head_sum(db_keep, db_send)
    grad_gate, grad_up, grad_down, out_keep, out_send = kernel_call(
        ffn_grads_kernel,
        (
            shaped((model, ffn_width), bf16),
            shaped((model, ffn_width), bf16),
            shaped((model, ffn_width), bf16),
            shaped(half, bf16),
            shaped(half, bf16),
        ),
        place, b, hidden, dgate, dup, cotangent, w_ffn_down,
        scratch=(pltpu.VMEM((rows, model), f32),),
        name="ffn_grads",
        flops=2 * rows * model * 4 * ffn_width,
    )
    ffn_share = lax.psum_scatter(
        jnp.concatenate([grad_gate, grad_up], axis=1), "seq", scatter_dimension=0, tiled=True
    ).astype(f32)
    out_parts = head_sum(out_keep, out_send)
    (block_output,) = kernel_call(
        output_kernel,
        (shaped((rows, model), bf16),),
        place, *out_parts, h,
        scratch=(pltpu.VMEM((rows, model), f32),),
        name="output",
    )
    dh, gh, d_out, d_gate_raw, pull, sums_a = kernel_call(
        residual_back_kernel,
        (
            shaped((rows, model), f32),
            shaped((rows, model), bf16),
            shaped(square, bf16),
            shaped(square, bf16),
            shaped((half_maps, HEAD_DIM), bf16),
            shaped((2, model), f32),
        ),
        place, *db_parts, h, cotangent, fgain_row, w_out, y, mixed, gate_raw, hgain_row,
        seg_rows, seg_cols, halo, q_eff, d_map,
        scratch=(pltpu.VMEM((rows, model), f32), joined_ids),
        name="residual_back",
        flops=2 * rows * model * head_width,
    )
    grad_out = jnp.einsum("td,tw->dw", gh, y, preferred_element_type=f32).astype(bf16)
    down_share = lax.psum_scatter(
        jnp.concatenate([grad_down, grad_out], axis=1), "seq", scatter_dimension=0, tiled=True
    ).astype(f32)
    after = pull
    for bit in range(rounds - 1):
        other = swap(pull, "seq", 1 << bit)
        own_maps, other_maps = round_maps[bit]
        pull, after = kernel_call(
            functools.partial(back_round_kernel, bit, bit == 0),
            (shaped(pull.shape, bf16), shaped(pull.shape, bf16)),
            place, own_maps[:half_maps], other_maps[:half_maps],
            suffixes[bit] if bit else own_maps[:half_maps], pull, other, after,
            name="back_round",
            flops=2 * heads * 128**3 * 2,
        )
    other_pull = swap(pull, "seq", 1 << (rounds - 1))
    gp, gp_last, gp_halo, gb, grad_taps, grad_bias = kernel_call(
        functools.partial(delta_back_kernel, rounds - 1),
        (
            shaped((rows, width), bf16),
            shaped((2 * SUB, width), f32),
            shaped((SUB, width), f32),
            shaped((rows, LANES), bf16),
            shaped(conv_weight.shape, f32),
            shaped((1, LANES), f32),
        ),
        place, p, halo, conv_weight, seg_rows, seg_cols, beta, qkv, w_rows, u_rows, inverse, scores,
        d_map, q_eff, states, d_out, suffixes[rounds - 1], after, other_pull,
        scratch=(
            joined,
            joined_ids,
            pltpu.VMEM((rows, width), f32),
            pltpu.VMEM((rows + 2 * SUB, LANES), f32),
            pltpu.VMEM((taps - 1, rows + 2 * SUB, LANES), f32),
        ),
        name="delta_back",
        flops=2 * heads * chunks * 128**3 * 20,
    )
    from_next = shift(gp_halo, "seq", -1)
    da_keep, da_send, gp_full, sums_b = kernel_call(
        input_back_kernel,
        (
            shaped(half, bf16),
            shaped(half, bf16),
            shaped((rows, width), bf16),
            shaped((1, model), f32),
        ),
        place, gp, gp_last, from_next, d_gate_raw, gb, w_query, w_key, w_value, w_gate, w_beta_wide,
        block_input,
        scratch=(pltpu.VMEM((rows, model), f32),),
        name="input_back",
        flops=2 * rows * model * (4 * head_width + LANES),
    )
    da_parts = head_sum(da_keep, da_send)
    order = []
    for index in range(seq_count // 2):
        relative = 0
        for position in range(rounds - 1):
            if index >> (rounds - 2 - position) & 1:
                relative |= 1 << (position + 1)
        order.append(relative)
    share_rows = model // 2
    keep, send, grad_beta_rows = kernel_call(
        functools.partial(project_grads_kernel, tuple(order)),
        (
            shaped((share_rows, 4 * head_width), bf16),
            shaped((share_rows, 4 * head_width), bf16),
            shaped((heads, model), f32),
        ),
        place, a, gp_full, d_gate_raw, gb,
        scratch=(pltpu.VMEM((model, 4 * head_width), bf16),),
        name="project_grads",
        flops=2 * rows * model * (4 * head_width + LANES),
    )
    (input_grad,) = kernel_call(
        input_grad_kernel,
        (shaped((rows, model), f32),),
        place, *da_parts, block_input, gain_row, dh,
        scratch=(pltpu.VMEM((rows, model), f32),),
        name="input_grad",
    )
    both_axes = jnp.concatenate([sums_b[0], sums_a[1, :LANES]])
    seq_only = jnp.concatenate(
        [sums_a[0], grad_taps.reshape(-1), grad_beta_rows.reshape(-1), grad_bias[0]]
    )
    small = jnp.concatenate([both_axes, seq_only])
    short = both_axes.shape[0]
    size = small.shape[0]
    small = jnp.pad(small, (0, -size % 1024)).reshape(-1, LANES)
    for bit in range(rounds):
        got = swap(send, "seq", 1 << bit)
        small = small + swap(small, "seq", 1 << bit)
        if bit < rounds - 1:
            middle = keep.shape[0] // 2
            send = keep[middle:] + got[middle:]
            keep = keep[:middle] + got[:middle]
        else:
            project_share = keep.astype(f32) + got.astype(f32)
    flat = small.reshape(-1)
    both_axes = flat[:short].reshape(-1, LANES)
    bit = 1
    while bit < lax.axis_size("head"):
        both_axes = both_axes + swap(both_axes, "head", bit)
        bit *= 2
    both_axes = both_axes.reshape(-1)
    norm_total, head_gain_total = both_axes[:model], both_axes[model:]
    flat = flat[short:size]
    ffn_gain_total, flat = flat[:model], flat[model:]
    conv_total, flat = flat[: conv_weight.size].reshape(conv_weight.shape), flat[conv_weight.size :]
    beta_rows, flat = flat[: heads * model].reshape(heads, model), flat[heads * model :]
    bias_total = flat[:heads]
    block = model // seq_count
    beta_share = lax.dynamic_slice(
        beta_rows, (0, lax.axis_index("seq") * block), (heads, block)
    ).T
    return (
        block_output,
        input_grad,
        norm_total,
        project_share[:, :head_width],
        project_share[:, head_width : 2 * head_width],
        project_share[:, 2 * head_width : 3 * head_width],
        project_share[:, 3 * head_width :],
        beta_share,
        bias_total,
        conv_total,
        head_gain_total,
        down_share[:, ffn_width:].T,
        ffn_gain_total,
        ffn_share[:, :ffn_width],
        ffn_share[:, ffn_width:],
        down_share[:, :ffn_width].T,
    )


def solution(mesh):
    return jax.shard_map(
        body,
        mesh=mesh,
        in_specs=(
            P("seq", None), P("seq", None), P("seq"), P(),
            P(None, "head"), P(None, "head"), P(None, "head"), P(None, "head"), P(None, "head"),
            P("head"), P(None, None, "head"), P(), P("head", None), P(),
            P(None, "head"), P(None, "head"), P("head", None),
        ),
        out_specs=(
            P("seq", None), P("seq", None), P(),
            P("seq", "head"), P("seq", "head"), P("seq", "head"), P("seq", "head"), P("seq", "head"),
            P("head"), P(None, None, "head"), P(), P("head", "seq"), P(),
            P("seq", "head"), P("seq", "head"), P("head", "seq"),
        ),
        check_vma=False,
    )
```

time: 1100 us -> 286 us (0.26)
  waiting for transfers between devices: 424 us -> 119 us
  matrix products: 262 us -> 1.72 us
  local copies, waits for them, and re-layouts: 173 us -> 31.9 us
  other arithmetic: 111 us -> 15.6 us
  Pallas kernels: 0 us -> 68.7 us
  blocking collectives: 43.9 us -> 0 us
  starting transfers between devices: 52 us -> 33.7 us
    dot_general x797 -> x1, matrix products: 262 us -> 1.72 us  [body(): jnp.einsum('td,tw->dw', gh, y, preferred_element_type=f32).astype(bf16)]
    unnamed x11 -> x2, waiting for transfers between devices: 123 us -> 0.03 us
    reduce_scatter x2, waiting for transfers between devices: 141 us -> 19 us  [the longest x1 19 us: body(): lax.psum_scatter(jnp.concatenate([grad_gate, grad_up], axis=1), 'seq', sc...]
    psum x3 -> x0, waiting for transfers between devices: 108 us -> none  [the longest x1 43.5 us: body(): lax.psum(jnp.dot(hidden_low, w_ffn_down, preferred_element_type=jnp.float...]
    pallas_call x0 -> x15, Pallas kernels: none -> 68.7 us  [kernel_call(): pl.pallas_call(body, out_shape=tuple(out_shapes), in_specs=[smem] + [vmem...]
    convert_element_type x107 -> x2, other arithmetic: 69.1 us -> 2.25 us  [the longest x1 1.26 us: body(): seg_rows = segment_ids.reshape(chunks, LANES).astype(f32)]
    ppermute x17 -> x32, waiting for transfers between devices: 52.7 us -> 99.9 us  [the longest x30 94.7 us: swap(): return lax.ppermute(value, axis, [(s, s ^ bit) for s in range(count)])]
    psum x2 -> x0, blocking collectives: 43.9 us -> none  [the longest x1 37.8 us: body(): lax.psum((grad_conv, grad_norm_gain, grad_ffn_gain, grad_head_gain_all, g...]
  transfers between devices with their start and end apart: 25 -> 34, of which waited for: 22 -> 18; matrix products, arithmetic and copies ran while one was open for 5% -> 10% of each run, Pallas kernels for 0% -> 19%
where the time goes in v1:
time: 286 us; the launch traced here: 285 us
  waiting for transfers between devices  119 us (42%)
  Pallas kernels  68.7 us (24%)
  starting transfers between devices  33.7 us (12%)
  local copies, waits for them, and re-layouts  31.9 us (11%)
  other arithmetic  15.6 us (5%)
  between operations  14.6 us (5%)
    ppermute x30, waiting for transfers between devices, swap(): return lax.ppermute(value, axis, [(s, s ^ bit) for s in range(count)])  94.7 us
    pallas_call x15, Pallas kernels, kernel_call(): pl.pallas_call(body, out_shape=tuple(out_shapes), in_specs=[smem] + [vmem...  68.7 us
    ppermute x30, starting transfers between devices, swap(): return lax.ppermute(value, axis, [(s, s ^ bit) for s in range(count)])  28.3 us
    unnamed x95, local copies, waits for them, and re-layouts  21.1 us
    reduce_scatter x1, waiting for transfers between devices, body(): lax.psum_scatter(jnp.concatenate([grad_gate, grad_up], axis=1), 'seq', sc...  19 us
    concatenate x4, other arithmetic, gathered(): blocks = jnp.concatenate([blocks, swap(blocks, 'head', bit)], axis=0)  6.72 us
  transfers between devices with their start and end apart: 34, of which 18 were waited for; matrix products, arithmetic and copies ran while one was open for 10% of the time, Pallas kernels for 19%

profile of v1, /device:TPU:0, one launch (start us, length us, event | category | flops | bytes accessed | tf_op | source)
XLA Modules:
  0.0 285.1 jit_solution(2114607374469851008)
XLA Ops:
  14.9 4.1 %project.1 = (bf16[384,1024]{1,0:T(8,128)(2,1)}, bf16[384,768]{1,0:T(8,128)(2,1)}, f32[384,256]{1,0:T(8,128)}, f32[384,256]{1,0:T(8,128)}, f32[384,128]{1,0:T(8,128)}, /*index=5*/f32[8,896]{1,0:T(8,128)}) custom-call(s32[2]{0:T(128)} %pad_add_fusion.place, bf16[384,1024]{1,0:T(8,128)(2,1)} %x_ref.7, f32[1,1024]{1,0:T(1,128)} %bitcast.56, ...), custom_call_target="tpu_custom_call" | custom-call | flops 905969664 | bytes 5539848 | tf_op jit(solution)/shard_map/project/pallas_call | solution.py:39
  19.0 3.6 %collective-permute-start = (f32[8,896]{1,0:T(8,128)}, f32[8,896]{1,0:T(8,128)S(1)}, u32[]{:S(2)}, u32[]{:S(2)}) collective-permute-start(f32[8,896]{1,0:T(8,128)} %get-tuple-element.77), channel_id=1, source_target_pairs={{0,4},{4,8},{8,12},{12,16},{16,20},{20,24},{24,28},{1,5},{5,9},{9,... | collective-permute-start | bytes 86024 | tf_op jit(solution)/shard_map/ppermute | solution.py:62
  25.0 5.7 %delta.1 = (bf16[384,768]{1,0:T(8,128)(2,1)}, bf16[384,256]{1,0:T(8,128)(2,1)}, bf16[384,256]{1,0:T(8,128)(2,1)}, bf16[384,256]{1,0:T(8,128)(2,1)}, bf16[384,256...) custom-call(s32[2]{0:T(128)} %pad_add_fusion.place, ...), custom_call_target="tpu_custom_call" | custom-call | flops 754974720 | bytes 3515912 | tf_op jit(solution)/shard_map/delta/pallas_call | solution.py:39
  32.9 3.2 %collective-permute-done.1.other_ref = bf16[512,128]{1,0:T(8,128)(2,1)S(1)} collective-permute-done((bf16[512,128]{1,0:T(8,128)(2,1)}, bf16[512,128]{1,0:T(8,128)(2,1)S(1)}, u32[]{:S(2)}, u32[]{:S(2)}) %collective-permute-start.1) | collective-permute-done | bytes 131104 | tf_op jit(solution)/shard_map/ppermute | solution.py:57
  54.3 3.3 %mixer.1 = (bf16[384,256]{1,0:T(8,128)(2,1)}, f32[384,256]{1,0:T(8,128)}, bf16[384,256]{1,0:T(8,128)(2,1)}) custom-call(s32[2]{0:T(128)} %pad_add_fusion.place, f32[3,128]{1,0:T(4,128)} %convert_bitcast_fusion.seg_ref, f32[384,128]{1,0:T(8,128)} %get-tuple-element.76.segc_ref, f32[8,896]{1,0:T(8,128)} %copy-done.31, ...), custom_call_target="tpu_custom_call" | custom-call | flops 50331648 | bytes 2390024 | tf_op jit(solution)/shard_map/mixer/pallas_call | solution.py:39
  58.1 5.3 %collective-permute-done.4 = bf16[1,384,256]{2,1,0:T(8,128)(2,1)S(1)} collective-permute-done((bf16[1,384,256]{2,1,0:T(8,128)(2,1)}, bf16[1,384,256]{2,1,0:T(8,128)(2,1)S(1)}, u32[]{:S(2)}, u32[]{:S(2)}) %collective-permute-start.4) | collective-permute-done | bytes 196640 | tf_op jit(solution)/shard_map/ppermute | solution.py:57
  74.9 10.2 %ffn.1 = (f32[384,1024]{1,0:T(8,128)}, bf16[384,1024]{1,0:T(8,128)(2,1)}, bf16[384,704]{1,0:T(8,128)(2,1)}, bf16[384,704]{1,0:T(8,128)(2,1)}, bf16[384,704]{1,0:...) custom-call(s32[2]{0:T(128)} %pad_add_fusion.place, bf16[384,1024]{1,0:T(8,128)(2,1)} %x_ref.7, ...), custom_call_target="tpu_custom_call" | custom-call | flops 3573547008 | bytes 13553672 | tf_op jit(solution)/shard_map/ffn/pallas_call | solution.py:39
  89.0 10.8 %collective-permute-done.13.mine_b = bf16[192,1024]{1,0:T(8,128)(2,1)S(1)} collective-permute-done((bf16[192,1024]{1,0:T(8,128)(2,1)S(1)}, bf16[192,1024]{1,0:T(8,128)(2,1)S(1)}, u32[]{:S(2)}, u32[]{:S(2)}) %collective-permute-start.13) | collective-permute-done | bytes 393248 | tf_op jit(solution)/shard_map/ppermute | solution.py:57
  99.8 7.2 %ffn_grads.1 = (bf16[1024,704]{1,0:T(8,128)(2,1)}, bf16[1024,704]{1,0:T(8,128)(2,1)}, bf16[1024,704]{1,0:T(8,128)(2,1)}, bf16[192,1024]{1,0:T(8,128)(2,1)}, bf16[192,1024]{1,0:T(8,128)(2,1)}) custom-call(s32[2]{0:T(128)} %pad_add_fusion.place, bf16[384,1024]{1,0:T(8,128)(2,1)} %get-tuple-element.92.b_ref, bf16[384,704]{1,0:T(8,128)(2,1)} %get-tuple-element.93.hid_ref, ...), custom_call_target="tpu_custom_call" | custom-call | flops 2214592512 | bytes 9748488 | tf_op jit(solution)/shard_map/ffn_grads/pallas_call | solution.py:39
  107.9 5.4 %residual_back.1 = (f32[384,1024]{1,0:T(8,128)}, bf16[384,1024]{1,0:T(8,128)(2,1)}, bf16[384,256]{1,0:T(8,128)(2,1)}, bf16[384,256]{1,0:T(8,128)(2,1)}, bf16[256,128]{1,0:T(8,128)(2,1)}, /*index=5*/f32[2,1024]{1,0:T(2,128)}) custom-call(s32[2]{0:T(128)} %pad_add_fusion.place, bf16[192,1024]{1,0:T(8,128)(2,1)} %copy-done.6, bf16[192,1024]{1,0:T(8,128)(2,1)} %copy-done.18, ...), custom_call_target="tpu_custom_call" | custom-call | flops 201326592 | bytes 8890376 | tf_op jit(solution)/shard_map/residual_back/pallas_call | solution.py:39
  137.8 4.0 %collective-permute-start.18 = (bf16[256,128]{1,0:T(8,128)(2,1)}, bf16[256,128]{1,0:T(8,128)(2,1)S(1)}, u32[]{:S(2)}, u32[]{:S(2)}) collective-permute-start(bf16[256,128]{1,0:T(8,128)(2,1)} %get-tuple-element.114), channel_id=1, source_target_pairs={{0,16},{4,20},{8,24},{12,28},{16,0},{20,4},{24,8},{28,12},{1,17},{... | collective-permute-start | bytes 196616 | tf_op jit(solution)/shard_map/ppermute | solution.py:57
  141.8 6.1 %collective-permute-done.18.other_ref = bf16[256,128]{1,0:T(8,128)(2,1)S(1)} collective-permute-done((bf16[256,128]{1,0:T(8,128)(2,1)}, bf16[256,128]{1,0:T(8,128)(2,1)S(1)}, u32[]{:S(2)}, u32[]{:S(2)}) %collective-permute-start.18) | collective-permute-done | bytes 65568 | tf_op jit(solution)/shard_map/ppermute | solution.py:57
  148.5 8.9 %delta_back.1 = (bf16[384,768]{1,0:T(8,128)(2,1)}, f32[16,768]{1,0:T(8,128)}, f32[8,768]{1,0:T(8,128)}, bf16[384,128]{1,0:T(8,128)(2,1)}, f32[3,4,256]{2,1,0:T(4,128)}, /*index=5*/f32[1,128]{1,0:T(1,128)}) custom-call(s32[2]{0:T(128)} %pad_add_fusion.place, bf16[384,768]{1,0:T(8,128)(2,1)} %get-tuple-element.78.p_ref, f32[8,896]{1,0:T(8,128)} %copy-done.31, ...), custom_call_target="tpu_custom_call" | custom-call | flops 503316480 | bytes 4356104 | tf_op jit(solution)/shard_map/delta_back/pallas_call | solution.py:39
  160.0 3.5 %collective-permute-done.19.next_ref = f32[8,768]{1,0:T(8,128)S(1)} collective-permute-done((f32[8,768]{1,0:T(8,128)}, f32[8,768]{1,0:T(8,128)S(1)}, u32[]{:S(2)}, u32[]{:S(2)}) %collective-permute-start.19) | collective-permute-done | bytes 24608 | tf_op jit(solution)/shard_map/ppermute | solution.py:62
  164.1 4.7 %input_back.1 = (bf16[192,1024]{1,0:T(8,128)(2,1)}, bf16[192,1024]{1,0:T(8,128)(2,1)}, bf16[384,768]{1,0:T(8,128)(2,1)}, f32[1,1024]{1,0:T(1,128)}) custom-call(s32[2]{0:T(128)} %pad_add_fusion.place, bf16[384,768]{1,0:T(8,128)(2,1)} %get-tuple-element.115.gp_ref, f32[16,768]{1,0:T(8,128)} %get-tuple-element.116.last_ref, f32[8,768]{1,0:T(8,128)} %copy-done.36, ...), custom_call_target="tpu_custom_call" | custom-call | flops 905969664 | bytes 5484552 | tf_op jit(solution)/shard_map/input_back/pallas_call | solution.py:39
  168.8 4.1 %project_grads.1 = (bf16[512,1024]{1,0:T(8,128)(2,1)}, bf16[512,1024]{1,0:T(8,128)(2,1)}, f32[2,1024]{1,0:T(2,128)}) custom-call(s32[2]{0:T(128)} %pad_add_fusion.place, bf16[384,1024]{1,0:T(8,128)(2,1)} %get-tuple-element.126.a_ref, bf16[384,768]{1,0:T(8,128)(2,1)} %get-tuple-element.127.gp_ref, bf16[384,256]{1,0:T(8,128)(2,1)} %get-tuple-element.118.dgr_ref, ...), custom_call_target="tpu_custom_call" | custom-call | flops 905969664 | bytes 3776520 | tf_op jit(solution)/shard_map/project_grads/pallas_call | solution.py:39
  176.3 22.9 %collective-permute-done.24 = f32[64,128]{1,0:T(8,128)S(1)} collective-permute-done((f32[64,128]{1,0:T(8,128)S(1)}, f32[64,128]{1,0:T(8,128)S(1)}, u32[]{:S(2)}, u32[]{:S(2)}) %collective-permute-start.24) | collective-permute-done | bytes 32800 | tf_op jit(solution)/shard_map/ppermute | solution.py:57
  199.4 5.5 %collective-permute-done.25 = f32[64,128]{1,0:T(8,128)S(1)} collective-permute-done((f32[64,128]{1,0:T(8,128)S(1)}, f32[64,128]{1,0:T(8,128)S(1)}, u32[]{:S(2)}, u32[]{:S(2)}) %collective-permute-start.25) | collective-permute-done | bytes 32800 | tf_op jit(solution)/shard_map/ppermute | solution.py:57
  206.5 3.3 %output.1 = bf16[384,1024]{1,0:T(8,128)(2,1)} custom-call(s32[2]{0:T(128)} %pad_add_fusion.place, bf16[192,1024]{1,0:T(8,128)(2,1)} %copy-done.4, bf16[192,1024]{1,0:T(8,128)(2,1)} %copy-done.14, bf16[192,1024]{1,0:T(8,128)(2,1)} %copy-done.16, bf16[192,1024]{1,0:T(8,128)(2,1)} %copy-done.17, f32[384,1024]{1,0:T(8,128)} %get-tuple-element.98.h_ref), custom_call_target="tpu_custom_call" | custom-call | bytes 3932168 | tf_op jit(solution)/shard_map/output/pallas_call | solution.py:39
  216.7 7.3 %collective-permute-done.28 = f32[9,128]{1,0:T(8,128)S(1)} collective-permute-done((f32[9,128]{1,0:T(8,128)S(1)}, f32[9,128]{1,0:T(8,128)S(1)}, u32[]{:S(2)}, u32[]{:S(2)}) %collective-permute-start.28) | collective-permute-done | bytes 4640 | tf_op jit(solution)/shard_map/ppermute | solution.py:57
  224.6 13.3 %collective-permute-done.30 = bf16[256,1024]{1,0:T(8,128)(2,1)S(1)} collective-permute-done((bf16[256,1024]{1,0:T(8,128)(2,1)S(1)}, bf16[256,1024]{1,0:T(8,128)(2,1)S(1)}, u32[]{:S(2)}, u32[]{:S(2)}) %collective-permute-start.30) | collective-permute-done | bytes 524320 | tf_op jit(solution)/shard_map/ppermute | solution.py:57
  241.3 4.2 %input_grad.1 = f32[384,1024]{1,0:T(8,128)} custom-call(s32[2]{0:T(128)} %pad_add_fusion.place, bf16[192,1024]{1,0:T(8,128)(2,1)} %copy-done.5, bf16[192,1024]{1,0:T(8,128)(2,1)} %copy-done.15, bf16[192,1024]{1,0:T(8,128)(2,1)} %copy-done.20, bf16[192,1024]{1,0:T(8,128)(2,1)} %copy-done.22, bf16[384,1024]{1,0:T(8,128)(2,1)} %x_ref.7, f32[1,1024]{1,0:T(1,128)} %bitcast.57, ...), custom_call_target="tpu_custom_call" | custom-call | bytes 5509128 | tf_op jit(solution)/shard_map/input_grad/pallas_call | solution.py:39
  245.5 7.2 %collective-permute-done.31 = bf16[128,1024]{1,0:T(8,128)(2,1)S(1)} collective-permute-done((bf16[128,1024]{1,0:T(8,128)(2,1)S(1)}, bf16[128,1024]{1,0:T(8,128)(2,1)S(1)}, u32[]{:S(2)}, u32[]{:S(2)}) %collective-permute-start.31) | collective-permute-done | bytes 262176 | tf_op jit(solution)/shard_map/ppermute | solution.py:57
  256.4 19.0 %reduce-scatter.5.cloned.1.call-done = bf16[128,1408]{1,0:T(8,128)(2,1)} async-done(((bf16[1024,1408]{1,0:T(8,128)(2,1)}), bf16[128,1408]{1,0:T(8,128)(2,1)}) %reduce-scatter.5.cloned.1.call-update) | async-done | bytes 360464 | tf_op jit(solution)/shard_map/reduce_scatter | solution.py:767
  (201 shorter events, 97.9 us)
Async XLA Ops:
  7.2 246.4 %reduce-scatter.3.cloned.1.call-start = ((), (), s32[]{:S(2)}) async-start(), calls=%async_computation.2 | async-start | bytes 2359296 | tf_op jit(solution)/shard_map/reduce_scatter | solution.py:795
  7.2 34.5 %collective-permute-start.6 = (bf16[1,256,1024]{2,1,0:T(8,128)(2,1)}, bf16[1,256,1024]{2,1,0:T(8,128)(2,1)S(1)}, u32[]{:S(2)}, u32[]{:S(2)}) collective-permute-start(bf16[1,256,1024]{2,1,0:T(8,128)(2,1)} %bitcast.44), channel_id=1, source_target_pairs={{0,2},{1,3},{2,0},{3,1},{4,6},{5,7},{6,4},{7,5},{8,10},{9,11},{10,... | collective-permute-start | bytes 1572872 | tf_op jit(solution)/shard_map/ppermute | solution.py:57
  38.7 6.1 %collective-permute-start.2 = (bf16[512,128]{1,0:T(8,128)(2,1)}, bf16[512,128]{1,0:T(8,128)(2,1)S(1)}, u32[]{:S(2)}, u32[]{:S(2)}) collective-permute-start(bf16[512,128]{1,0:T(8,128)(2,1)} %get-tuple-element.81.own_ref), channel_id=1, source_target_pairs={{0,8},{4,12},{8,0},{12,4},{16,24},{20,28},{24,16},{28,20},{1,9},{5... | collective-permute-start | bytes 393224 | tf_op jit(solution)/shard_map/ppermute | solution.py:57
  41.8 30.3 %collective-permute-start.7 = (bf16[2,256,1024]{2,1,0:T(8,128)(2,1)S(1)}, bf16[2,256,1024]{2,1,0:T(8,128)(2,1)}, u32[]{:S(2)}, u32[]{:S(2)}) collective-permute-start(bf16[2,256,1024]{2,1,0:T(8,128)(2,1)S(1)} %pad_maximum_fusion.3), channel_id=1, source_target_pairs={{0,1},{1,0},{2,3},{3,2},{4,5},{5,4},{6,7},{7,6},{8,9},{9,8},{10,11... | collective-permute-start | bytes 3145736 | tf_op jit(solution)/shard_map/ppermute | solution.py:57
  88.3 11.5 %collective-permute-start.13 = (bf16[192,1024]{1,0:T(8,128)(2,1)S(1)}, bf16[192,1024]{1,0:T(8,128)(2,1)S(1)}, u32[]{:S(2)}, u32[]{:S(2)}) collective-permute-start(bf16[192,1024]{1,0:T(8,128)(2,1)S(1)} %add.53.mine_a), channel_id=1, source_target_pairs={{0,2},{1,3},{2,0},{3,1},{4,6},{5,7},{6,4},{7,5},{8,10},{9,11},{10,... | collective-permute-start | bytes 1179656 | tf_op jit(solution)/shard_map/ppermute | solution.py:57
  89.0 18.1 %collective-permute-start.14 = (bf16[192,1024]{1,0:T(8,128)(2,1)S(1)}, bf16[192,1024]{1,0:T(8,128)(2,1)S(1)}, u32[]{:S(2)}, u32[]{:S(2)}) collective-permute-start(bf16[192,1024]{1,0:T(8,128)(2,1)S(1)} %add.53.mine_a), channel_id=1, source_target_pairs={{0,1},{1,0},{2,3},{3,2},{4,5},{5,4},{6,7},{7,6},{8,9},{9,8},{10,11... | collective-permute-start | bytes 1179656 | tf_op jit(solution)/shard_map/ppermute | solution.py:57
  99.8 7.2 %collective-permute-start.15 = (bf16[192,1024]{1,0:T(8,128)(2,1)S(1)}, bf16[192,1024]{1,0:T(8,128)(2,1)S(1)}, u32[]{:S(2)}, u32[]{:S(2)}) collective-permute-start(bf16[192,1024]{1,0:T(8,128)(2,1)S(1)} %collective-permute-done.13.mine_b), channel_id=1, source_target_pairs={{0,1},{1,0},{2,3},{3,2},{4,5},{5,4},{6,7},{7,6},{8,9},{9,8},{10,11... | collective-permute-start | bytes 1179656 | tf_op jit(solution)/shard_map/ppermute | solution.py:57
  117.0 158.4 %reduce-scatter.5.cloned.1.call-start = ((), (), s32[]{:S(2)}) async-start(), calls=%async_computation.3 | async-start | bytes 3244032 | tf_op jit(solution)/shard_map/reduce_scatter | solution.py:767
  121.8 37.2 %collective-permute-start.8 = (bf16[192,1024]{1,0:T(8,128)(2,1)S(1)}, bf16[192,1024]{1,0:T(8,128)(2,1)S(1)}, u32[]{:S(2)}, u32[]{:S(2)}) collective-permute-start(bf16[192,1024]{1,0:T(8,128)(2,1)S(1)} %copy-done.39), channel_id=1, source_target_pairs={{0,1},{1,0},{2,3},{3,2},{4,5},{5,4},{6,7},{7,6},{8,9},{9,8},{10,11... | collective-permute-start | bytes 1179656 | tf_op jit(solution)/shard_map/ppermute | solution.py:57
  129.0 6.3 %collective-permute-start.17 = (bf16[256,128]{1,0:T(8,128)(2,1)}, bf16[256,128]{1,0:T(8,128)(2,1)S(1)}, u32[]{:S(2)}, u32[]{:S(2)}) collective-permute-start(bf16[256,128]{1,0:T(8,128)(2,1)} %get-tuple-element.111.own_ref), channel_id=1, source_target_pairs={{0,8},{4,12},{8,0},{12,4},{16,24},{20,28},{24,16},{28,20},{1,9},{5... | collective-permute-start | bytes 196616 | tf_op jit(solution)/shard_map/ppermute | solution.py:57
  137.8 10.1 %collective-permute-start.18 = (bf16[256,128]{1,0:T(8,128)(2,1)}, bf16[256,128]{1,0:T(8,128)(2,1)S(1)}, u32[]{:S(2)}, u32[]{:S(2)}) collective-permute-start(bf16[256,128]{1,0:T(8,128)(2,1)} %get-tuple-element.114), channel_id=1, source_target_pairs={{0,16},{4,20},{8,24},{12,28},{16,0},{20,4},{24,8},{28,12},{1,17},{... | collective-permute-start | bytes 196616 | tf_op jit(solution)/shard_map/ppermute | solution.py:57
  159.2 16.6 %collective-permute-start.9 = (bf16[192,1024]{1,0:T(8,128)(2,1)S(1)}, bf16[192,1024]{1,0:T(8,128)(2,1)S(1)}, u32[]{:S(2)}, u32[]{:S(2)}) collective-permute-start(bf16[192,1024]{1,0:T(8,128)(2,1)S(1)} %add.52.mine_a), channel_id=1, source_target_pairs={{0,2},{1,3},{2,0},{3,1},{4,6},{5,7},{6,4},{7,5},{8,10},{9,11},{10,... | collective-permute-start | bytes 1179656 | tf_op jit(solution)/shard_map/ppermute | solution.py:57
  172.9 39.4 %collective-permute-start.29 = (bf16[512,1024]{1,0:T(8,128)(2,1)}, bf16[512,1024]{1,0:T(8,128)(2,1)S(1)}, u32[]{:S(2)}, u32[]{:S(2)}) collective-permute-start(bf16[512,1024]{1,0:T(8,128)(2,1)} %get-tuple-element.131), channel_id=1, source_target_pairs={{0,4},{4,0},{8,12},{12,8},{16,20},{20,16},{24,28},{28,24},{1,5},{5... | collective-permute-start | bytes 3145736 | tf_op jit(solution)/shard_map/ppermute | solution.py:57
  175.2 24.0 %collective-permute-start.24 = (f32[64,128]{1,0:T(8,128)S(1)}, f32[64,128]{1,0:T(8,128)S(1)}, u32[]{:S(2)}, u32[]{:S(2)}) collective-permute-start(f32[64,128]{1,0:T(8,128)S(1)} %pad_bitcast_fusion), channel_id=1, source_target_pairs={{0,4},{4,0},{8,12},{12,8},{16,20},{20,16},{24,28},{28,24},{1,5},{5... | collective-permute-start | bytes 98312 | tf_op jit(solution)/shard_map/ppermute | solution.py:57
  175.8 29.2 %collective-permute-start.10 = (bf16[192,1024]{1,0:T(8,128)(2,1)S(1)}, bf16[192,1024]{1,0:T(8,128)(2,1)S(1)}, u32[]{:S(2)}, u32[]{:S(2)}) collective-permute-start(bf16[192,1024]{1,0:T(8,128)(2,1)S(1)} %add.52.mine_a), channel_id=1, source_target_pairs={{0,1},{1,0},{2,3},{3,2},{4,5},{5,4},{6,7},{7,6},{8,9},{9,8},{10,11... | collective-permute-start | bytes 1179656 | tf_op jit(solution)/shard_map/ppermute | solution.py:57
  175.8 29.2 %collective-permute-start.11 = (bf16[192,1024]{1,0:T(8,128)(2,1)S(1)}, bf16[192,1024]{1,0:T(8,128)(2,1)S(1)}, u32[]{:S(2)}, u32[]{:S(2)}) collective-permute-start(bf16[192,1024]{1,0:T(8,128)(2,1)S(1)} %collective-permute-done.9.mine_b), channel_id=1, source_target_pairs={{0,1},{1,0},{2,3},{3,2},{4,5},{5,4},{6,7},{7,6},{8,9},{9,8},{10,11... | collective-permute-start | bytes 1179656 | tf_op jit(solution)/shard_map/ppermute | solution.py:57
  199.3 12.9 %collective-permute-start.20 = (bf16[192,1024]{1,0:T(8,128)(2,1)}, bf16[192,1024]{1,0:T(8,128)(2,1)S(1)}, u32[]{:S(2)}, u32[]{:S(2)}) collective-permute-start(bf16[192,1024]{1,0:T(8,128)(2,1)} %get-tuple-element.121), channel_id=1, source_target_pairs={{0,1},{1,0},{2,3},{3,2},{4,5},{5,4},{6,7},{7,6},{8,9},{9,8},{10,11... | collective-permute-start | bytes 1179656 | tf_op jit(solution)/shard_map/ppermute | solution.py:57
  204.9 6.5 %collective-permute-start.26 = (f32[64,128]{1,0:T(8,128)S(1)}, f32[64,128]{1,0:T(8,128)S(1)}, u32[]{:S(2)}, u32[]{:S(2)}) collective-permute-start(f32[64,128]{1,0:T(8,128)S(1)} %fusion.5), channel_id=1, source_target_pairs={{0,16},{4,20},{8,24},{12,28},{16,0},{20,4},{24,8},{28,12},{1,17},{... | collective-permute-start | bytes 98312 | tf_op jit(solution)/shard_map/ppermute | solution.py:57
  212.3 11.8 %collective-permute-start.21 = (bf16[192,1024]{1,0:T(8,128)(2,1)S(1)}, bf16[192,1024]{1,0:T(8,128)(2,1)S(1)}, u32[]{:S(2)}, u32[]{:S(2)}) collective-permute-start(bf16[192,1024]{1,0:T(8,128)(2,1)S(1)} %add.54.mine_a), channel_id=1, source_target_pairs={{0,2},{1,3},{2,0},{3,1},{4,6},{5,7},{6,4},{7,5},{8,10},{9,11},{10,... | collective-permute-start | bytes 1179656 | tf_op jit(solution)/shard_map/ppermute | solution.py:57
  212.5 25.3 %collective-permute-start.30 = (bf16[256,1024]{1,0:T(8,128)(2,1)S(1)}, bf16[256,1024]{1,0:T(8,128)(2,1)S(1)}, u32[]{:S(2)}, u32[]{:S(2)}) collective-permute-start(bf16[256,1024]{1,0:T(8,128)(2,1)S(1)} %get-tuple-element.153), channel_id=1, source_target_pairs={{0,8},{4,12},{8,0},{12,4},{16,24},{20,28},{24,16},{28,20},{1,9},{5... | collective-permute-start | bytes 1572872 | tf_op jit(solution)/shard_map/ppermute | solution.py:57
  214.4 9.7 %collective-permute-start.28 = (f32[9,128]{1,0:T(8,128)S(1)}, f32[9,128]{1,0:T(8,128)S(1)}, u32[]{:S(2)}, u32[]{:S(2)}) collective-permute-start(f32[9,128]{1,0:T(8,128)S(1)} %slice_add_fusion.4), channel_id=1, source_target_pairs={{0,2},{1,3},{2,0},{3,1},{4,6},{5,7},{6,4},{7,5},{8,10},{9,11},{10,... | collective-permute-start | bytes 13832 | tf_op jit(solution)/shard_map/ppermute | solution.py:57
  224.1 16.3 %collective-permute-start.22 = (bf16[192,1024]{1,0:T(8,128)(2,1)S(1)}, bf16[192,1024]{1,0:T(8,128)(2,1)S(1)}, u32[]{:S(2)}, u32[]{:S(2)}) collective-permute-start(bf16[192,1024]{1,0:T(8,128)(2,1)S(1)} %add.54.mine_a), channel_id=1, source_target_pairs={{0,1},{1,0},{2,3},{3,2},{4,5},{5,4},{6,7},{7,6},{8,9},{9,8},{10,11... | collective-permute-start | bytes 1179656 | tf_op jit(solution)/shard_map/ppermute | solution.py:57
  224.1 16.3 %collective-permute-start.23 = (bf16[192,1024]{1,0:T(8,128)(2,1)S(1)}, bf16[192,1024]{1,0:T(8,128)(2,1)S(1)}, u32[]{:S(2)}, u32[]{:S(2)}) collective-permute-start(bf16[192,1024]{1,0:T(8,128)(2,1)S(1)} %collective-permute-done.21.mine_b), channel_id=1, source_target_pairs={{0,1},{1,0},{2,3},{3,2},{4,5},{5,4},{6,7},{7,6},{8,9},{9,8},{10,11... | collective-permute-start | bytes 1179656 | tf_op jit(solution)/shard_map/ppermute | solution.py:57
  237.9 14.8 %collective-permute-start.31 = (bf16[128,1024]{1,0:T(8,128)(2,1)S(1)}, bf16[128,1024]{1,0:T(8,128)(2,1)S(1)}, u32[]{:S(2)}, u32[]{:S(2)}) collective-permute-start(bf16[128,1024]{1,0:T(8,128)(2,1)S(1)} %slice_add_fusion.2), channel_id=1, source_target_pairs={{0,16},{4,20},{8,24},{12,28},{16,0},{20,4},{24,8},{28,12},{1,17},{... | collective-permute-start | bytes 786440 | tf_op jit(solution)/shard_map/ppermute | solution.py:57
  (51 other events, 339.2 us)
Sparse Core Ops, SparseCore 0:
  117.1 72.5 reduce-scatter.2
  193.3 82.0 reduce-scatter.4

commit v2 on v1

v2 whole, which is shorter than its diff:
```python
import functools
import math

import jax
import jax.numpy as jnp
from jax import lax
from jax.experimental import pallas as pl
from jax.experimental.pallas import tpu as pltpu
from jax.sharding import PartitionSpec as P

HEAD_DIM = 128
CHUNK = 128
LANES = 128
SUB = 8
Q_SCALE = HEAD_DIM ** (-0.5)
VMEM_SLACK = 14 * 1024 * 1024

bf16 = jnp.bfloat16
f32 = jnp.float32


def mm(left, right, left_dim=1, right_dim=0):
    return lax.dot_general(
        left.astype(bf16),
        right.astype(bf16),
        (((left_dim,), (right_dim,)), ((), ())),
        preferred_element_type=f32,
    )


def sigmoid(value):
    return 1.0 / (1.0 + jnp.exp(-value))


class Free:
    def __init__(self, value):
        self.value = value


class Held(Free):
    pass


class Far(Free):
    pass


class Place:
    def __getitem__(self, which):
        return lax.axis_index(("seq", "head")[which])


class Direct:
    def __init__(self, shape, dtype):
        self.shape, self.dtype = tuple(shape), dtype


def kernel_call(body, out_shapes, place, *args, scratch=(), name, flops=0, deps=()):
    vmem = pl.BlockSpec(memory_space=pltpu.VMEM)
    smem = pl.BlockSpec(memory_space=pltpu.SMEM)
    anywhere = pl.BlockSpec(memory_space=pl.ANY)
    size_of = lambda a: math.prod(a.shape) * jnp.dtype(a.dtype).itemsize
    held = sum(size_of(s) for s in scratch if hasattr(s, "dtype") and not is_semaphore(s))
    operands, specs, moved = [], [], 0
    here = Place()
    for arg in args:
        if isinstance(arg, Free):
            value = arg.value
            if not type(arg) is Free:
                value = pltpu.with_memory_space_constraint(value, pltpu.HBM)
            operands.append(value)
            specs.append(anywhere if isinstance(arg, Far) else vmem)
            if not isinstance(arg, Far):
                held += size_of(value)
        elif arg.ndim == 1:
            operands.append(arg)
            specs.append(smem)
        else:
            operands.append(pltpu.with_memory_space_constraint(arg, pltpu.VMEM))
            specs.append(vmem)
        moved += size_of(operands[-1])
    count = len(args)
    run = lambda *refs: body(here, *refs[:count], *refs[count + len(deps) :])
    operands += [
        pltpu.with_memory_space_constraint(dep.value, pltpu.HBM)
        if isinstance(dep, Free)
        else pltpu.with_memory_space_constraint(dep, pltpu.VMEM)
        for dep in deps
    ]
    specs += [anywhere] * len(deps)
    results, result_specs = [], []
    for out in out_shapes:
        moved += size_of(out)
        if isinstance(out, Direct):
            results.append(pltpu.HBM(out.shape, out.dtype))
            result_specs.append(anywhere)
        else:
            results.append(out)
            result_specs.append(vmem)
            if isinstance(out, jax.ShapeDtypeStruct) or out.memory_space == pltpu.HBM:
                held += size_of(out)
    return pl.pallas_call(
        run,
        out_shape=tuple(results),
        in_specs=specs,
        out_specs=tuple(result_specs),
        scratch_shapes=list(scratch),
        compiler_params=pltpu.CompilerParams(vmem_limit_bytes=int(held) + VMEM_SLACK),
        cost_estimate=pl.CostEstimate(flops=0, bytes_accessed=0, transcendentals=0),
        name=name,
    )(*operands)


def stored(shape, dtype):
    return pltpu.HBM(tuple(shape), dtype)


def send_out(source, target, sems, index):
    copy = pltpu.make_async_copy(source, target, sems.at[index])
    copy.start()
    return copy


def is_semaphore(scratch):
    return not (
        jnp.issubdtype(scratch.dtype, jnp.floating) or jnp.issubdtype(scratch.dtype, jnp.integer)
    )


def final(shape, dtype):
    return jax.ShapeDtypeStruct(tuple(shape), dtype)


def shaped(shape, dtype):
    return pltpu.VMEM(tuple(shape), dtype)


def swap(value, axis, bit):
    count = lax.axis_size(axis)
    return lax.ppermute(value, axis, [(s, s ^ bit) for s in range(count)])


def shift(value, axis, step):
    count = lax.axis_size(axis)
    return lax.ppermute(
        value, axis, [(s, s + step) for s in range(count) if 0 <= s + step < count]
    )


def bit_of(place_ref, which, bit):
    return lax.rem(lax.shift_right_logical(place_ref[which], bit), 2)


def chosen(flag, when_one, when_zero):
    return jnp.where(flag == 1, when_one, when_zero)


def tri_masks():
    rows = lax.broadcasted_iota(jnp.int32, (CHUNK, CHUNK), 0)
    cols = lax.broadcasted_iota(jnp.int32, (CHUNK, CHUNK), 1)
    return rows, cols


def unit_inverses(lowers):
    rows, cols = tri_masks()
    eye = jnp.where(rows == cols, 1.0, 0.0).astype(f32)
    width = 1
    inverses = None
    while width < CHUNK:
        shift_bits = width.bit_length() - 1
        row_block = lax.shift_right_logical(rows, shift_bits)
        col_block = lax.shift_right_logical(cols, shift_bits)
        within = (
            lax.shift_right_logical(row_block, 1) == lax.shift_right_logical(col_block, 1)
        ) & (row_block != col_block)
        couplings = [jnp.where(within, low, 0.0) for low in lowers]
        if inverses is None:
            inverses = [eye - coupling for coupling in couplings]
        else:
            halves = [mm(inv, coupling) for inv, coupling in zip(inverses, couplings)]
            inverses = [inv - mm(half, inv) for inv, half in zip(inverses, halves)]
        width *= 2
    return inverses


def project_kernel(
    place, x_hbm, wq_hbm, wk_hbm, wv_hbm, wg_hbm, gain_hbm, wb_hbm, bias_hbm, seg_hbm, wo_hbm,
    p_ref, beta_ref, segc_ref, tail_ref, a_hbm, gate_hbm, wb8_hbm, wo_out,
    x_s, weights, gain_s, wb_s, bias_s, seg_s, a_s, gate_s, wb8_s, wo_s, arrived, left,
):
    rows = x_s.shape[0]
    head_width = wq_hbm.shape[1]
    heads = head_width // LANES
    pairs = ((x_hbm, x_s), (gain_hbm, gain_s), (seg_hbm, seg_s), (wb_hbm, wb_s), (bias_hbm, bias_s))
    pairs += ((wo_hbm, wo_s),)
    pairs += tuple(
        (source, weights.at[index]) for index, source in enumerate((wg_hbm, wq_hbm, wk_hbm, wv_hbm))
    )
    copies = [send_out(source, target, arrived, index) for index, (source, target) in enumerate(pairs)]
    for copy in copies[:5]:
        copy.wait()
    wo_copy, *copies = copies[5:]
    segr = seg_s[...].astype(f32)
    wb8_s[...] = jnp.zeros(wb8_s.shape, f32)
    wb8_s[0:heads, :] = wb_s[...].astype(f32)
    leaving = [send_out(wb8_s, wb8_hbm, left, 2)]
    x = x_s[...].astype(f32)
    scale = lax.rsqrt(jnp.mean(x * x, axis=-1, keepdims=True) + 1e-06)
    a = (x * scale * gain_s[...]).astype(bf16)
    a_s[...] = a
    tail_ref[:, 3 * head_width + LANES :] = a.astype(f32)[rows - SUB :, :]
    leaving.append(send_out(a_s, a_hbm, left, 0))
    logits = mm(a, wb8_s[...], 1, 1)
    for head in range(heads):
        column = logits[:, head : head + 1] + bias_s[:, head : head + 1]
        beta_ref[:, head * LANES : (head + 1) * LANES] = sigmoid(
            jnp.broadcast_to(column, (rows, LANES))
        )
    for chunk in range(rows // CHUNK):
        ids = jnp.broadcast_to(segr[chunk : chunk + 1, :], (CHUNK, LANES))
        turned = ids.T
        segc_ref[chunk * CHUNK : (chunk + 1) * CHUNK, :] = turned
        if chunk == rows // CHUNK - 1:
            tail_ref[:, 3 * head_width : 3 * head_width + LANES] = turned[CHUNK - SUB :, :]
    wo_copy.wait()
    leaving.append(send_out(wo_s, wo_out, left, 3))
    copies[0].wait()
    gate_s[...] = mm(a, weights[0])
    leaving.append(send_out(gate_s, gate_hbm, left, 1))
    for part in range(3):
        copies[part + 1].wait()
        value = mm(a, weights[part + 1])
        cols = slice(part * head_width, (part + 1) * head_width)
        low = value.astype(bf16)
        p_ref[:, cols] = low
        tail_ref[:, cols] = low.astype(f32)[rows - SUB :, :]
    for copy in leaving:
        copy.wait()


def lag_masks(joined_ids, lags):
    rows = joined_ids.shape[0] - SUB
    ids = joined_ids[SUB : SUB + rows, :]
    return [None] + [
        jnp.where(joined_ids[SUB - lag : SUB - lag + rows, :] == ids, 1.0, 0.0)
        for lag in range(1, lags + 1)
    ]


def conv_sum(joined, taps_ref, masks, part, head, head_width, rows):
    lags = taps_ref.shape[1] - 1
    col = part * head_width + head * LANES
    tap_cols = slice(head * LANES, (head + 1) * LANES)
    total = taps_ref[part, lags : lags + 1, tap_cols] * joined[SUB : SUB + rows, col : col + LANES]
    for lag in range(1, lags + 1):
        tap = taps_ref[part, lags - lag : lags - lag + 1, tap_cols]
        total = total + tap * joined[SUB - lag : SUB - lag + rows, col : col + LANES] * masks[lag]
    return total


def chunk_flags(joined_ids, chunk):
    start = chunk * CHUNK
    ids = joined_ids[SUB + start : SUB + start + CHUNK, :]
    same = jnp.where(ids == ids.T, 1.0, 0.0)
    before = joined_ids[SUB + start - 1 : SUB + start, :]
    final_id = joined_ids[SUB + start + CHUNK - 1 : SUB + start + CHUNK, :]
    opened = jnp.where(ids == before, 1.0, 0.0)
    closing = jnp.where(ids == final_id, 1.0, 0.0)
    kept = jnp.where(final_id == before, 1.0, 0.0)
    return same, opened, closing, kept


def delta_kernel(
    place, p_ref, tail_ref, taps_ref, segc_ref, beta_ref,
    maps_ref, mix_ref, back_ref, facts_ref, before_ref,
    joined, joined_ids,
):
    rows, width = p_ref.shape
    head_width = width // 3
    heads = head_width // LANES
    chunks = rows // CHUNK
    first = 2 * SUB
    joined[0:SUB, :] = tail_ref[:, :width]
    joined[SUB : SUB + rows, :] = p_ref[...].astype(f32)
    joined_ids[0:SUB, :] = tail_ref[:, width : width + LANES]
    joined_ids[SUB : SUB + rows, :] = segc_ref[...]
    facts_ref[SUB:, 0:head_width] = beta_ref[...]
    facts_ref[0:SUB, 0:head_width] = jnp.zeros((SUB, head_width), f32)
    facts_ref[:, head_width:] = joined_ids[...]
    before_ref[...] = jnp.concatenate(
        [jnp.zeros((SUB, before_ref.shape[1]), f32), tail_ref[:, width + LANES :]], axis=0
    ).astype(bf16)
    back_ref[first:, 0:width] = p_ref[...]
    back_ref[0:first, 0:width] = jnp.concatenate(
        [jnp.zeros((SUB, width), f32), tail_ref[:, :width]], axis=0
    ).astype(bf16)
    back_ref[0:first, width:] = jnp.zeros((first, back_ref.shape[1] - width), bf16)
    masks = lag_masks(joined_ids, taps_ref.shape[1] - 1)
    for part in range(3):
        for head in range(heads):
            total = conv_sum(joined, taps_ref, masks, part, head, head_width, rows)
            z = total * sigmoid(total)
            if part < 2:
                z = z * lax.rsqrt(jnp.sum(z * z, axis=-1, keepdims=True) + 1e-06)
                if part == 0:
                    z = z * Q_SCALE
            col = width + part * head_width + head * LANES
            back_ref[first:, col : col + LANES] = z.astype(bf16)
    row_ids, col_ids = tri_masks()
    flags = [chunk_flags(joined_ids, chunk) for chunk in range(chunks)]
    mix_ref[rows:, :] = jnp.concatenate(
        [jnp.concatenate([flags[min(row, chunks - 1)][3]] * (4 * heads), axis=1) for row in range(2 * SUB)],
        axis=0,
    ).astype(bf16)
    sets = [(head, chunk) for head in range(heads) for chunk in range(chunks)]

    def at_of(head, chunk, part=0):
        col = part * head_width + head * LANES
        return (slice(chunk * CHUNK, (chunk + 1) * CHUNK), slice(col, col + LANES))

    def kept_at(head, chunk, part):
        col = (3 + part) * head_width + head * LANES
        return (slice(first + chunk * CHUNK, first + (chunk + 1) * CHUNK), slice(col, col + LANES))

    lowers = []
    for head, chunk in sets:
        same = flags[chunk][0]
        q, k = back_ref[kept_at(head, chunk, 0)], back_ref[kept_at(head, chunk, 1)]
        inner = mm(jnp.concatenate([q, k], axis=0), k, 1, 1)
        scores = jnp.where(row_ids >= col_ids, inner[:CHUNK] * same, 0.0)
        back_ref[kept_at(head, chunk, 6)] = scores.astype(bf16)
        lowers.append(
            jnp.where(row_ids > col_ids, inner[CHUNK:] * same * beta_ref[at_of(head, chunk)], 0.0)
        )
    inverses = unit_inverses(lowers)
    eye = jnp.where(row_ids == col_ids, 1.0, 0.0).astype(f32)
    maps = [
        jnp.concatenate([eye, jnp.zeros((HEAD_DIM, HEAD_DIM), f32)], axis=1) for _ in range(heads)
    ]
    products = []
    for (head, chunk), inverse in zip(sets, inverses):
        beta = beta_ref[at_of(head, chunk)]
        k = back_ref[kept_at(head, chunk, 1)].astype(f32)
        v = back_ref[kept_at(head, chunk, 2)].astype(f32)
        both = jnp.concatenate([beta * k, beta * v], axis=1)
        products.append(mm(inverse, both))
    steps = {}
    for (head, chunk), inverse, product in zip(sets, inverses, products):
        same, opened, closing, kept = flags[chunk]
        w_rows, u_rows = product[:, :HEAD_DIM], product[:, HEAD_DIM:]
        back_ref[kept_at(head, chunk, 3)] = w_rows.astype(bf16)
        back_ref[kept_at(head, chunk, 4)] = u_rows.astype(bf16)
        back_ref[kept_at(head, chunk, 5)] = inverse.astype(bf16)
        both = jnp.concatenate([opened * w_rows, u_rows], axis=1)
        k = back_ref[kept_at(head, chunk, 1)].astype(f32)
        q = back_ref[kept_at(head, chunk, 0)].astype(f32)
        step = mm(closing * k, both, 0, 0)
        through = mm(back_ref[kept_at(head, chunk, 6)], both)
        mix_ref[at_of(head, chunk, 0)] = (opened * q - through[:, :HEAD_DIM]).astype(bf16)
        mix_ref[at_of(head, chunk, 1)] = step[:, :HEAD_DIM].astype(bf16)
        mix_ref[at_of(head, chunk, 2)] = through[:, HEAD_DIM:].astype(bf16)
        mix_ref[at_of(head, chunk, 3)] = step[:, HEAD_DIM:].astype(bf16)
        steps[head, chunk] = step
    for chunk in range(chunks):
        kept = flags[chunk][3]
        kept_wide = jnp.concatenate([kept, kept], axis=1)
        for head in range(heads):
            step = steps[head, chunk]
            pushed = kept_wide * maps[head] - mm(step[:, :HEAD_DIM], maps[head])
            maps[head] = jnp.concatenate(
                [pushed[:, :HEAD_DIM], pushed[:, HEAD_DIM:] + step[:, HEAD_DIM:]], axis=1
            )
    for head in range(heads):
        maps_ref[head * HEAD_DIM : (head + 1) * HEAD_DIM, :] = maps[head][:, :HEAD_DIM].astype(bf16)
        base = (heads + head) * HEAD_DIM
        maps_ref[base : base + HEAD_DIM, :] = maps[head][:, HEAD_DIM:].astype(bf16)


def park_kernel(count, place, *refs):
    sources, targets, left = refs[:count], refs[count : 2 * count], refs[-1]
    copies = []
    for index, (source, target) in enumerate(zip(sources, targets)):
        if source.shape != target.shape:
            source = source.at[:, 0 : target.shape[1]]
        copies.append(send_out(source, target, left, index))
    for copy in copies:
        copy.wait()


def park(place, *pairs, name, deps=()):
    arrays = [value.value if isinstance(value, Free) else value for value, _ in pairs]
    return kernel_call(
        functools.partial(park_kernel, len(pairs)),
        [
            Direct((array.shape[0], array.shape[1] if cols is None else cols), array.dtype)
            for array, (_, cols) in zip(arrays, pairs)
        ],
        place,
        *[value for value, _ in pairs],
        scratch=(pltpu.SemaphoreType.DMA((len(pairs),)),),
        name=name,
        deps=deps,
    )


def scan_round_kernel(bit, place, own_ref, other_ref, prefix_ref, pack_ref, total_ref, prefix_out, pack_out):
    upper = bit_of(place, 0, bit)
    half = own_ref.shape[0] // 2
    heads = half // HEAD_DIM
    base = 2 * half * bit
    if bit:
        pack_out[0:base, :] = pack_ref[...]
    for head in range(heads):
        m_at = slice(head * HEAD_DIM, (head + 1) * HEAD_DIM)
        a_at = slice((heads + head) * HEAD_DIM, (heads + head + 1) * HEAD_DIM)
        low_at = slice(base + head * HEAD_DIM, base + (head + 1) * HEAD_DIM)
        suffix_at = slice(base + half + head * HEAD_DIM, base + half + (head + 1) * HEAD_DIM)
        own_m, own_a = own_ref[m_at, :].astype(f32), own_ref[a_at, :].astype(f32)
        other_m, other_a = other_ref[m_at, :].astype(f32), other_ref[a_at, :].astype(f32)
        high_m, high_a = chosen(upper, own_m, other_m), chosen(upper, own_a, other_a)
        low_m, low_a = chosen(upper, other_m, own_m), chosen(upper, other_a, own_a)
        pack_out[low_at, :] = low_m.astype(bf16)
        total = mm(high_m, jnp.concatenate([low_m, low_a], axis=1))
        added_part = (total[:, HEAD_DIM:] + high_a).astype(bf16)
        if total_ref.shape[0] == own_ref.shape[0]:
            total_ref[m_at, :] = total[:, :HEAD_DIM].astype(bf16)
            total_ref[a_at, :] = added_part
        else:
            total_ref[m_at, :] = added_part
        if bit == 0:
            rows, cols = tri_masks()
            eye = jnp.where(rows == cols, 1.0, 0.0).astype(f32)
            prefix_out[m_at, :] = chosen(upper, other_m, eye).astype(bf16)
            prefix_out[a_at, :] = chosen(upper, other_a, jnp.zeros_like(other_a)).astype(bf16)
            pack_out[suffix_at, :] = chosen(upper, eye, other_m.T).astype(bf16)
        else:
            before_m, before_a = prefix_ref[m_at, :].astype(f32), prefix_ref[a_at, :].astype(f32)
            at = base - half + head * HEAD_DIM
            after_m = pack_ref[at : at + HEAD_DIM, :].astype(f32)
            joint = mm(before_m, jnp.concatenate([other_m, other_a], axis=1))
            prefix_out[m_at, :] = chosen(upper, joint[:, :HEAD_DIM], before_m).astype(bf16)
            prefix_out[a_at, :] = chosen(
                upper, joint[:, HEAD_DIM:] + before_a, before_a
            ).astype(bf16)
            pack_out[suffix_at, :] = chosen(upper, after_m, mm(after_m, other_m, 1, 1)).astype(bf16)


def back_round_kernel(bit, place, pack_ref, own_ref, other_ref, after_ref, total_ref, after_out):
    upper = bit_of(place, 0, bit)
    half = own_ref.shape[0]
    base = 2 * half * bit
    for head in range(half // HEAD_DIM):
        at = slice(head * HEAD_DIM, (head + 1) * HEAD_DIM)
        own, other = own_ref[at, :].astype(f32), other_ref[at, :].astype(f32)
        high, low = chosen(upper, own, other), chosen(upper, other, own)
        low_m = pack_ref[base + head * HEAD_DIM : base + (head + 1) * HEAD_DIM, :]
        total_ref[at, :] = (mm(low_m, high, 0, 0) + low).astype(bf16)
        if bit == 0:
            after_out[at, :] = chosen(upper, jnp.zeros_like(other), other).astype(bf16)
        else:
            start = base - half + head * HEAD_DIM
            suffix_m = pack_ref[start : start + HEAD_DIM, :]
            after = after_ref[at, :].astype(f32)
            after_out[at, :] = chosen(upper, after, mm(suffix_m, other) + after).astype(bf16)


def mixer_kernel(
    last_bit, place, prefix_ref, other_a_ref, mix_ref, gate_ref, hgain_ref,
    y_ref, o_ref, keep_ref,
):
    rows, head_width = gate_ref.shape
    heads = head_width // LANES
    upper = bit_of(place, 0, last_bit)
    kept_rows = mix_ref[rows:, 0:LANES].astype(f32)
    for head in range(heads):
        m_at = slice(head * HEAD_DIM, (head + 1) * HEAD_DIM)
        a_at = slice((heads + head) * HEAD_DIM, (heads + head + 1) * HEAD_DIM)
        before_m, before_a = prefix_ref[m_at, :], prefix_ref[a_at, :].astype(f32)
        state = chosen(upper, mm(before_m, other_a_ref[m_at, :]) + before_a, before_a)
        for chunk in range(rows // CHUNK):
            chunk_rows = slice(chunk * CHUNK, (chunk + 1) * CHUNK)
            cols = [
                slice(part * head_width + head * LANES, part * head_width + (head + 1) * LANES)
                for part in range(4)
            ]
            at = (chunk_rows, cols[0])
            low = state.astype(bf16)
            keep_ref[at] = low
            out = mm(mix_ref[at], low) + mix_ref[chunk_rows, cols[2]].astype(f32)
            o_ref[at] = out
            state = (
                kept_rows[chunk : chunk + 1, :] * state
                - mm(mix_ref[chunk_rows, cols[1]], low)
                + mix_ref[chunk_rows, cols[3]].astype(f32)
            )
            gate = gate_ref[at]
            scale = lax.rsqrt(jnp.mean(out * out, axis=-1, keepdims=True) + 1e-05)
            y = (out * scale * hgain_ref[...] * (gate * sigmoid(gate))).astype(bf16)
            y_ref[at] = y
            keep_ref[chunk_rows, cols[1]] = y


def ffn_kernel(
    share, place, x_ref, g_ref, fgain_ref, wg_ref, wu_ref, wd_ref, *rest,
):
    *parts, send_ref, h_hbm, grads_hbm, hid_hbm, keep_hbm, h_s, grads_s, hid_s, keep_s, whole, left = rest
    y_refs, wo_refs = parts[: len(parts) // 2], parts[len(parts) // 2 :]
    att = None
    for y_ref, wo_ref in zip(y_refs, wo_refs):
        part = mm(y_ref[...], wo_ref[...])
        att = part if att is None else att + part
    h = x_ref[...].astype(f32) + att
    h_s[...] = h
    leaving = [send_out(h_s, h_hbm, left, 0)]
    scale = lax.rsqrt(jnp.mean(h * h, axis=-1, keepdims=True) + 1e-06)
    b = (h * scale * fgain_ref[...]).astype(bf16)
    gate = mm(b, wg_ref[...], 1, 1)
    up = mm(b, wu_ref[...], 1, 1)
    sg = sigmoid(gate)
    act = gate * sg
    hid = (act * up).astype(bf16)
    hid_s[...] = hid
    leaving.append(send_out(hid_s, hid_hbm, left, 2))
    dhid = mm(g_ref[...], wd_ref[...], 1, 1)
    dgate = (dhid * up * (sg * (1.0 + gate * (1.0 - sg)))).astype(bf16)
    dup = (dhid * act).astype(bf16)
    owners = grads_s.shape[0] // (3 * share)
    for index, (left_side, right_side) in enumerate(((g_ref[...], hid), (b, dgate), (b, dup))):
        grad = mm(left_side, right_side, 0, 0).astype(bf16)
        for owner in range(owners):
            at = (3 * owner + index) * share
            grads_s[at : at + share, :] = grad[owner * share : (owner + 1) * share]
    leaving.append(send_out(grads_s, grads_hbm, left, 1))
    whole[...] = mm(dgate, wg_ref[...]) + mm(dup, wu_ref[...])
    split_rows(place, whole, keep_s, send_ref)
    leaving.append(send_out(keep_s, keep_hbm, left, 3))
    for copy in leaving:
        copy.wait()


def split_rows(place, whole, keep_ref, send_ref):
    half = whole.shape[0] // 2
    core = bit_of(place, 1, 0)
    keep_ref[0:half, :] = whole[pl.ds(pl.multiple_of(core * half, half), half), :].astype(bf16)
    send_ref[0:half, :] = whole[pl.ds(pl.multiple_of((1 - core) * half, half), half), :].astype(bf16)


def join_rows(place, mine, theirs, whole):
    half = whole.shape[0] // 2
    core = bit_of(place, 1, 0)
    mine, theirs = mine[:half], theirs[:half]
    whole[pl.ds(pl.multiple_of(core * half, half), half), :] = mine
    whole[pl.ds(pl.multiple_of((1 - core) * half, half), half), :] = theirs


def emit_shares(place, bits, whole, keep_ref, send_ref):
    order = [0]
    for bit in reversed(bits[1:]):
        order = order + [relative | (1 << bit) for relative in order]
    block = whole.shape[0] // (2 * len(order))
    for index, relative in enumerate(order):
        for ref, first in ((keep_ref, 0), (send_ref, 1 << bits[0])):
            owner = lax.bitwise_xor(place[0], jnp.int32(relative | first))
            ref[index * block : (index + 1) * block, :] = whole[
                pl.ds(pl.multiple_of(owner * block, block), block), :
            ]


def share_round_kernel(place, keep_ref, got_ref, *rest):
    keep_out, send_out = rest[-2:]
    half = keep_out.shape[0]
    keep_out[...] = keep_ref[:half] + got_ref[:half]
    send_out[...] = keep_ref[half:] + got_ref[half:]


def out_part_kernel(place, hid_ref, wd_ref, keep_ref, send_ref, whole):
    whole[...] = mm(hid_ref[...], wd_ref[...])
    split_rows(place, whole, keep_ref, send_ref)


def early_grads_kernel(bits, place, gh_ref, y_ref, a_ref, dgr_ref, keep_ref, send_ref, whole):
    width = dgr_ref.shape[1]
    whole[:, :width] = mm(gh_ref[...], y_ref[:, width:], 0, 0).astype(bf16)
    whole[:, width:] = mm(a_ref[...], dgr_ref[...], 0, 0).astype(bf16)
    emit_shares(place, bits, whole, keep_ref, send_ref)


def early_sum_kernel(place, keep_ref, got_ref, turned_ref, plain_ref):
    total = keep_ref[...].astype(f32) + got_ref[...].astype(f32)
    width = plain_ref.shape[1]
    turned_ref[...] = total[:, :width].T
    plain_ref[...] = total[:, width:]


def project_sum_kernel(place, keep_ref, got_ref, *out_refs):
    total = keep_ref[...].astype(f32) + got_ref[...].astype(f32)
    width = out_refs[0].shape[1]
    for index, out_ref in enumerate(out_refs):
        out_ref[...] = total[:, index * width : (index + 1) * width]


def ffn_shares_kernel(place, shares_ref, down_ref, gate_ref, up_ref):
    share = shares_ref.shape[0] // 3
    for index, ref in enumerate((down_ref, gate_ref, up_ref)):
        ref[...] = shares_ref[index * share : (index + 1) * share].astype(f32).T


def residual_back_kernel(
    place, mine, theirs, h_ref, g_ref, fgain_ref, wo_ref, o_ref,
    gate_ref, hgain_ref, steps_ref,
    gh_ref, pull_ref, dh_ref, do_ref, dgr_ref, sums_ref, whole,
):
    rows, head_width = o_ref.shape
    heads = head_width // LANES
    join_rows(place, mine[...].astype(f32), theirs[...].astype(f32), whole)
    h = h_ref[...]
    db = whole[...]
    scale = lax.rsqrt(jnp.mean(h * h, axis=-1, keepdims=True) + 1e-06)
    hat = h * scale
    prod = db * hat
    sums_ref[...] = jnp.zeros(sums_ref.shape, f32)
    sums_ref[0:1, :] = jnp.sum(prod, axis=0, keepdims=True)
    inner = jnp.mean(prod * fgain_ref[...], axis=-1, keepdims=True)
    dh = g_ref[...].astype(f32) + scale * (db * fgain_ref[...] - hat * inner)
    dh_ref[...] = dh
    gh = dh.astype(bf16)
    gh_ref[...] = gh
    dy_all = mm(gh, wo_ref[...], 1, 1)
    hg_sum = jnp.zeros((1, LANES), f32)
    for head in range(heads):
        cols = slice(head * LANES, (head + 1) * LANES)
        out, gate, dy = o_ref[:, cols], gate_ref[:, cols], dy_all[:, cols]
        norm = lax.rsqrt(jnp.mean(out * out, axis=-1, keepdims=True) + 1e-05)
        hat_o = out * norm
        sg = sigmoid(gate)
        act = gate * sg
        hg_sum = hg_sum + jnp.sum(dy * hat_o * act, axis=0, keepdims=True)
        dgain = dy * hgain_ref[...]
        dgr_ref[:, cols] = (dgain * hat_o * (sg * (1.0 + gate * (1.0 - sg)))).astype(bf16)
        e = dgain * act
        do_ref[:, cols] = (norm * (e - hat_o * jnp.mean(e * hat_o, axis=-1, keepdims=True))).astype(bf16)
    sums_ref[1:2, 0:LANES] = hg_sum
    chunks = rows // CHUNK
    kept_rows = steps_ref[rows:, 0:LANES].astype(f32)
    pulls = [None] * heads
    for chunk in range(chunks - 1, -1, -1):
        chunk_rows = slice(chunk * CHUNK, (chunk + 1) * CHUNK)
        for head in range(heads):
            cols = slice(head * LANES, (head + 1) * LANES)
            map_cols = slice(head_width + head * LANES, head_width + (head + 1) * LANES)
            local = mm(steps_ref[chunk_rows, cols], do_ref[chunk_rows, cols], 0, 0)
            if pulls[head] is not None:
                local = (
                    local
                    + kept_rows[chunk : chunk + 1, :] * pulls[head]
                    - mm(steps_ref[chunk_rows, map_cols], pulls[head], 0, 0)
                )
            pulls[head] = local
    for head in range(heads):
        pull_ref[head * HEAD_DIM : (head + 1) * HEAD_DIM, :] = pulls[head].astype(bf16)


def delta_back_kernel(
    last_bit, place, taps_ref, back_ref, facts_ref, steps_ref, keep_ref, do_ref,
    pack_ref, after_ref, other_ref,
    gp_ref, halo_ref, small_ref,
    joined, joined_ids, dq_s, du_s, mask_s,
):
    rows, head_width = do_ref.shape
    width = 3 * head_width
    heads = head_width // LANES
    chunks = rows // CHUNK
    lags = taps_ref.shape[1] - 1
    joined[0:SUB, :] = back_ref[0 : 2 * SUB, :width].astype(f32)[SUB:, :]
    joined[SUB : SUB + rows, :] = back_ref[2 * SUB :, :width].astype(f32)
    joined_ids[...] = facts_ref[:, head_width : head_width + LANES]
    masks = lag_masks(joined_ids, lags)
    row_ids, col_ids = tri_masks()
    flags = [chunk_flags(joined_ids, chunk) for chunk in range(chunks)]
    upper = bit_of(place, 0, last_bit)
    sets = [(head, chunk) for head in range(heads) for chunk in range(chunks)]

    def at_of(head, chunk, part=0):
        col = part * head_width + head * LANES
        return (slice(chunk * CHUNK, (chunk + 1) * CHUNK), slice(col, col + LANES))

    def saved(head, chunk, part):
        col = (3 + part) * head_width + head * LANES
        return back_ref[2 * SUB + chunk * CHUNK : 2 * SUB + (chunk + 1) * CHUNK, col : col + LANES]

    state_grads = {}
    for head in range(heads):
        at = slice(head * HEAD_DIM, (head + 1) * HEAD_DIM)
        after = after_ref[at, :].astype(f32)
        start = pack_ref.shape[0] - after_ref.shape[0] + head * HEAD_DIM
        suffix_m = pack_ref[start : start + HEAD_DIM, :]
        grad = chosen(upper, after, mm(suffix_m, other_ref[at, :]) + after)
        for chunk in range(chunks - 1, -1, -1):
            state_grads[head, chunk] = grad
            if chunk:
                low = grad.astype(bf16)
                grad = (
                    flags[chunk][3] * grad
                    - mm(steps_ref[at_of(head, chunk, 1)], low, 0, 0)
                    + mm(steps_ref[at_of(head, chunk)], do_ref[at_of(head, chunk)], 0, 0)
                )
    lane_ids = lax.broadcasted_iota(jnp.int32, (CHUNK, LANES), 1)
    gb_cols = [jnp.zeros((CHUNK, LANES), f32) for _ in range(chunks)]
    for head, chunk in sets:
        same, opened, closing, kept = flags[chunk]
        at = at_of(head, chunk)
        q, k, v, w_rows, u_rows, inverse, scores = (saved(head, chunk, part) for part in range(7))
        kf, vf = k.astype(f32), v.astype(f32)
        beta = facts_ref[
            SUB + chunk * CHUNK : SUB + (chunk + 1) * CHUNK, head * LANES : (head + 1) * LANES
        ]
        state, do = keep_ref[at], do_ref[at]
        sgrad = state_grads[head, chunk].astype(bf16)
        fresh = (u_rows.astype(f32) - opened * mm(w_rows, state)).astype(bf16)
        dfresh = mm(scores, do, 0, 0) + mm(closing * kf, sgrad)
        dscore = jnp.where(row_ids >= col_ids, mm(do, fresh, 1, 1) * same, 0.0).astype(bf16)
        dw = -(opened * mm(dfresh, state, 1, 1))
        dx = mm(inverse, jnp.concatenate([dfresh, dw], axis=1), 0, 0)
        dxv, dxk = dx[:, :HEAD_DIM], dx[:, HEAD_DIM:]
        dlow = mm(dx, jnp.concatenate([u_rows, w_rows], axis=1), 1, 1)
        dlow = jnp.where(row_ids > col_ids, -dlow * same, 0.0)
        inner = mm(k, k, 1, 1)
        dbeta = jnp.sum(dxv * vf + dxk * kf + dlow * inner, axis=-1, keepdims=True)
        glow = (dlow * beta).astype(bf16)
        dq_s[at_of(head, chunk, 0)] = opened * mm(do, state, 1, 1) + mm(dscore, k)
        dq_s[at_of(head, chunk, 1)] = (
            beta * dxk
            + mm(dscore, q, 0, 0)
            + closing * mm(fresh, sgrad, 1, 1)
            + mm(glow, k)
            + mm(glow, k, 0, 0)
        )
        dq_s[at_of(head, chunk, 2)] = beta * dxv
        raw = jnp.broadcast_to(dbeta, (CHUNK, LANES)) * beta * (1.0 - beta)
        gb_cols[chunk] = jnp.where(lane_ids == head, raw, gb_cols[chunk])
    bias_sum = jnp.zeros((1, LANES), f32)
    for chunk in range(chunks):
        gp_ref[chunk * CHUNK : (chunk + 1) * CHUNK, width:] = gb_cols[chunk]
        bias_sum = bias_sum + jnp.sum(gb_cols[chunk], axis=0, keepdims=True)
    small_ref[...] = jnp.zeros(small_ref.shape, f32)
    tap_count = lags + 1
    small_ref[3 * tap_count : 3 * tap_count + 1, 0:LANES] = bias_sum
    du_s[0:SUB, :] = jnp.zeros((SUB, LANES), f32)
    du_s[SUB + rows :, :] = jnp.zeros((SUB, LANES), f32)
    for lag in range(1, lags + 1):
        mask_s[lag - 1, 0:SUB, :] = jnp.zeros((SUB, LANES), f32)
        mask_s[lag - 1, SUB : SUB + rows, :] = masks[lag]
        mask_s[lag - 1, SUB + rows :, :] = jnp.zeros((SUB, LANES), f32)
    for part in range(3):
        for head in range(heads):
            col = part * head_width + head * LANES
            cols = slice(col, col + LANES)
            tap_cols = slice(head * LANES, (head + 1) * LANES)
            total = conv_sum(joined, taps_ref, masks, part, head, head_width, rows)
            sg = sigmoid(total)
            grad = dq_s[:, cols]
            if part < 2:
                z = total * sg
                norm = lax.rsqrt(jnp.sum(z * z, axis=-1, keepdims=True) + 1e-06)
                hat = z * norm
                grad = norm * (grad - hat * jnp.sum(grad * hat, axis=-1, keepdims=True))
                if part == 0:
                    grad = grad * Q_SCALE
            grad = grad * (sg * (1.0 + total * (1.0 - sg)))
            du_s[SUB : SUB + rows, :] = grad
            dp = taps_ref[part, lags : lags + 1, tap_cols] * grad
            halo = jnp.zeros((SUB, LANES), f32)
            row = part * tap_count + lags
            small_ref[row : row + 1, tap_cols] = jnp.sum(
                grad * joined[SUB : SUB + rows, cols], axis=0, keepdims=True
            )
            for lag in range(1, lags + 1):
                tap = taps_ref[part, lags - lag : lags - lag + 1, tap_cols]
                row = part * tap_count + lags - lag
                small_ref[row : row + 1, tap_cols] = jnp.sum(
                    grad * joined[SUB - lag : SUB - lag + rows, cols] * masks[lag],
                    axis=0,
                    keepdims=True,
                )
                moved = du_s[SUB + lag : SUB + lag + rows, :]
                dp = dp + tap * moved * mask_s[lag - 1, SUB + lag : SUB + lag + rows, :]
                halo = halo + tap * du_s[lag : lag + SUB, :] * mask_s[lag - 1, lag : lag + SUB, :]
            gp_ref[:, cols] = dp
            halo_ref[:, cols] = halo


def input_back_kernel(
    place, gp_ref, next_ref, dgr_ref, wq_ref, wk_ref, wv_ref, wg_ref, wb_ref,
    x_ref, sums_ref, keep_ref, send_ref, whole, gpf_ref,
):
    rows, wide = gp_ref.shape
    width = next_ref.shape[1]
    head_width = width // 3
    gpf_ref[...] = gp_ref[...].astype(bf16)
    last = gp_ref[rows - 2 * SUB :, :width]
    gpf_ref[rows - 2 * SUB :, :width] = jnp.concatenate(
        [last[:SUB], last[SUB:] + next_ref[...]], axis=0
    ).astype(bf16)
    total = mm(dgr_ref[...], wg_ref[...], 1, 1) + mm(gpf_ref[:, width : width + SUB], wb_ref[...])
    for part, w_ref in enumerate((wq_ref, wk_ref, wv_ref)):
        total = total + mm(gpf_ref[:, part * head_width : (part + 1) * head_width], w_ref[...], 1, 1)
    whole[...] = total
    split_rows(place, whole, keep_ref, send_ref)
    x = x_ref[...].astype(f32)
    scale = lax.rsqrt(jnp.mean(x * x, axis=-1, keepdims=True) + 1e-06)
    sums = jnp.concatenate(
        [
            jnp.sum(total * (x * scale), axis=0, keepdims=True),
            sums_ref[1:2, :],
            jnp.zeros((2 * SUB - 2, total.shape[1]), f32),
        ],
        axis=0,
    ).astype(bf16)
    keep_ref[rows // 2 :, :] = sums
    send_ref[rows // 2 :, :] = sums


def small_places(model, taps, heads, width):
    sizes = [model, LANES, model, 3 * taps * heads * LANES, heads * model, LANES]
    starts = [0]
    for size in sizes:
        starts.append(starts[-1] + size // LANES)
    across = width // LANES
    rows = -(-starts[-1] // across)
    return starts[:-1], -(-rows // (2 * SUB)) * 2 * SUB


def piece_at(index, width):
    across = width // LANES
    col = index % across * LANES
    return (slice(index // across, index // across + 1), slice(col, col + LANES))


def project_grads_kernel(
    bits, taps, place, a_ref, before_ref, gp_ref, halo_ref, sums_a, gsmall_ref,
    keep_ref, send_ref, whole, small,
):
    a = a_ref[...]
    model = a.shape[1]
    width = whole.shape[1]
    heads = width // (3 * LANES)
    starts, _ = small_places(model, taps, heads, width)
    small[...] = jnp.zeros(small.shape, f32)
    beta_rows = mm(gp_ref[:, width:], a, 0, 0)
    pieces = model // LANES
    for piece in range(pieces):
        cols = slice(piece * LANES, (piece + 1) * LANES)
        small[piece_at(starts[2] + piece, width)] = sums_a[0:1, cols]
        for head in range(heads):
            small[piece_at(starts[4] + head * pieces + piece, width)] = beta_rows[head : head + 1, cols]
    for row in range(3 * taps):
        for head in range(heads):
            small[piece_at(starts[3] + row * heads + head, width)] = gsmall_ref[
                row : row + 1, head * LANES : (head + 1) * LANES
            ]
    small[piece_at(starts[5], width)] = gsmall_ref[3 * taps : 3 * taps + 1, 0:LANES]
    edge = jnp.concatenate([jnp.zeros((SUB, width), f32), halo_ref[...]], axis=0)
    whole[...] = (mm(a, gp_ref[:, :width], 0, 0) + mm(before_ref[...], edge, 0, 0)).astype(bf16)
    emit_shares(place, bits, whole, keep_ref, send_ref)
    keep_ref[model // 2 :, :] = small[...].astype(bf16)
    send_ref[model // 2 :, :] = small[...].astype(bf16)


def head_rows_kernel(place, da_ref, out_ref):
    out_ref[...] = da_ref[da_ref.shape[0] - 2 * SUB :, :].astype(f32)[0:SUB, :]


def share_small_kernel(taps, place, keep_ref, got_ref, *rest):
    keep_out, send_out_ref, small = rest[-3:]
    width = keep_ref.shape[1]
    heads = width // (3 * LANES)
    tail = small.shape[0]
    half = keep_out.shape[0] - tail
    total = keep_ref[2 * half :, :].astype(f32) + got_ref[2 * half :, :].astype(f32)
    small[...] = total
    if len(rest) > 3:
        head_own, head_got = rest[:2]
        joint = head_own[...] + head_got[...]
        model = joint.shape[1]
        starts, _ = small_places(model, taps, heads, width)
        for piece in range(model // LANES):
            small[piece_at(starts[0] + piece, width)] = joint[0:1, piece * LANES : (piece + 1) * LANES]
        small[piece_at(starts[1], width)] = joint[1:2, 0:LANES]
    keep_out[0:half, :] = keep_ref[0:half, :] + got_ref[0:half, :]
    send_out_ref[0:half, :] = keep_ref[half : 2 * half, :] + got_ref[half : 2 * half, :]
    keep_out[half:, :] = small[...].astype(bf16)
    send_out_ref[half:, :] = small[...].astype(bf16)


def project_sum_kernel(
    taps, place, keep_ref, got_ref, q_ref, k_ref, v_ref,
    norm_ref, hgain_ref, fgain_ref, taps_ref, beta_ref, bias_ref, small, rows_s,
):
    share, head_width = q_ref.shape
    width = 3 * head_width
    heads = head_width // LANES
    total = keep_ref[...].astype(f32) + got_ref[...].astype(f32)
    for index, out_ref in enumerate((q_ref, k_ref, v_ref)):
        out_ref[...] = total[:share, index * head_width : (index + 1) * head_width]
    small[...] = total[share:, :]
    model = norm_ref.shape[1]
    starts, _ = small_places(model, taps, heads, width)
    pieces = model // LANES
    for piece in range(pieces):
        cols = slice(piece * LANES, (piece + 1) * LANES)
        norm_ref[0:1, cols] = small[piece_at(starts[0] + piece, width)]
        fgain_ref[0:1, cols] = small[piece_at(starts[2] + piece, width)]
        for head in range(heads):
            row = small[piece_at(starts[4] + head * pieces + piece, width)]
            rows_s[head * pieces + piece : head * pieces + piece + 1, :] = row
    hgain_ref[...] = small[piece_at(starts[1], width)]
    for part in range(3):
        for tap in range(taps):
            for head in range(heads):
                taps_ref[part, tap : tap + 1, head * LANES : (head + 1) * LANES] = small[
                    piece_at(starts[3] + (part * taps + tap) * heads + head, width)
                ]
    bias_ref[...] = small[piece_at(starts[5], width)][:, : bias_ref.shape[1]]
    if share % LANES:
        for head in range(heads):
            for piece in range(pieces):
                at = head * pieces + piece
                beta_ref[head : head + 1, piece * LANES : (piece + 1) * LANES] = rows_s[at : at + 1, :]
    else:
        for head in range(heads):
            for piece in range(share // LANES):
                at = head * pieces + place[0] * (share // LANES) + piece
                beta_ref[head : head + 1, piece * LANES : (piece + 1) * LANES] = rows_s[pl.ds(at, 1), :]


def input_grad_kernel(place, mine, theirs, x_ref, gain_ref, dh_ref, out_ref, whole):
    join_rows(place, mine[...].astype(f32), theirs[...].astype(f32), whole)
    x = x_ref[...].astype(f32)
    scale = lax.rsqrt(jnp.mean(x * x, axis=-1, keepdims=True) + 1e-06)
    hat = x * scale
    grad = whole[...] * gain_ref[...]
    inner = jnp.mean(grad * hat, axis=-1, keepdims=True)
    out_ref[...] = dh_ref[...] + scale * (grad - hat * inner)


def output_kernel(place, mine, theirs, h_ref, out_ref, whole):
    join_rows(place, mine[...].astype(f32), theirs[...].astype(f32), whole)
    out_ref[...] = (h_ref[...] + whole[...]).astype(bf16)


def add_kernel(place, left_ref, right_ref, out_ref):
    out_ref[...] = (left_ref[...].astype(f32) + right_ref[...].astype(f32)).astype(out_ref.dtype)


def added(place, left, right, deps=()):
    shape = left.value.shape if isinstance(left, Free) else left.shape
    (out,) = kernel_call(
        add_kernel, (shaped(shape, right.dtype),), place, left, right, name="added", deps=deps
    )
    return out


def head_sum(place, keep, send, first=(), second=()):
    count = lax.axis_size("head")
    mine = added(place, keep, swap(send, "head", 1), first)
    bit = 2
    while bit < count:
        mine = added(place, mine, swap(mine, "head", bit), second)
        bit *= 2
    return mine, swap(mine, "head", 1)


def gathered(value):
    count = lax.axis_size("head")
    blocks = [value]
    bit = 2
    while bit < count:
        blocks = blocks + [swap(block, "head", bit) for block in blocks]
        bit *= 2
    return blocks + [swap(block, "head", 1) for block in blocks]


def share_rounds(place, keep, send, bits, waits=None):
    arrived = []
    for index, bit in enumerate(bits):
        got = swap(send, "seq", 1 << bit)
        arrived.append(got)
        if index == len(bits) - 1:
            return (keep, got), arrived
        shape = keep.value.shape if isinstance(keep, Free) else keep.shape
        half = (shape[0] // 2,) + shape[1:]
        keep, send = kernel_call(
            share_round_kernel, (shaped(half, bf16), shaped(half, bf16)),
            place, keep, got, name="share_round",
            deps=waits[index] if waits and index < len(waits) else (),
        )


def body(
    block_input, cotangent, segment_ids, norm_gain, w_query, w_key, w_value, w_gate, w_beta,
    beta_bias, conv_weight, head_gain, w_out, ffn_gain, w_ffn_gate, w_ffn_up, w_ffn_down,
):
    rows, model = block_input.shape
    heads = w_beta.shape[1]
    head_width = w_query.shape[1]
    ffn_width = w_ffn_gate.shape[1]
    taps = conv_weight.shape[1]
    seq_count = lax.axis_size("seq")
    rounds = seq_count.bit_length() - 1
    share = model // seq_count
    width = 3 * head_width
    chunks = rows // CHUNK
    y_first = list(range(rounds))

    place = Place()
    bias_in = beta_bias[None] if heads > 1 else jnp.broadcast_to(beta_bias[None], (1, 2))
    gain_row, fgain_row, hgain_row = Free(norm_gain[None]), Free(ffn_gain[None]), Free(head_gain[None])
    taps_in = Free(conv_weight)

    square = (rows, head_width)
    p, beta, seg_cols, tail, a, gate_raw, w_beta8, w_out_copy = kernel_call(
        project_kernel,
        (
            shaped((rows, width), bf16),
            shaped(square, f32),
            shaped((rows, LANES), f32),
            shaped((SUB, width + LANES + model), f32),
            Direct((rows, model), bf16),
            Direct(square, f32),
            Direct((SUB, model), f32),
            Direct(w_out.shape, bf16),
        ),
        place, Far(block_input), Far(w_query), Far(w_key), Far(w_value), Far(w_gate),
        Far(norm_gain[None]), Far(w_beta.T), Far(bias_in),
        Far(segment_ids.reshape(chunks, LANES)), Far(w_out),
        scratch=(
            pltpu.VMEM((rows, model), bf16),
            pltpu.VMEM((4, model, head_width), bf16),
            pltpu.VMEM((1, model), f32),
            pltpu.VMEM((heads, model), bf16),
            pltpu.VMEM(bias_in.shape, f32),
            pltpu.VMEM((chunks, LANES), jnp.int32),
            pltpu.VMEM((rows, model), bf16),
            pltpu.VMEM(square, f32),
            pltpu.VMEM((SUB, model), f32),
            pltpu.VMEM(w_out.shape, bf16),
            pltpu.SemaphoreType.DMA((10,)),
            pltpu.SemaphoreType.DMA((4,)),
        ),
        name="project",
        flops=2 * rows * model * (4 * head_width + LANES),
    )
    halo = shift(tail, "seq", 1)
    joined = pltpu.VMEM((rows + SUB, width), f32)
    joined_ids = pltpu.VMEM((rows + SUB, LANES), f32)
    maps, mix, back, facts, a_before = kernel_call(
        delta_kernel,
        (
            shaped((2 * heads * HEAD_DIM, HEAD_DIM), bf16),
            shaped((rows + 2 * SUB, 4 * head_width), bf16),
            shaped((rows + 2 * SUB, 2 * width + 4 * head_width), bf16),
            shaped((rows + SUB, head_width + LANES), f32),
            shaped((2 * SUB, model), bf16),
        ),
        place, p, halo, Held(conv_weight), seg_cols, beta,
        scratch=(joined, joined_ids),
        name="delta",
        flops=2 * heads * chunks * 128**3 * 30,
    )
    half_maps = heads * HEAD_DIM
    back, facts, steps, a_before = park(
        place, (back, None), (facts, None), (mix, 2 * head_width), (a_before, None), name="park_delta"
    )
    w_out_all = gathered(w_out_copy)
    prefix = pack = maps
    for bit in range(rounds - 1):
        other = swap(maps, "seq", 1 << bit)
        maps, prefix, pack = kernel_call(
            functools.partial(scan_round_kernel, bit),
            (
                shaped((half_maps if bit == rounds - 2 else 2 * half_maps, HEAD_DIM), bf16),
                shaped((2 * half_maps, HEAD_DIM), bf16),
                shaped((2 * half_maps * (bit + 1), HEAD_DIM), bf16),
            ),
            place, maps, other, prefix, pack,
            name="scan_round",
            flops=2 * heads * 128**3 * 5,
            deps=(Held(steps),) if bit == 0 else (),
        )
    other_a = swap(maps, "seq", 1 << (rounds - 1))
    y, mixed, keep_y = kernel_call(
        functools.partial(mixer_kernel, rounds - 1),
        (shaped(square, bf16), shaped(square, f32), shaped((rows, 2 * head_width), bf16)),
        place, prefix, other_a, mix, Free(gate_raw), hgain_row,
        name="mixer",
        flops=2 * heads * chunks * 128**3 * 2,
    )
    mixed, keep_y, pack = park(
        place, (mixed, None), (keep_y, None), (pack, None), name="park_mixer"
    )
    y_all = gathered(y)
    half = (rows // 2, model)
    wide = pltpu.VMEM((rows, model), f32)
    db_send, h, grad_ffn, hidden, db_keep = kernel_call(
        functools.partial(ffn_kernel, share),
        (
            shaped(half, bf16),
            Direct((rows, model), f32),
            Direct((3 * model, ffn_width), bf16),
            Direct((rows, ffn_width), bf16),
            Direct(half, bf16),
        ),
        place, Free(block_input), Free(cotangent), fgain_row,
        Free(w_ffn_gate.T), Free(w_ffn_up.T), Free(w_ffn_down),
        *y_all, Free(w_out_all[0]), *w_out_all[1:],
        scratch=(
            wide,
            pltpu.VMEM((3 * model, ffn_width), bf16),
            pltpu.VMEM((rows, ffn_width), bf16),
            pltpu.VMEM(half, bf16),
            wide,
            pltpu.SemaphoreType.DMA((4,)),
        ),
        deps=(Held(keep_y),),
        name="ffn",
        flops=2 * rows * model * (model + 8 * ffn_width),
    )
    ffn_shares = lax.psum_scatter(grad_ffn, "seq", scatter_dimension=0, tiled=True)
    out_keep, out_send = kernel_call(
        out_part_kernel,
        (shaped(half, bf16), shaped(half, bf16)),
        place, Held(hidden), Held(w_ffn_down),
        scratch=(wide,),
        name="out_part",
        flops=2 * rows * model * ffn_width,
    )
    db_parts = head_sum(place, Held(db_keep), db_send, second=(out_keep,))
    gh, pull, dh, d_out, d_gate_raw, sums_a = kernel_call(
        residual_back_kernel,
        (
            shaped((rows, model), bf16),
            shaped((half_maps, HEAD_DIM), bf16),
            shaped((rows, model), f32),
            shaped(square, bf16),
            shaped(square, bf16),
            shaped((SUB, model), f32),
        ),
        place, *db_parts, Free(h), Free(cotangent), fgain_row, Free(w_out), Free(mixed),
        Free(gate_raw), hgain_row, Free(steps),
        scratch=(wide,),
        name="residual_back",
        flops=2 * rows * model * head_width,
    )
    dh, d_out, d_gate_raw, sums_a = park(
        place, (dh, None), (d_out, None), (d_gate_raw, None), (sums_a, None), name="park_residual"
    )
    other_pulls = [swap(pull, "seq", 1)]
    early_keep, early_send = kernel_call(
        functools.partial(early_grads_kernel, y_first),
        (shaped((model // 2, 2 * head_width), bf16), shaped((model // 2, 2 * head_width), bf16)),
        place, gh, Free(keep_y), Free(a), Free(d_gate_raw),
        scratch=(pltpu.VMEM((model, 2 * head_width), bf16),),
        deps=(other_pulls[0],),
        name="early_grads",
        flops=2 * rows * model * 2 * head_width,
    )
    early_pair, early_got = share_rounds(place, early_keep, early_send, y_first)
    out_parts = head_sum(place, out_keep, out_send, first=(pull,))
    after = pull
    for bit in range(rounds - 1):
        pull, after = kernel_call(
            functools.partial(back_round_kernel, bit),
            (shaped(pull.shape, bf16), shaped(pull.shape, bf16)),
            place, Free(pack), pull, other_pulls[bit], after,
            name="back_round",
            flops=2 * heads * 128**3 * 2,
            deps=((Held(dh),), (early_keep,))[min(bit, 1)],
        )
        other_pulls.append(swap(pull, "seq", 2 << bit))
    gp, gp_halo, grad_small = kernel_call(
        functools.partial(delta_back_kernel, rounds - 1),
        (
            shaped((rows, width + LANES), f32),
            shaped((SUB, width), f32),
            stored((-(-(3 * taps + 1) // SUB) * SUB, head_width), f32),
        ),
        place, taps_in, Free(back), Free(facts), Free(steps), Free(keep_y), Free(d_out),
        Free(pack), after, other_pulls[-1],
        deps=(out_parts[0],),
        scratch=(
            joined,
            joined_ids,
            pltpu.VMEM((rows, width), f32),
            pltpu.VMEM((rows + 2 * SUB, LANES), f32),
            pltpu.VMEM((taps - 1, rows + 2 * SUB, LANES), f32),
        ),
        name="delta_back",
        flops=2 * heads * chunks * 128**3 * 20,
    )
    from_next = shift(gp_halo, "seq", -1)
    _, small_extra = small_places(model, taps, heads, width)
    keep, send = kernel_call(
        functools.partial(project_grads_kernel, y_first, taps),
        (
            shaped((model // 2 + small_extra, width), bf16),
            shaped((model // 2 + small_extra, width), bf16),
        ),
        place, Free(a), Free(a_before), gp, gp_halo, Free(sums_a), Free(grad_small),
        scratch=(pltpu.VMEM((model, width), bf16), pltpu.VMEM((small_extra, width), f32)),
        name="project_grads",
    )
    (block_output,) = kernel_call(
        output_kernel,
        (final((rows, model), bf16),),
        place, *out_parts, Free(h),
        scratch=(wide,),
        name="output",
    )
    da_keep, da_send = kernel_call(
        input_back_kernel,
        (
            shaped((rows // 2 + 2 * SUB, model), bf16),
            shaped((rows // 2 + 2 * SUB, model), bf16),
        ),
        place, gp, from_next, Free(d_gate_raw),
        Free(w_query), Free(w_key), Free(w_value), Free(w_gate), Free(w_beta8), Free(block_input),
        Free(sums_a),
        deps=(early_got[0], keep),
        scratch=(wide, pltpu.VMEM((rows, width + LANES), bf16)),
        name="input_back",
    )
    da_parts = head_sum(place, da_keep, da_send, second=(Held(block_output), early_got[1]))
    (head_small,) = kernel_call(
        head_rows_kernel, (shaped((SUB, model), f32),), place, da_parts[0], name="head_rows"
    )
    head_got = swap(head_small, "seq", 1)
    (input_grad,) = kernel_call(
        input_grad_kernel,
        (final((rows, model), f32),),
        place, *da_parts, Free(block_input), gain_row, Free(dh),
        scratch=(wide,),
        name="input_grad",
    )
    for bit in range(rounds):
        got = swap(send, "seq", 1 << bit)
        if bit < rounds - 1:
            shape = ((keep.shape[0] - small_extra) // 2 + small_extra, width)
            keep, send = kernel_call(
                functools.partial(share_small_kernel, taps),
                (shaped(shape, bf16), shaped(shape, bf16)),
                place, keep, got, *((head_small, head_got) if bit == 0 else ()),
                scratch=(pltpu.VMEM((small_extra, width), f32),),
                name="share_small",
            )
    out_share, w_gate_share = kernel_call(
        early_sum_kernel,
        (final((head_width, share), f32), final((share, head_width), f32)),
        place, *early_pair, name="early_sum",
    )
    beta_shape = (heads, model if share % LANES else share)
    (
        q_share, k_share, v_share, norm_total, head_gain_total, ffn_gain_total, conv_total, beta_rows,
        bias_total,
    ) = kernel_call(
        functools.partial(project_sum_kernel, taps),
        tuple(final((share, head_width), f32) for _ in range(3))
        + (
            final((1, model), f32),
            final((1, LANES), f32),
            final((1, model), f32),
            final(conv_weight.shape, f32),
            final(beta_shape, f32),
            final((1, heads), f32),
        ),
        place, keep, got,
        deps=(Held(input_grad), Held(out_share)),
        scratch=(
            pltpu.VMEM((small_extra, width), f32),
            pltpu.VMEM((-(-heads * model // LANES // SUB) * SUB, LANES), f32),
        ),
        name="project_sum",
    )
    if share % LANES:
        beta_rows = lax.dynamic_slice(beta_rows, (0, lax.axis_index("seq") * share), (heads, share))
    beta_share = beta_rows.T
    down_share, ffn_gate_share, ffn_up_share = kernel_call(
        ffn_shares_kernel,
        tuple(final((ffn_width, share), f32) for _ in range(3)),
        place, Free(ffn_shares), name="ffn_shares",
    )
    return (
        block_output,
        input_grad,
        norm_total[0],
        q_share,
        k_share,
        v_share,
        w_gate_share,
        beta_share,
        bias_total[0],
        conv_total,
        head_gain_total[0],
        out_share,
        ffn_gain_total[0],
        ffn_gate_share.T,
        ffn_up_share.T,
        down_share,
    )


def solution(mesh):
    return jax.shard_map(
        body,
        mesh=mesh,
        in_specs=(
            P("seq", None), P("seq", None), P("seq"), P(),
            P(None, "head"), P(None, "head"), P(None, "head"), P(None, "head"), P(None, "head"),
            P("head"), P(None, None, "head"), P(), P("head", None), P(),
            P(None, "head"), P(None, "head"), P("head", None),
        ),
        out_specs=(
            P("seq", None), P("seq", None), P(),
            P("seq", "head"), P("seq", "head"), P("seq", "head"), P("seq", "head"), P("seq", "head"),
            P("head"), P(None, None, "head"), P(), P("head", "seq"), P(),
            P("seq", "head"), P("seq", "head"), P("head", "seq"),
        ),
        check_vma=False,
    )
```

time: 286 us -> 204 us (0.71)
  local copies, waits for them, and re-layouts: 31.9 us -> 4.56 us
  Pallas kernels: 68.7 us -> 47.5 us
  waiting for transfers between devices: 119 us -> 103 us
  other arithmetic: 15.6 us -> 0 us
    pallas_call x15 -> x33, Pallas kernels: 68.7 us -> 47.5 us  [kernel_call(): pl.pallas_call(run, out_shape=tuple(results), in_specs=specs, out_specs=t...]
    reduce_scatter x2 -> x1, waiting for transfers between devices: 19 us -> 0.01 us  [body(): lax.psum_scatter(grad_ffn, 'seq', scatter_dimension=0, tiled=True)]
    unnamed x95 -> x70, local copies, waits for them, and re-layouts: 21.1 us -> 4.56 us
    concatenate x6 -> x0, other arithmetic: 11.1 us -> none  [the longest x4 6.72 us: gathered(): blocks = jnp.concatenate([blocks, swap(blocks, 'head', bit)], axis=0)]
    slice x15 -> x0, local copies, waits for them, and re-layouts: 7.55 us -> none  [the longest x2 1.27 us: body(): other_maps[:half_maps]]
    ppermute x30 -> x28, waiting for transfers between devices: 94.7 us -> 99 us  [swap(): return lax.ppermute(value, axis, [(s, s ^ bit) for s in range(count)])]
    ppermute x30 -> x28, starting transfers between devices: 28.3 us -> 29.4 us  [swap(): return lax.ppermute(value, axis, [(s, s ^ bit) for s in range(count)])]
  transfers between devices with their start and end apart: 34 -> 31, of which waited for: 18 -> 20; matrix products, arithmetic and copies ran while one was open for 10% -> 0% of each run, Pallas kernels for 19% -> 16%
where the time goes in v2:
time: 204 us
  waiting for transfers between devices  103 us (50%)
  Pallas kernels  47.5 us (23%)
  starting transfers between devices  34.5 us (17%)
  between operations  14.6 us (7%)
  local copies, waits for them, and re-layouts  4.56 us (2%)
    ppermute x28, waiting for transfers between devices, swap(): return lax.ppermute(value, axis, [(s, s ^ bit) for s in range(count)])  99 us
    pallas_call x33, Pallas kernels, kernel_call(): pl.pallas_call(run, out_shape=tuple(results), in_specs=specs, out_specs=t...  47.5 us
    ppermute x28, starting transfers between devices, swap(): return lax.ppermute(value, axis, [(s, s ^ bit) for s in range(count)])  29.4 us
    ppermute x2, starting transfers between devices, shift(): lax.ppermute(value, axis, [(s, s + step) for s in range(count) if 0 <= s...  5.06 us
    unnamed x70, local copies, waits for them, and re-layouts  4.56 us
  transfers between devices with their start and end apart: 31, of which 20 were waited for; matrix products, arithmetic and copies ran while one was open for 0% of the time, Pallas kernels for 16%

profile of v2, /device:TPU:0, one launch (start us, length us, event | category | flops | bytes accessed | tf_op | source)
XLA Modules:
  0.0 203.8 jit_solution(9735668115406673315)
XLA Ops:
  7.2 4.2 %project.1 = (bf16[384,768]{1,0:T(8,128)(2,1)S(1)}, f32[384,256]{1,0:T(8,128)S(1)}, f32[384,128]{1,0:T(8,128)S(1)}, f32[8,1920]{1,0:T(8,128)S(1)}, bf16[384,1024...) custom-call(bf16[384,1024]{1,0:T(8,128)(2,1)} %refs_2_.5, ...), custom_call_target="tpu_custom_call" | custom-call | tf_op jit(solution)/shard_map/project/pallas_call | solution.py:102
  11.4 3.0 %collective-permute-start.7 = (bf16[256,1024]{1,0:T(8,128)(2,1)}, bf16[256,1024]{1,0:T(8,128)(2,1)S(1)}, u32[]{:S(2)}, u32[]{:S(2)}) collective-permute-start(bf16[256,1024]{1,0:T(8,128)(2,1)} %get-tuple-element.114.refs_10_), channel_id=1, source_target_pairs={{0,2},{1,3},{2,0},{3,1},{4,6},{5,7},{6,4},{7,5},{8,10},{9,11},{10,... | collective-permute-start | bytes 1572872 | tf_op jit(solution)/shard_map/ppermute | solution.py:140
  14.4 3.4 %collective-permute-start = (f32[8,1920]{1,0:T(8,128)S(1)}, f32[8,1920]{1,0:T(8,128)S(1)}, u32[]{:S(2)}, u32[]{:S(2)}) collective-permute-start(f32[8,1920]{1,0:T(8,128)S(1)} %get-tuple-element.98), channel_id=1, source_target_pairs={{0,4},{4,8},{8,12},{12,16},{16,20},{20,24},{24,28},{1,5},{5,9},{9,... | collective-permute-start | bytes 184328 | tf_op jit(solution)/shard_map/ppermute | solution.py:145
  19.7 4.6 %delta.1 = (bf16[512,128]{1,0:T(8,128)(2,1)S(1)}, bf16[400,1024]{1,0:T(8,128)(2,1)S(1)}, bf16[400,2560]{1,0:T(8,128)(2,1)S(1)}, f32[392,384]{1,0:T(8,128)S(1)}, bf16[16,1024]{1,0:T(8,128)(2,1)S(1)}) custom-call(bf16[384,768]{1,0:T(8,128)(2,1)S(1)} %get-tuple-element.97.refs_0_, f32[8,1920]{1,0:T(8,128)S(1)} %collective-permute-done.refs_1_, ...), custom_call_target="tpu_custom_call" | custom-call | tf_op jit(solution)/shard_map/delta/pallas_call | solution.py:102
  24.3 2.4 %collective-permute-start.1 = (bf16[512,128]{1,0:T(8,128)(2,1)S(1)}, bf16[512,128]{1,0:T(8,128)(2,1)S(1)}, u32[]{:S(2)}, u32[]{:S(2)}) collective-permute-start(bf16[512,128]{1,0:T(8,128)(2,1)S(1)} %get-tuple-element.101.refs_0_.refs_2_.refs_3_), channel_id=1, source_target_pairs={{0,4},{4,0},{8,12},{12,8},{16,20},{20,16},{24,28},{28,24},{1,5},{5... | collective-permute-start | bytes 393224 | tf_op jit(solution)/shard_map/ppermute | solution.py:140
  29.9 3.0 %collective-permute-start.2 = (bf16[512,128]{1,0:T(8,128)(2,1)S(1)}, bf16[512,128]{1,0:T(8,128)(2,1)S(1)}, u32[]{:S(2)}, u32[]{:S(2)}) collective-permute-start(bf16[512,128]{1,0:T(8,128)(2,1)S(1)} %get-tuple-element.107.refs_0_), channel_id=1, source_target_pairs={{0,8},{4,12},{8,0},{12,4},{16,24},{20,28},{24,16},{28,20},{1,9},{5... | collective-permute-start | bytes 393224 | tf_op jit(solution)/shard_map/ppermute | solution.py:140
  33.4 2.4 %collective-permute-done.2.refs_1_ = bf16[512,128]{1,0:T(8,128)(2,1)S(1)} collective-permute-done((bf16[512,128]{1,0:T(8,128)(2,1)S(1)}, bf16[512,128]{1,0:T(8,128)(2,1)S(1)}, u32[]{:S(2)}, u32[]{:S(2)}) %collective-permute-start.2) | collective-permute-done | bytes 131104 | tf_op jit(solution)/shard_map/ppermute | solution.py:140
  36.1 3.8 %collective-permute-start.3 = (bf16[256,128]{1,0:T(8,128)(2,1)S(1)}, bf16[256,128]{1,0:T(8,128)(2,1)S(1)}, u32[]{:S(2)}, u32[]{:S(2)}) collective-permute-start(bf16[256,128]{1,0:T(8,128)(2,1)S(1)} %get-tuple-element.111), channel_id=1, source_target_pairs={{0,16},{4,20},{8,24},{12,28},{16,0},{20,4},{24,8},{28,12},{1,17},{... | collective-permute-start | bytes 196616 | tf_op jit(solution)/shard_map/ppermute | solution.py:140
  39.9 2.3 %collective-permute-done.3.refs_1_ = bf16[256,128]{1,0:T(8,128)(2,1)S(1)} collective-permute-done((bf16[256,128]{1,0:T(8,128)(2,1)S(1)}, bf16[256,128]{1,0:T(8,128)(2,1)S(1)}, u32[]{:S(2)}, u32[]{:S(2)}) %collective-permute-start.3) | collective-permute-done | bytes 65568 | tf_op jit(solution)/shard_map/ppermute | solution.py:140
  43.8 5.1 %collective-permute-done.4.refs_7_ = bf16[384,256]{1,0:T(8,128)(2,1)S(1)} collective-permute-done((bf16[384,256]{1,0:T(8,128)(2,1)S(1)}, bf16[384,256]{1,0:T(8,128)(2,1)S(1)}, u32[]{:S(2)}, u32[]{:S(2)}) %collective-permute-start.4) | collective-permute-done | bytes 196640 | tf_op jit(solution)/shard_map/ppermute | solution.py:140
  50.4 9.9 %ffn.1 = (bf16[192,1024]{1,0:T(8,128)(2,1)S(1)}, f32[384,1024]{1,0:T(8,128)}, bf16[3072,704]{1,0:T(8,128)(2,1)}, bf16[384,704]{1,0:T(8,128)(2,1)}, bf16[192,1024]{1,0:T(8,128)(2,1)}) custom-call(bf16[384,1024]{1,0:T(8,128)(2,1)S(1)} %copy-done, bf16[384,1024]{1,0:T(8,128)(2,1)S(1)} %copy-done.7, f32[1,1024]{1,0:T(1,128)S(1)} %bitcast.17, ...), custom_call_target="tpu_custom_call" | custom-call | tf_op jit(solution)/shard_map/ffn/pallas_call | solution.py:102
  65.5 2.8 %out_part.1 = (bf16[192,1024]{1,0:T(8,128)(2,1)S(1)}, bf16[192,1024]{1,0:T(8,128)(2,1)S(1)}) custom-call(bf16[384,704]{1,0:T(8,128)(2,1)} %get-tuple-element.119.refs_0_, bf16[704,1024]{1,0:T(8,128)(2,1)} %refs_1_.5), custom_call_target="tpu_custom_call" | custom-call | tf_op jit(solution)/shard_map/out_part/pallas_call | solution.py:102
  68.3 7.8 %collective-permute-done.12.refs_1_ = bf16[192,1024]{1,0:T(8,128)(2,1)S(1)} collective-permute-done((bf16[192,1024]{1,0:T(8,128)(2,1)S(1)}, bf16[192,1024]{1,0:T(8,128)(2,1)S(1)}, u32[]{:S(2)}, u32[]{:S(2)}) %collective-permute-start.12) | collective-permute-done | bytes 393248 | tf_op jit(solution)/shard_map/ppermute | solution.py:140
  82.0 2.3 %collective-permute-done.16.refs_2_.refs_4_ = bf16[256,128]{1,0:T(8,128)(2,1)S(1)} collective-permute-done((bf16[256,128]{1,0:T(8,128)(2,1)S(1)}, bf16[256,128]{1,0:T(8,128)(2,1)S(1)}, u32[]{:S(2)}, u32[]{:S(2)}) %collective-permute-start.16) | collective-permute-done | bytes 65568 | tf_op jit(solution)/shard_map/ppermute | solution.py:140
  89.0 7.5 %collective-permute-done.17.refs_2_ = bf16[256,128]{1,0:T(8,128)(2,1)S(1)} collective-permute-done((bf16[256,128]{1,0:T(8,128)(2,1)S(1)}, bf16[256,128]{1,0:T(8,128)(2,1)S(1)}, u32[]{:S(2)}, u32[]{:S(2)}) %collective-permute-start.17) | collective-permute-done | bytes 65568 | tf_op jit(solution)/shard_map/ppermute | solution.py:140
  98.2 9.1 %collective-permute-done.18.refs_8_ = bf16[256,128]{1,0:T(8,128)(2,1)S(1)} collective-permute-done((bf16[256,128]{1,0:T(8,128)(2,1)S(1)}, bf16[256,128]{1,0:T(8,128)(2,1)S(1)}, u32[]{:S(2)}, u32[]{:S(2)}) %collective-permute-start.18) | collective-permute-done | bytes 65568 | tf_op jit(solution)/shard_map/ppermute | solution.py:140
  107.3 6.6 %delta_back.1 = (f32[384,896]{1,0:T(8,128)S(1)}, f32[8,768]{1,0:T(8,128)S(1)}, f32[16,256]{1,0:T(8,128)}) custom-call(f32[3,4,256]{2,1,0:T(4,128)S(1)} %copy-done.26, bf16[400,2560]{1,0:T(8,128)(2,1)S(1)} %copy-done.14, f32[392,384]{1,0:T(8,128)S(1)} %copy-done.20, bf16[400,512]{1,0:T(8,128)(2,1)S(1)} %copy-done.4, bf16[384,512]{1,0:T(8,128)(2,1)S(1)} %copy-done.5, ...), custom_call_target="tpu_custom_call" | custom-call | tf_op jit(solution)/shard_map/delta_back/pallas_call | solution.py:102
  121.3 2.7 %collective-permute-start.25 = (bf16[528,768]{1,0:T(8,128)(2,1)S(1)}, bf16[528,768]{1,0:T(8,128)(2,1)S(1)}, u32[]{:S(2)}, u32[]{:S(2)}) collective-permute-start(bf16[528,768]{1,0:T(8,128)(2,1)S(1)} %get-tuple-element.155), channel_id=1, source_target_pairs={{0,4},{4,0},{8,12},{12,8},{16,20},{20,16},{24,28},{28,24},{1,5},{5... | collective-permute-start | bytes 2433032 | tf_op jit(solution)/shard_map/ppermute | solution.py:140
  128.2 6.0 %collective-permute-done.23.refs_3_.refs_1_ = bf16[256,512]{1,0:T(8,128)(2,1)S(1)} collective-permute-done((bf16[256,512]{1,0:T(8,128)(2,1)S(1)}, bf16[256,512]{1,0:T(8,128)(2,1)S(1)}, u32[]{:S(2)}, u32[]{:S(2)}) %collective-permute-start.23) | collective-permute-done | bytes 262176 | tf_op jit(solution)/shard_map/ppermute | solution.py:140
  137.9 9.2 %collective-permute-done.25.refs_1_ = bf16[528,768]{1,0:T(8,128)(2,1)S(1)} collective-permute-done((bf16[528,768]{1,0:T(8,128)(2,1)S(1)}, bf16[528,768]{1,0:T(8,128)(2,1)S(1)}, u32[]{:S(2)}, u32[]{:S(2)}) %collective-permute-start.25) | collective-permute-done | bytes 811040 | tf_op jit(solution)/shard_map/ppermute | solution.py:140
  148.6 24.1 %collective-permute-done.27.refs_1_ = bf16[272,768]{1,0:T(8,128)(2,1)S(1)} collective-permute-done((bf16[272,768]{1,0:T(8,128)(2,1)S(1)}, bf16[272,768]{1,0:T(8,128)(2,1)S(1)}, u32[]{:S(2)}, u32[]{:S(2)}) %collective-permute-start.27) | collective-permute-done | bytes 417824 | tf_op jit(solution)/shard_map/ppermute | solution.py:140
  173.2 2.5 %collective-permute-start.29 = (bf16[128,512]{1,0:T(8,128)(2,1)S(1)}, bf16[128,512]{1,0:T(8,128)(2,1)S(1)}, u32[]{:S(2)}, u32[]{:S(2)}) collective-permute-start(bf16[128,512]{1,0:T(8,128)(2,1)S(1)} %get-tuple-element.162), channel_id=1, source_target_pairs={{0,16},{4,20},{8,24},{12,28},{16,0},{20,4},{24,8},{28,12},{1,17},{... | collective-permute-start | bytes 393224 | tf_op jit(solution)/shard_map/ppermute | solution.py:140
  175.8 15.4 %collective-permute-done.29.refs_1_ = bf16[128,512]{1,0:T(8,128)(2,1)S(1)} collective-permute-done((bf16[128,512]{1,0:T(8,128)(2,1)S(1)}, bf16[128,512]{1,0:T(8,128)(2,1)S(1)}, u32[]{:S(2)}, u32[]{:S(2)}) %collective-permute-start.29) | collective-permute-done | bytes 131104 | tf_op jit(solution)/shard_map/ppermute | solution.py:140
  191.9 2.1 %input_grad.1.refs_2_ = f32[384,1024]{1,0:T(8,128)} custom-call(bf16[208,1024]{1,0:T(8,128)(2,1)S(1)} %added.11.refs_0_, bf16[208,1024]{1,0:T(8,128)(2,1)S(1)} %collective-permute-done.24.refs_1_, bf16[384,1024]{1,0:T(8,128)(2,1)S(1)} %copy-done, f32[1,1024]{1,0:T(1,128)S(1)} %bitcast.20, f32[384,1024]{1,0:T(8,128)S(1)} %copy-done.2), custom_call_target="tpu_custom_call" | custom-call | tf_op jit(solution)/shard_map/input_grad/pallas_call | solution.py:102
  (142 shorter events, 47.2 us)
Async XLA Ops:
  7.2 187.6 %reduce-scatter.2.cloned.1.call-start = ((), (), s32[]{:S(2)}) async-start(), calls=%async_computation.1 | async-start | bytes 5308416 | tf_op jit(solution)/shard_map/reduce_scatter | solution.py:1128
  11.4 21.5 %collective-permute-start.7 = (bf16[256,1024]{1,0:T(8,128)(2,1)}, bf16[256,1024]{1,0:T(8,128)(2,1)S(1)}, u32[]{:S(2)}, u32[]{:S(2)}) collective-permute-start(bf16[256,1024]{1,0:T(8,128)(2,1)} %get-tuple-element.114.refs_10_), channel_id=1, source_target_pairs={{0,2},{1,3},{2,0},{3,1},{4,6},{5,7},{6,4},{7,5},{8,10},{9,11},{10,... | collective-permute-start | bytes 1572872 | tf_op jit(solution)/shard_map/ppermute | solution.py:140
  24.3 5.4 %collective-permute-start.1 = (bf16[512,128]{1,0:T(8,128)(2,1)S(1)}, bf16[512,128]{1,0:T(8,128)(2,1)S(1)}, u32[]{:S(2)}, u32[]{:S(2)}) collective-permute-start(bf16[512,128]{1,0:T(8,128)(2,1)S(1)} %get-tuple-element.101.refs_0_.refs_2_.refs_3_), channel_id=1, source_target_pairs={{0,4},{4,0},{8,12},{12,8},{16,20},{20,16},{24,28},{28,24},{1,5},{5... | collective-permute-start | bytes 393224 | tf_op jit(solution)/shard_map/ppermute | solution.py:140
  29.9 6.0 %collective-permute-start.2 = (bf16[512,128]{1,0:T(8,128)(2,1)S(1)}, bf16[512,128]{1,0:T(8,128)(2,1)S(1)}, u32[]{:S(2)}, u32[]{:S(2)}) collective-permute-start(bf16[512,128]{1,0:T(8,128)(2,1)S(1)} %get-tuple-element.107.refs_0_), channel_id=1, source_target_pairs={{0,8},{4,12},{8,0},{12,4},{16,24},{20,28},{24,16},{28,20},{1,9},{5... | collective-permute-start | bytes 393224 | tf_op jit(solution)/shard_map/ppermute | solution.py:140
  32.9 17.0 %collective-permute-start.8 = (bf16[256,1024]{1,0:T(8,128)(2,1)S(1)}, bf16[256,1024]{1,0:T(8,128)(2,1)S(1)}, u32[]{:S(2)}, u32[]{:S(2)}) collective-permute-start(bf16[256,1024]{1,0:T(8,128)(2,1)S(1)} %copy-done.22), channel_id=1, source_target_pairs={{0,1},{1,0},{2,3},{3,2},{4,5},{5,4},{6,7},{7,6},{8,9},{9,8},{10,11... | collective-permute-start | bytes 1572872 | tf_op jit(solution)/shard_map/ppermute | solution.py:140
  32.9 17.4 %collective-permute-start.9 = (bf16[256,1024]{1,0:T(8,128)(2,1)S(1)}, bf16[256,1024]{1,0:T(8,128)(2,1)S(1)}, u32[]{:S(2)}, u32[]{:S(2)}) collective-permute-start(bf16[256,1024]{1,0:T(8,128)(2,1)S(1)} %collective-permute-done.7.refs_11_), channel_id=1, source_target_pairs={{0,1},{1,0},{2,3},{3,2},{4,5},{5,4},{6,7},{7,6},{8,9},{9,8},{10,11... | collective-permute-start | bytes 1572872 | tf_op jit(solution)/shard_map/ppermute | solution.py:140
  36.1 6.1 %collective-permute-start.3 = (bf16[256,128]{1,0:T(8,128)(2,1)S(1)}, bf16[256,128]{1,0:T(8,128)(2,1)S(1)}, u32[]{:S(2)}, u32[]{:S(2)}) collective-permute-start(bf16[256,128]{1,0:T(8,128)(2,1)S(1)} %get-tuple-element.111), channel_id=1, source_target_pairs={{0,16},{4,20},{8,24},{12,28},{16,0},{20,4},{24,8},{28,12},{1,17},{... | collective-permute-start | bytes 196616 | tf_op jit(solution)/shard_map/ppermute | solution.py:140
  43.2 5.7 %collective-permute-start.4 = (bf16[384,256]{1,0:T(8,128)(2,1)S(1)}, bf16[384,256]{1,0:T(8,128)(2,1)S(1)}, u32[]{:S(2)}, u32[]{:S(2)}) collective-permute-start(bf16[384,256]{1,0:T(8,128)(2,1)S(1)} %get-tuple-element.113.refs_6_), channel_id=1, source_target_pairs={{0,2},{1,3},{2,0},{3,1},{4,6},{5,7},{6,4},{7,5},{8,10},{9,11},{10,... | collective-permute-start | bytes 589832 | tf_op jit(solution)/shard_map/ppermute | solution.py:140
  43.8 6.1 %collective-permute-start.5 = (bf16[384,256]{1,0:T(8,128)(2,1)S(1)}, bf16[384,256]{1,0:T(8,128)(2,1)S(1)}, u32[]{:S(2)}, u32[]{:S(2)}) collective-permute-start(bf16[384,256]{1,0:T(8,128)(2,1)S(1)} %get-tuple-element.113.refs_6_), channel_id=1, source_target_pairs={{0,1},{1,0},{2,3},{3,2},{4,5},{5,4},{6,7},{7,6},{8,9},{9,8},{10,11... | collective-permute-start | bytes 589832 | tf_op jit(solution)/shard_map/ppermute | solution.py:140
  64.8 11.2 %collective-permute-start.12 = (bf16[192,1024]{1,0:T(8,128)(2,1)S(1)}, bf16[192,1024]{1,0:T(8,128)(2,1)S(1)}, u32[]{:S(2)}, u32[]{:S(2)}) collective-permute-start(bf16[192,1024]{1,0:T(8,128)(2,1)S(1)} %added.6.refs_0_), channel_id=1, source_target_pairs={{0,2},{1,3},{2,0},{3,1},{4,6},{5,7},{6,4},{7,5},{8,10},{9,11},{10,... | collective-permute-start | bytes 1179656 | tf_op jit(solution)/shard_map/ppermute | solution.py:140
  76.2 10.6 %collective-permute-start.10 = (bf16[192,1024]{1,0:T(8,128)(2,1)S(1)}, bf16[192,1024]{1,0:T(8,128)(2,1)S(1)}, u32[]{:S(2)}, u32[]{:S(2)}) collective-permute-start(bf16[192,1024]{1,0:T(8,128)(2,1)S(1)} %get-tuple-element.121), channel_id=1, source_target_pairs={{0,1},{1,0},{2,3},{3,2},{4,5},{5,4},{6,7},{7,6},{8,9},{9,8},{10,11... | collective-permute-start | bytes 1179656 | tf_op jit(solution)/shard_map/ppermute | solution.py:140
  86.1 33.7 %collective-permute-start.20 = (bf16[512,512]{1,0:T(8,128)(2,1)S(1)}, bf16[512,512]{1,0:T(8,128)(2,1)S(1)}, u32[]{:S(2)}, u32[]{:S(2)}) collective-permute-start(bf16[512,512]{1,0:T(8,128)(2,1)S(1)} %get-tuple-element.148), channel_id=1, source_target_pairs={{0,4},{4,0},{8,12},{12,8},{16,20},{20,16},{24,28},{28,24},{1,5},{5... | collective-permute-start | bytes 1572872 | tf_op jit(solution)/shard_map/ppermute | solution.py:140
  86.9 11.2 %collective-permute-start.14 = (bf16[192,1024]{1,0:T(8,128)(2,1)S(1)}, bf16[192,1024]{1,0:T(8,128)(2,1)S(1)}, u32[]{:S(2)}, u32[]{:S(2)}) collective-permute-start(bf16[192,1024]{1,0:T(8,128)(2,1)S(1)} %added.8.refs_0_), channel_id=1, source_target_pairs={{0,2},{1,3},{2,0},{3,1},{4,6},{5,7},{6,4},{7,5},{8,10},{9,11},{10,... | collective-permute-start | bytes 1179656 | tf_op jit(solution)/shard_map/ppermute | solution.py:140
  87.6 8.9 %collective-permute-start.17 = (bf16[256,128]{1,0:T(8,128)(2,1)S(1)}, bf16[256,128]{1,0:T(8,128)(2,1)S(1)}, u32[]{:S(2)}, u32[]{:S(2)}) collective-permute-start(bf16[256,128]{1,0:T(8,128)(2,1)S(1)} %get-tuple-element.136.refs_1_), channel_id=1, source_target_pairs={{0,8},{4,12},{8,0},{12,4},{16,24},{20,28},{24,16},{28,20},{1,9},{5... | collective-permute-start | bytes 196616 | tf_op jit(solution)/shard_map/ppermute | solution.py:140
  96.7 10.5 %collective-permute-start.18 = (bf16[256,128]{1,0:T(8,128)(2,1)S(1)}, bf16[256,128]{1,0:T(8,128)(2,1)S(1)}, u32[]{:S(2)}, u32[]{:S(2)}) collective-permute-start(bf16[256,128]{1,0:T(8,128)(2,1)S(1)} %get-tuple-element.143), channel_id=1, source_target_pairs={{0,16},{4,20},{8,24},{12,28},{16,0},{20,4},{24,8},{28,12},{1,17},{... | collective-permute-start | bytes 196616 | tf_op jit(solution)/shard_map/ppermute | solution.py:140
  113.9 5.9 %collective-permute-start.19 = (f32[8,768]{1,0:T(8,128)S(1)}, f32[8,768]{1,0:T(8,128)S(1)}, u32[]{:S(2)}, u32[]{:S(2)}) collective-permute-start(f32[8,768]{1,0:T(8,128)S(1)} %get-tuple-element.145.refs_3_), channel_id=1, source_target_pairs={{4,0},{8,4},{12,8},{16,12},{20,16},{24,20},{28,24},{5,1},{9,5},{13... | collective-permute-start | bytes 73736 | tf_op jit(solution)/shard_map/ppermute | solution.py:145
  121.3 25.8 %collective-permute-start.25 = (bf16[528,768]{1,0:T(8,128)(2,1)S(1)}, bf16[528,768]{1,0:T(8,128)(2,1)S(1)}, u32[]{:S(2)}, u32[]{:S(2)}) collective-permute-start(bf16[528,768]{1,0:T(8,128)(2,1)S(1)} %get-tuple-element.155), channel_id=1, source_target_pairs={{0,4},{4,0},{8,12},{12,8},{16,20},{20,16},{24,28},{28,24},{1,5},{5... | collective-permute-start | bytes 2433032 | tf_op jit(solution)/shard_map/ppermute | solution.py:140
  124.1 12.0 %collective-permute-start.22 = (bf16[208,1024]{1,0:T(8,128)(2,1)S(1)}, bf16[208,1024]{1,0:T(8,128)(2,1)S(1)}, u32[]{:S(2)}, u32[]{:S(2)}) collective-permute-start(bf16[208,1024]{1,0:T(8,128)(2,1)S(1)} %added.10.refs_0_), channel_id=1, source_target_pairs={{0,2},{1,3},{2,0},{3,1},{4,6},{5,7},{6,4},{7,5},{8,10},{9,11},{10,... | collective-permute-start | bytes 1277960 | tf_op jit(solution)/shard_map/ppermute | solution.py:140
  125.4 8.8 %collective-permute-start.23 = (bf16[256,512]{1,0:T(8,128)(2,1)S(1)}, bf16[256,512]{1,0:T(8,128)(2,1)S(1)}, u32[]{:S(2)}, u32[]{:S(2)}) collective-permute-start(bf16[256,512]{1,0:T(8,128)(2,1)S(1)} %get-tuple-element.154), channel_id=1, source_target_pairs={{0,8},{4,12},{8,0},{12,4},{16,24},{20,28},{24,16},{28,20},{1,9},{5... | collective-permute-start | bytes 786440 | tf_op jit(solution)/shard_map/ppermute | solution.py:140
  136.2 12.1 %collective-permute-start.26 = (f32[8,1024]{1,0:T(8,128)S(1)}, f32[8,1024]{1,0:T(8,128)S(1)}, u32[]{:S(2)}, u32[]{:S(2)}) collective-permute-start(f32[8,1024]{1,0:T(8,128)S(1)} %head_rows.1.refs_2_), channel_id=1, source_target_pairs={{0,4},{4,0},{8,12},{12,8},{16,20},{20,16},{24,28},{28,24},{1,5},{5... | collective-permute-start | bytes 98312 | tf_op jit(solution)/shard_map/ppermute | solution.py:140
  148.4 24.2 %collective-permute-start.27 = (bf16[272,768]{1,0:T(8,128)(2,1)S(1)}, bf16[272,768]{1,0:T(8,128)(2,1)S(1)}, u32[]{:S(2)}, u32[]{:S(2)}) collective-permute-start(bf16[272,768]{1,0:T(8,128)(2,1)S(1)} %get-tuple-element.157), channel_id=1, source_target_pairs={{0,8},{4,12},{8,0},{12,4},{16,24},{20,28},{24,16},{28,20},{1,9},{5... | collective-permute-start | bytes 1253384 | tf_op jit(solution)/shard_map/ppermute | solution.py:140
  148.5 43.4 %collective-permute-start.24 = (bf16[208,1024]{1,0:T(8,128)(2,1)S(1)}, bf16[208,1024]{1,0:T(8,128)(2,1)S(1)}, u32[]{:S(2)}, u32[]{:S(2)}) collective-permute-start(bf16[208,1024]{1,0:T(8,128)(2,1)S(1)} %added.11.refs_0_), channel_id=1, source_target_pairs={{0,1},{1,0},{2,3},{3,2},{4,5},{5,4},{6,7},{7,6},{8,9},{9,8},{10,11... | collective-permute-start | bytes 1277960 | tf_op jit(solution)/shard_map/ppermute | solution.py:140
  172.7 21.3 %collective-permute-start.28 = (bf16[144,768]{1,0:T(8,128)(2,1)S(1)}, bf16[144,768]{1,0:T(8,128)(2,1)S(1)}, u32[]{:S(2)}, u32[]{:S(2)}) collective-permute-start(bf16[144,768]{1,0:T(8,128)(2,1)S(1)} %get-tuple-element.159), channel_id=1, source_target_pairs={{0,16},{4,20},{8,24},{12,28},{16,0},{20,4},{24,8},{28,12},{1,17},{... | collective-permute-start | bytes 663560 | tf_op jit(solution)/shard_map/ppermute | solution.py:140
  173.2 17.9 %collective-permute-start.29 = (bf16[128,512]{1,0:T(8,128)(2,1)S(1)}, bf16[128,512]{1,0:T(8,128)(2,1)S(1)}, u32[]{:S(2)}, u32[]{:S(2)}) collective-permute-start(bf16[128,512]{1,0:T(8,128)(2,1)S(1)} %get-tuple-element.162), channel_id=1, source_target_pairs={{0,16},{4,20},{8,24},{12,28},{16,0},{20,4},{24,8},{28,12},{1,17},{... | collective-permute-start | bytes 393224 | tf_op jit(solution)/shard_map/ppermute | solution.py:140
  (42 other events, 498.6 us)
Sparse Core Ops, SparseCore 0:
  61.2 111.8 reduce-scatter.1

commit v3 on v2

--- a/solution.py
+++ b/solution.py
@@ -15,6 +15,46 @@
 Q_SCALE = HEAD_DIM ** (-0.5)
 VMEM_SLACK = 14 * 1024 * 1024
 
+ORDER = (
+    "db_core",
+    "out_part",
+    "db_far",
+    "residual_back",
+    "park_back",
+    "down_one",
+    "gate_one",
+    "scan_back",
+    "up_blocks",
+    "out_core",
+    "scan_rest",
+    "delta_query",
+    "early_grads",
+    "down_two",
+    "gate_two",
+    "out_far",
+    "delta_back",
+    "input_back",
+    "up_one",
+    "rows_core",
+    "input_split",
+    "rows_far",
+    "project_grads",
+    "up_two",
+    "early_one",
+    "da_core",
+    "output",
+    "down_out",
+    "share_one",
+    "early_two",
+    "up_out",
+    "da_far",
+    "input_grad",
+    "share_two",
+    "early_out",
+    "gate_out",
+)
+PLANS = {"down": "first", "gate": "last", "up": "first", "early": "first", "project": "first"}
+
 bf16 = jnp.bfloat16
 f32 = jnp.float32
 
@@ -55,14 +95,17 @@
         self.shape, self.dtype = tuple(shape), dtype
 
 
-def kernel_call(body, out_shapes, place, *args, scratch=(), name, flops=0, deps=()):
+class Chain:
+    def __init__(self):
+        self.token = None
+
+
+def kernel_call(body, out_shapes, chain, *args, scratch=(), name, deps=()):
     vmem = pl.BlockSpec(memory_space=pltpu.VMEM)
-    smem = pl.BlockSpec(memory_space=pltpu.SMEM)
     anywhere = pl.BlockSpec(memory_space=pl.ANY)
     size_of = lambda a: math.prod(a.shape) * jnp.dtype(a.dtype).itemsize
     held = sum(size_of(s) for s in scratch if hasattr(s, "dtype") and not is_semaphore(s))
-    operands, specs, moved = [], [], 0
-    here = Place()
+    operands, specs = [], []
     for arg in args:
         if isinstance(arg, Free):
             value = arg.value
@@ -72,25 +115,18 @@
             specs.append(anywhere if isinstance(arg, Far) else vmem)
             if not isinstance(arg, Far):
                 held += size_of(value)
-        elif arg.ndim == 1:
-            operands.append(arg)
-            specs.append(smem)
         else:
             operands.append(pltpu.with_memory_space_constraint(arg, pltpu.VMEM))
             specs.append(vmem)
-        moved += size_of(operands[-1])
-    count = len(args)
-    run = lambda *refs: body(here, *refs[:count], *refs[count + len(deps) :])
-    operands += [
-        pltpu.with_memory_space_constraint(dep.value, pltpu.HBM)
-        if isinstance(dep, Free)
-        else pltpu.with_memory_space_constraint(dep, pltpu.VMEM)
-        for dep in deps
-    ]
+    ins, outs = len(args), len(out_shapes)
+    waits = (0 if chain.token is None else 1) + len(deps)
+    operands += list(deps)
     specs += [anywhere] * len(deps)
+    if chain.token is not None:
+        operands.append(pltpu.with_memory_space_constraint(chain.token, pltpu.VMEM))
+        specs.append(vmem)
     results, result_specs = [], []
     for out in out_shapes:
-        moved += size_of(out)
         if isinstance(out, Direct):
             results.append(pltpu.HBM(out.shape, out.dtype))
             result_specs.append(anywhere)
@@ -99,7 +135,15 @@
             result_specs.append(vmem)
             if isinstance(out, jax.ShapeDtypeStruct) or out.memory_space == pltpu.HBM:
                 held += size_of(out)
-    return pl.pallas_call(
+    results.append(shaped((SUB, LANES), f32))
+    result_specs.append(vmem)
+    here = Place()
+
+    def run(*refs):
+        refs[ins + waits + outs][...] = jnp.zeros((SUB, LANES), f32)
+        body(here, *refs[:ins], *refs[ins + waits : ins + waits + outs], *refs[ins + waits + outs + 1 :])
+
+    *values, chain.token = pl.pallas_call(
         run,
         out_shape=tuple(results),
         in_specs=specs,
@@ -109,6 +153,7 @@
         cost_estimate=pl.CostEstimate(flops=0, bytes_accessed=0, transcendentals=0),
         name=name,
     )(*operands)
+    return values
 
 
 def stored(shape, dtype):
@@ -387,7 +432,7 @@
         copy.wait()
 
 
-def park(place, *pairs, name, deps=()):
+def park(chain, *pairs, name):
     arrays = [value.value if isinstance(value, Free) else value for value, _ in pairs]
     return kernel_call(
         functools.partial(park_kernel, len(pairs)),
@@ -395,11 +440,10 @@
             Direct((array.shape[0], array.shape[1] if cols is None else cols), array.dtype)
             for array, (_, cols) in zip(arrays, pairs)
         ],
-        place,
+        chain,
         *[value for value, _ in pairs],
         scratch=(pltpu.SemaphoreType.DMA((len(pairs),)),),
         name=name,
-        deps=deps,
     )
 
 
@@ -501,9 +545,12 @@
 
 
 def ffn_kernel(
-    share, place, x_ref, g_ref, fgain_ref, wg_ref, wu_ref, wd_ref, *rest,
+    axis, down_bits, gate_bits, place, x_ref, g_ref, fgain_ref, wg_ref, wu_ref, wd_ref, *rest,
 ):
-    *parts, send_ref, h_hbm, grads_hbm, hid_hbm, keep_hbm, h_s, grads_s, hid_s, keep_s, whole, left = rest
+    (
+        *parts, send_ref, down_send, gate_send, h_hbm, hid_hbm, keep_hbm, down_hbm, gate_hbm, up_hbm,
+        h_s, hid_s, keep_s, down_keep, gate_keep, grad_s, up_s, whole, left,
+    ) = rest
     y_refs, wo_refs = parts[: len(parts) // 2], parts[len(parts) // 2 :]
     att = None
     for y_ref, wo_ref in zip(y_refs, wo_refs):
@@ -524,13 +571,24 @@
     dhid = mm(g_ref[...], wd_ref[...], 1, 1)
     dgate = (dhid * up * (sg * (1.0 + gate * (1.0 - sg)))).astype(bf16)
     dup = (dhid * act).astype(bf16)
-    owners = grads_s.shape[0] // (3 * share)
-    for index, (left_side, right_side) in enumerate(((g_ref[...], hid), (b, dgate), (b, dup))):
-        grad = mm(left_side, right_side, 0, 0).astype(bf16)
-        for owner in range(owners):
-            at = (3 * owner + index) * share
-            grads_s[at : at + share, :] = grad[owner * share : (owner + 1) * share]
-    leaving.append(send_out(grads_s, grads_hbm, left, 1))
+
+    def grad_of(by_units, by_model, out):
+        if axis:
+            out[...] = mm(by_units, by_model, 0, 0).astype(bf16)
+            return
+        units = by_units.shape[1]
+        if out.shape[1] > units:
+            out[:, units:] = jnp.zeros((out.shape[0], out.shape[1] - units), bf16)
+        out[:, :units] = mm(by_model, by_units, 0, 0).astype(bf16)
+
+    grad_of(hid, g_ref[...], grad_s)
+    emit_shares(place, down_bits, grad_s, down_keep, down_send, axis)
+    leaving.append(send_out(down_keep, down_hbm, left, 1))
+    grad_of(dgate, b, grad_s)
+    emit_shares(place, gate_bits, grad_s, gate_keep, gate_send, axis)
+    leaving.append(send_out(gate_keep, gate_hbm, left, 4))
+    grad_of(dup, b, up_s)
+    leaving.append(send_out(up_s, up_hbm, left, 5))
     whole[...] = mm(dgate, wg_ref[...]) + mm(dup, wu_ref[...])
     split_rows(place, whole, keep_s, send_ref)
     leaving.append(send_out(keep_s, keep_hbm, left, 3))
@@ -553,24 +611,29 @@
     whole[pl.ds(pl.multiple_of((1 - core) * half, half), half), :] = theirs
 
 
-def emit_shares(place, bits, whole, keep_ref, send_ref):
+def emit_shares(place, bits, whole, keep_ref, send_ref, axis=0):
     order = [0]
     for bit in reversed(bits[1:]):
         order = order + [relative | (1 << bit) for relative in order]
-    block = whole.shape[0] // (2 * len(order))
+    block = whole.shape[axis] // (2 * len(order))
     for index, relative in enumerate(order):
         for ref, first in ((keep_ref, 0), (send_ref, 1 << bits[0])):
             owner = lax.bitwise_xor(place[0], jnp.int32(relative | first))
-            ref[index * block : (index + 1) * block, :] = whole[
-                pl.ds(pl.multiple_of(owner * block, block), block), :
-            ]
-
-
-def share_round_kernel(place, keep_ref, got_ref, *rest):
-    keep_out, send_out = rest[-2:]
-    half = keep_out.shape[0]
-    keep_out[...] = keep_ref[:half] + got_ref[:half]
-    send_out[...] = keep_ref[half:] + got_ref[half:]
+            source = pl.ds(pl.multiple_of(owner * block, block), block)
+            target = slice(index * block, (index + 1) * block)
+            if axis:
+                ref[:, target] = whole[:, source]
+            else:
+                ref[target, :] = whole[source, :]
+
+
+def share_round_kernel(axis, place, keep_ref, got_ref, keep_out, send_out):
+    half = keep_out.shape[axis]
+    for at, ref in ((slice(0, half), keep_out), (slice(half, 2 * half), send_out)):
+        if axis:
+            ref[...] = keep_ref[:, at] + got_ref[:, at]
+        else:
+            ref[...] = keep_ref[at] + got_ref[at]
 
 
 def out_part_kernel(place, hid_ref, wd_ref, keep_ref, send_ref, whole):
@@ -578,31 +641,35 @@
     split_rows(place, whole, keep_ref, send_ref)
 
 
-def early_grads_kernel(bits, place, gh_ref, y_ref, a_ref, dgr_ref, keep_ref, send_ref, whole):
+def emit_kernel(axis, bits, place, whole, keep_ref, send_ref):
+    emit_shares(place, bits, whole, keep_ref, send_ref, axis)
+
+
+def early_grads_kernel(
+    bits, place, gh_ref, y_ref, a_ref, dgr_ref, gq_ref, halo_ref, before_ref,
+    keep_ref, send_ref, whole,
+):
     width = dgr_ref.shape[1]
     whole[:, :width] = mm(gh_ref[...], y_ref[:, width:], 0, 0).astype(bf16)
-    whole[:, width:] = mm(a_ref[...], dgr_ref[...], 0, 0).astype(bf16)
+    whole[:, width : 2 * width] = mm(a_ref[...], dgr_ref[...], 0, 0).astype(bf16)
+    edge = jnp.concatenate([jnp.zeros((SUB, width), f32), halo_ref[...]], axis=0)
+    whole[:, 2 * width :] = (
+        mm(a_ref[...], gq_ref[...], 0, 0) + mm(before_ref[...], edge, 0, 0)
+    ).astype(bf16)
     emit_shares(place, bits, whole, keep_ref, send_ref)
 
 
-def early_sum_kernel(place, keep_ref, got_ref, turned_ref, plain_ref):
+def early_sum_kernel(place, keep_ref, got_ref, turned_ref, gate_ref, query_ref):
     total = keep_ref[...].astype(f32) + got_ref[...].astype(f32)
-    width = plain_ref.shape[1]
+    width = gate_ref.shape[1]
     turned_ref[...] = total[:, :width].T
-    plain_ref[...] = total[:, width:]
-
-
-def project_sum_kernel(place, keep_ref, got_ref, *out_refs):
+    gate_ref[...] = total[:, width : 2 * width]
+    query_ref[...] = total[:, 2 * width :]
+
+
+def ffn_share_kernel(axis, place, keep_ref, got_ref, out_ref):
     total = keep_ref[...].astype(f32) + got_ref[...].astype(f32)
-    width = out_refs[0].shape[1]
-    for index, out_ref in enumerate(out_refs):
-        out_ref[...] = total[:, index * width : (index + 1) * width]
-
-
-def ffn_shares_kernel(place, shares_ref, down_ref, gate_ref, up_ref):
-    share = shares_ref.shape[0] // 3
-    for index, ref in enumerate((down_ref, gate_ref, up_ref)):
-        ref[...] = shares_ref[index * share : (index + 1) * share].astype(f32).T
+    out_ref[...] = total if axis else total.T[: out_ref.shape[0], :]
 
 
 def residual_back_kernel(
@@ -660,34 +727,122 @@
         pull_ref[head * HEAD_DIM : (head + 1) * HEAD_DIM, :] = pulls[head].astype(bf16)
 
 
-def delta_back_kernel(
-    last_bit, place, taps_ref, back_ref, facts_ref, steps_ref, keep_ref, do_ref,
-    pack_ref, after_ref, other_ref,
-    gp_ref, halo_ref, small_ref,
+def back_places(head_width):
+    def at_of(head, chunk, part=0):
+        col = part * head_width + head * LANES
+        return (slice(chunk * CHUNK, (chunk + 1) * CHUNK), slice(col, col + LANES))
+
+    def kept_at(head, chunk, part):
+        col = (3 + part) * head_width + head * LANES
+        start = 2 * SUB + chunk * CHUNK
+        return (slice(start, start + CHUNK), slice(col, col + LANES))
+
+    return at_of, kept_at
+
+
+def fill_joined(back_ref, facts_ref, joined, joined_ids, head_width):
+    width = 3 * head_width
+    joined[0:SUB, :] = back_ref[0 : 2 * SUB, :width].astype(f32)[SUB:, :]
+    joined[SUB:, :] = back_ref[2 * SUB :, :width].astype(f32)
+    joined_ids[...] = facts_ref[:, head_width : head_width + LANES]
+
+
+def fill_lag_masks(masks, mask_s, du_s):
+    rows = mask_s.shape[1] - 2 * SUB
+    du_s[0:SUB, :] = jnp.zeros((SUB, LANES), f32)
+    du_s[SUB + rows :, :] = jnp.zeros((SUB, LANES), f32)
+    for lag in range(1, len(masks)):
+        mask_s[lag - 1, 0:SUB, :] = jnp.zeros((SUB, LANES), f32)
+        mask_s[lag - 1, SUB : SUB + rows, :] = masks[lag]
+        mask_s[lag - 1, SUB + rows :, :] = jnp.zeros((SUB, LANES), f32)
+
+
+def conv_back(taps_ref, joined, masks, mask_s, du_s, part, head, head_width, rows, grad):
+    lags = len(masks) - 1
+    col = part * head_width + head * LANES
+    cols = slice(col, col + LANES)
+    tap_cols = slice(head * LANES, (head + 1) * LANES)
+    total = conv_sum(joined, taps_ref, masks, part, head, head_width, rows)
+    sg = sigmoid(total)
+    if part < 2:
+        z = total * sg
+        norm = lax.rsqrt(jnp.sum(z * z, axis=-1, keepdims=True) + 1e-06)
+        hat = z * norm
+        grad = norm * (grad - hat * jnp.sum(grad * hat, axis=-1, keepdims=True))
+        if part == 0:
+            grad = grad * Q_SCALE
+    grad = grad * (sg * (1.0 + total * (1.0 - sg)))
+    du_s[SUB : SUB + rows, :] = grad
+    before = taps_ref[part, lags : lags + 1, tap_cols] * grad
+    halo = jnp.zeros((SUB, LANES), f32)
+    tap_grads = [None] * (lags + 1)
+    tap_grads[lags] = jnp.sum(grad * joined[SUB : SUB + rows, cols], axis=0, keepdims=True)
+    for lag in range(1, lags + 1):
+        tap = taps_ref[part, lags - lag : lags - lag + 1, tap_cols]
+        tap_grads[lags - lag] = jnp.sum(
+            grad * joined[SUB - lag : SUB - lag + rows, cols] * masks[lag], axis=0, keepdims=True
+        )
+        moved = du_s[SUB + lag : SUB + lag + rows, :]
+        before = before + tap * moved * mask_s[lag - 1, SUB + lag : SUB + lag + rows, :]
+        halo = halo + tap * du_s[lag : lag + SUB, :] * mask_s[lag - 1, lag : lag + SUB, :]
+    return before, halo, tap_grads
+
+
+def delta_query_kernel(
+    place, taps_ref, back_ref, facts_ref, keep_ref, do_ref,
+    pre_ref, dk_ref, gq_ref, halo_ref, small_ref,
     joined, joined_ids, dq_s, du_s, mask_s,
 ):
     rows, head_width = do_ref.shape
-    width = 3 * head_width
     heads = head_width // LANES
     chunks = rows // CHUNK
-    lags = taps_ref.shape[1] - 1
-    joined[0:SUB, :] = back_ref[0 : 2 * SUB, :width].astype(f32)[SUB:, :]
-    joined[SUB : SUB + rows, :] = back_ref[2 * SUB :, :width].astype(f32)
-    joined_ids[...] = facts_ref[:, head_width : head_width + LANES]
-    masks = lag_masks(joined_ids, lags)
+    fill_joined(back_ref, facts_ref, joined, joined_ids, head_width)
+    masks = lag_masks(joined_ids, taps_ref.shape[1] - 1)
+    row_ids, col_ids = tri_masks()
+    flags = [chunk_flags(joined_ids, chunk) for chunk in range(chunks)]
+    at_of, kept_at = back_places(head_width)
+    for head in range(heads):
+        for chunk in range(chunks):
+            same, opened, closing, kept = flags[chunk]
+            at = at_of(head, chunk)
+            q, k, w_rows, u_rows, scores = (
+                back_ref[kept_at(head, chunk, part)] for part in (0, 1, 3, 4, 6)
+            )
+            state, do = keep_ref[at], do_ref[at]
+            fresh = (u_rows.astype(f32) - opened * mm(w_rows, state)).astype(bf16)
+            pre_ref[at] = fresh
+            pre_ref[at_of(head, chunk, 1)] = mm(scores, do, 0, 0).astype(bf16)
+            dscore = jnp.where(row_ids >= col_ids, mm(do, fresh, 1, 1) * same, 0.0).astype(bf16)
+            dq_s[at] = opened * mm(do, state, 1, 1) + mm(dscore, k)
+            dk_ref[at] = mm(dscore, q, 0, 0)
+    fill_lag_masks(masks, mask_s, du_s)
+    small_ref[...] = jnp.zeros(small_ref.shape, f32)
+    for head in range(heads):
+        cols = slice(head * LANES, (head + 1) * LANES)
+        gq_ref[:, cols], halo_ref[:, cols], tap_grads = conv_back(
+            taps_ref, joined, masks, mask_s, du_s, 0, head, head_width, rows, dq_s[:, cols]
+        )
+        for row, tap_grad in enumerate(tap_grads):
+            small_ref[row : row + 1, cols] = tap_grad
+
+
+def delta_back_kernel(
+    last_bit, place, taps_ref, back_ref, facts_ref, steps_ref, keep_ref, do_ref, pre_ref, dk_ref,
+    pack_ref, after_ref, other_ref,
+    gp_ref, halo_ref, small_ref,
+    joined, joined_ids, dk_s, du_s, mask_s,
+):
+    rows, head_width = do_ref.shape
+    width = 2 * head_width
+    heads = head_width // LANES
+    chunks = rows // CHUNK
+    fill_joined(back_ref, facts_ref, joined, joined_ids, head_width)
+    masks = lag_masks(joined_ids, taps_ref.shape[1] - 1)
     row_ids, col_ids = tri_masks()
     flags = [chunk_flags(joined_ids, chunk) for chunk in range(chunks)]
     upper = bit_of(place, 0, last_bit)
     sets = [(head, chunk) for head in range(heads) for chunk in range(chunks)]
-
-    def at_of(head, chunk, part=0):
-        col = part * head_width + head * LANES
-        return (slice(chunk * CHUNK, (chunk + 1) * CHUNK), slice(col, col + LANES))
-
-    def saved(head, chunk, part):
-        col = (3 + part) * head_width + head * LANES
-        return back_ref[2 * SUB + chunk * CHUNK : 2 * SUB + (chunk + 1) * CHUNK, col : col + LANES]
-
+    at_of, kept_at = back_places(head_width)
     state_grads = {}
     for head in range(heads):
         at = slice(head * HEAD_DIM, (head + 1) * HEAD_DIM)
@@ -709,16 +864,17 @@
     for head, chunk in sets:
         same, opened, closing, kept = flags[chunk]
         at = at_of(head, chunk)
-        q, k, v, w_rows, u_rows, inverse, scores = (saved(head, chunk, part) for part in range(7))
+        k, v, w_rows, u_rows, inverse = (
+            back_ref[kept_at(head, chunk, part)] for part in (1, 2, 3, 4, 5)
+        )
         kf, vf = k.astype(f32), v.astype(f32)
         beta = facts_ref[
             SUB + chunk * CHUNK : SUB + (chunk + 1) * CHUNK, head * LANES : (head + 1) * LANES
         ]
-        state, do = keep_ref[at], do_ref[at]
+        state = keep_ref[at]
         sgrad = state_grads[head, chunk].astype(bf16)
-        fresh = (u_rows.astype(f32) - opened * mm(w_rows, state)).astype(bf16)
-        dfresh = mm(scores, do, 0, 0) + mm(closing * kf, sgrad)
-        dscore = jnp.where(row_ids >= col_ids, mm(do, fresh, 1, 1) * same, 0.0).astype(bf16)
+        fresh = pre_ref[at]
+        dfresh = pre_ref[at_of(head, chunk, 1)].astype(f32) + mm(closing * kf, sgrad)
         dw = -(opened * mm(dfresh, state, 1, 1))
         dx = mm(inverse, jnp.concatenate([dfresh, dw], axis=1), 0, 0)
         dxv, dxk = dx[:, :HEAD_DIM], dx[:, HEAD_DIM:]
@@ -727,15 +883,14 @@
         inner = mm(k, k, 1, 1)
         dbeta = jnp.sum(dxv * vf + dxk * kf + dlow * inner, axis=-1, keepdims=True)
         glow = (dlow * beta).astype(bf16)
-        dq_s[at_of(head, chunk, 0)] = opened * mm(do, state, 1, 1) + mm(dscore, k)
-        dq_s[at_of(head, chunk, 1)] = (
+        dk_s[at_of(head, chunk, 0)] = (
             beta * dxk
-            + mm(dscore, q, 0, 0)
+            + dk_ref[at]
             + closing * mm(fresh, sgrad, 1, 1)
             + mm(glow, k)
             + mm(glow, k, 0, 0)
         )
-        dq_s[at_of(head, chunk, 2)] = beta * dxv
+        dk_s[at_of(head, chunk, 1)] = beta * dxv
         raw = jnp.broadcast_to(dbeta, (CHUNK, LANES)) * beta * (1.0 - beta)
         gb_cols[chunk] = jnp.where(lane_ids == head, raw, gb_cols[chunk])
     bias_sum = jnp.zeros((1, LANES), f32)
@@ -743,81 +898,56 @@
         gp_ref[chunk * CHUNK : (chunk + 1) * CHUNK, width:] = gb_cols[chunk]
         bias_sum = bias_sum + jnp.sum(gb_cols[chunk], axis=0, keepdims=True)
     small_ref[...] = jnp.zeros(small_ref.shape, f32)
-    tap_count = lags + 1
-    small_ref[3 * tap_count : 3 * tap_count + 1, 0:LANES] = bias_sum
-    du_s[0:SUB, :] = jnp.zeros((SUB, LANES), f32)
-    du_s[SUB + rows :, :] = jnp.zeros((SUB, LANES), f32)
-    for lag in range(1, lags + 1):
-        mask_s[lag - 1, 0:SUB, :] = jnp.zeros((SUB, LANES), f32)
-        mask_s[lag - 1, SUB : SUB + rows, :] = masks[lag]
-        mask_s[lag - 1, SUB + rows :, :] = jnp.zeros((SUB, LANES), f32)
-    for part in range(3):
+    tap_count = len(masks)
+    small_ref[2 * tap_count : 2 * tap_count + 1, 0:LANES] = bias_sum
+    fill_lag_masks(masks, mask_s, du_s)
+    for part in (1, 2):
         for head in range(heads):
-            col = part * head_width + head * LANES
+            col = (part - 1) * head_width + head * LANES
             cols = slice(col, col + LANES)
-            tap_cols = slice(head * LANES, (head + 1) * LANES)
-            total = conv_sum(joined, taps_ref, masks, part, head, head_width, rows)
-            sg = sigmoid(total)
-            grad = dq_s[:, cols]
-            if part < 2:
-                z = total * sg
-                norm = lax.rsqrt(jnp.sum(z * z, axis=-1, keepdims=True) + 1e-06)
-                hat = z * norm
-                grad = norm * (grad - hat * jnp.sum(grad * hat, axis=-1, keepdims=True))
-                if part == 0:
-                    grad = grad * Q_SCALE
-            grad = grad * (sg * (1.0 + total * (1.0 - sg)))
-            du_s[SUB : SUB + rows, :] = grad
-            dp = taps_ref[part, lags : lags + 1, tap_cols] * grad
-            halo = jnp.zeros((SUB, LANES), f32)
-            row = part * tap_count + lags
-            small_ref[row : row + 1, tap_cols] = jnp.sum(
-                grad * joined[SUB : SUB + rows, cols], axis=0, keepdims=True
+            gp_ref[:, cols], halo_ref[:, cols], tap_grads = conv_back(
+                taps_ref, joined, masks, mask_s, du_s, part, head, head_width, rows, dk_s[:, cols]
             )
-            for lag in range(1, lags + 1):
-                tap = taps_ref[part, lags - lag : lags - lag + 1, tap_cols]
-                row = part * tap_count + lags - lag
-                small_ref[row : row + 1, tap_cols] = jnp.sum(
-                    grad * joined[SUB - lag : SUB - lag + rows, cols] * masks[lag],
-                    axis=0,
-                    keepdims=True,
-                )
-                moved = du_s[SUB + lag : SUB + lag + rows, :]
-                dp = dp + tap * moved * mask_s[lag - 1, SUB + lag : SUB + lag + rows, :]
-                halo = halo + tap * du_s[lag : lag + SUB, :] * mask_s[lag - 1, lag : lag + SUB, :]
-            gp_ref[:, cols] = dp
-            halo_ref[:, cols] = halo
+            for tap, tap_grad in enumerate(tap_grads):
+                row = (part - 1) * tap_count + tap
+                small_ref[row : row + 1, head * LANES : (head + 1) * LANES] = tap_grad
 
 
 def input_back_kernel(
-    place, gp_ref, next_ref, dgr_ref, wq_ref, wk_ref, wv_ref, wg_ref, wb_ref,
-    x_ref, sums_ref, keep_ref, send_ref, whole, gpf_ref,
+    place, gp_ref, halo_ref, gq_ref, qhalo_ref, dgr_ref, wq_ref, wk_ref, wv_ref, wg_ref, wb_ref,
+    x_ref, gain_ref, before_ref, sums_ref, whole, edge_ref, rows_ref,
 ):
-    rows, wide = gp_ref.shape
-    width = next_ref.shape[1]
-    head_width = width // 3
-    gpf_ref[...] = gp_ref[...].astype(bf16)
-    last = gp_ref[rows - 2 * SUB :, :width]
-    gpf_ref[rows - 2 * SUB :, :width] = jnp.concatenate(
-        [last[:SUB], last[SUB:] + next_ref[...]], axis=0
-    ).astype(bf16)
-    total = mm(dgr_ref[...], wg_ref[...], 1, 1) + mm(gpf_ref[:, width : width + SUB], wb_ref[...])
-    for part, w_ref in enumerate((wq_ref, wk_ref, wv_ref)):
-        total = total + mm(gpf_ref[:, part * head_width : (part + 1) * head_width], w_ref[...], 1, 1)
+    width = halo_ref.shape[1]
+    head_width = width // 2
+    zeros = jnp.zeros((SUB, head_width), f32)
+    total = mm(dgr_ref[...], wg_ref[...], 1, 1) + mm(gp_ref[:, width : width + SUB], wb_ref[...])
+    edge = None
+    first, second = slice(0, head_width), slice(head_width, width)
+    for grads, halo, w_ref in (
+        (gq_ref[...], qhalo_ref[...], wq_ref),
+        (gp_ref[:, first], halo_ref[:, first], wk_ref),
+        (gp_ref[:, second], halo_ref[:, second], wv_ref),
+    ):
+        total = total + mm(grads, w_ref[...], 1, 1)
+        piece = mm(jnp.concatenate([zeros, halo], axis=0), w_ref[...], 1, 1)
+        edge = piece if edge is None else edge + piece
     whole[...] = total
-    split_rows(place, whole, keep_ref, send_ref)
+    edge_ref[...] = edge[SUB:, :]
     x = x_ref[...].astype(f32)
     scale = lax.rsqrt(jnp.mean(x * x, axis=-1, keepdims=True) + 1e-06)
-    sums = jnp.concatenate(
-        [
-            jnp.sum(total * (x * scale), axis=0, keepdims=True),
-            sums_ref[1:2, :],
-            jnp.zeros((2 * SUB - 2, total.shape[1]), f32),
-        ],
-        axis=0,
-    ).astype(bf16)
-    keep_ref[rows // 2 :, :] = sums
-    send_ref[rows // 2 :, :] = sums
+    hat_before = before_ref[...].astype(f32) / gain_ref[...]
+    rows_ref[...] = jnp.zeros(rows_ref.shape, f32)
+    rows_ref[0:1, :] = jnp.sum(total * (x * scale), axis=0, keepdims=True) + jnp.sum(
+        edge * hat_before, axis=0, keepdims=True
+    )
+    rows_ref[1:2, :] = sums_ref[1:2, :]
+
+
+def input_split_kernel(place, whole_ref, next_ref, keep_ref, send_ref, whole):
+    rows = whole.shape[0]
+    whole[...] = whole_ref[...]
+    whole[rows - SUB :, :] = whole[rows - SUB :, :] + next_ref[...]
+    split_rows(place, whole, keep_ref, send_ref)
 
 
 def small_places(model, taps, heads, width):
@@ -837,28 +967,31 @@
 
 
 def project_grads_kernel(
-    bits, taps, place, a_ref, before_ref, gp_ref, halo_ref, sums_a, gsmall_ref,
+    bits, taps, place, a_ref, before_ref, gp_ref, halo_ref, sums_a, qsmall_ref, gsmall_ref, head_rows,
     keep_ref, send_ref, whole, small,
 ):
     a = a_ref[...]
     model = a.shape[1]
     width = whole.shape[1]
-    heads = width // (3 * LANES)
+    heads = width // (2 * LANES)
     starts, _ = small_places(model, taps, heads, width)
     small[...] = jnp.zeros(small.shape, f32)
     beta_rows = mm(gp_ref[:, width:], a, 0, 0)
     pieces = model // LANES
     for piece in range(pieces):
         cols = slice(piece * LANES, (piece + 1) * LANES)
+        small[piece_at(starts[0] + piece, width)] = head_rows[0:1, cols]
         small[piece_at(starts[2] + piece, width)] = sums_a[0:1, cols]
         for head in range(heads):
             small[piece_at(starts[4] + head * pieces + piece, width)] = beta_rows[head : head + 1, cols]
     for row in range(3 * taps):
+        ref, at = (qsmall_ref, row) if row < taps else (gsmall_ref, row - taps)
         for head in range(heads):
-            small[piece_at(starts[3] + row * heads + head, width)] = gsmall_ref[
-                row : row + 1, head * LANES : (head + 1) * LANES
+            small[piece_at(starts[3] + row * heads + head, width)] = ref[
+                at : at + 1, head * LANES : (head + 1) * LANES
             ]
-    small[piece_at(starts[5], width)] = gsmall_ref[3 * taps : 3 * taps + 1, 0:LANES]
+    small[piece_at(starts[1], width)] = head_rows[1:2, 0:LANES]
+    small[piece_at(starts[5], width)] = gsmall_ref[2 * taps : 2 * taps + 1, 0:LANES]
     edge = jnp.concatenate([jnp.zeros((SUB, width), f32), halo_ref[...]], axis=0)
     whole[...] = (mm(a, gp_ref[:, :width], 0, 0) + mm(before_ref[...], edge, 0, 0)).astype(bf16)
     emit_shares(place, bits, whole, keep_ref, send_ref)
@@ -866,41 +999,25 @@
     send_ref[model // 2 :, :] = small[...].astype(bf16)
 
 
-def head_rows_kernel(place, da_ref, out_ref):
-    out_ref[...] = da_ref[da_ref.shape[0] - 2 * SUB :, :].astype(f32)[0:SUB, :]
-
-
-def share_small_kernel(taps, place, keep_ref, got_ref, *rest):
-    keep_out, send_out_ref, small = rest[-3:]
-    width = keep_ref.shape[1]
-    heads = width // (3 * LANES)
-    tail = small.shape[0]
-    half = keep_out.shape[0] - tail
-    total = keep_ref[2 * half :, :].astype(f32) + got_ref[2 * half :, :].astype(f32)
-    small[...] = total
-    if len(rest) > 3:
-        head_own, head_got = rest[:2]
-        joint = head_own[...] + head_got[...]
-        model = joint.shape[1]
-        starts, _ = small_places(model, taps, heads, width)
-        for piece in range(model // LANES):
-            small[piece_at(starts[0] + piece, width)] = joint[0:1, piece * LANES : (piece + 1) * LANES]
-        small[piece_at(starts[1], width)] = joint[1:2, 0:LANES]
+def share_small_kernel(place, keep_ref, got_ref, keep_out, send_out_ref):
+    extra = 2 * keep_out.shape[0] - keep_ref.shape[0]
+    half = keep_out.shape[0] - extra
+    small = keep_ref[2 * half :, :] + got_ref[2 * half :, :]
     keep_out[0:half, :] = keep_ref[0:half, :] + got_ref[0:half, :]
     send_out_ref[0:half, :] = keep_ref[half : 2 * half, :] + got_ref[half : 2 * half, :]
-    keep_out[half:, :] = small[...].astype(bf16)
-    send_out_ref[half:, :] = small[...].astype(bf16)
+    keep_out[half:, :] = small
+    send_out_ref[half:, :] = small
 
 
 def project_sum_kernel(
-    taps, place, keep_ref, got_ref, q_ref, k_ref, v_ref,
+    taps, place, keep_ref, got_ref, k_ref, v_ref,
     norm_ref, hgain_ref, fgain_ref, taps_ref, beta_ref, bias_ref, small, rows_s,
 ):
-    share, head_width = q_ref.shape
-    width = 3 * head_width
+    share, head_width = k_ref.shape
+    width = 2 * head_width
     heads = head_width // LANES
     total = keep_ref[...].astype(f32) + got_ref[...].astype(f32)
-    for index, out_ref in enumerate((q_ref, k_ref, v_ref)):
+    for index, out_ref in enumerate((k_ref, v_ref)):
         out_ref[...] = total[:share, index * head_width : (index + 1) * head_width]
     small[...] = total[share:, :]
     model = norm_ref.shape[1]
@@ -952,22 +1069,12 @@
     out_ref[...] = (left_ref[...].astype(f32) + right_ref[...].astype(f32)).astype(out_ref.dtype)
 
 
-def added(place, left, right, deps=()):
+def added(chain, left, right):
     shape = left.value.shape if isinstance(left, Free) else left.shape
     (out,) = kernel_call(
-        add_kernel, (shaped(shape, right.dtype),), place, left, right, name="added", deps=deps
+        add_kernel, (shaped(shape, right.dtype),), chain, left, right, name="added"
     )
     return out
-
-
-def head_sum(place, keep, send, first=(), second=()):
-    count = lax.axis_size("head")
-    mine = added(place, keep, swap(send, "head", 1), first)
-    bit = 2
-    while bit < count:
-        mine = added(place, mine, swap(mine, "head", bit), second)
-        bit *= 2
-    return mine, swap(mine, "head", 1)
 
 
 def gathered(value):
@@ -980,20 +1087,37 @@
     return blocks + [swap(block, "head", 1) for block in blocks]
 
 
-def share_rounds(place, keep, send, bits, waits=None):
-    arrived = []
-    for index, bit in enumerate(bits):
-        got = swap(send, "seq", 1 << bit)
-        arrived.append(got)
-        if index == len(bits) - 1:
-            return (keep, got), arrived
-        shape = keep.value.shape if isinstance(keep, Free) else keep.shape
-        half = (shape[0] // 2,) + shape[1:]
-        keep, send = kernel_call(
-            share_round_kernel, (shaped(half, bf16), shaped(half, bf16)),
-            place, keep, got, name="share_round",
-            deps=waits[index] if waits and index < len(waits) else (),
-        )
+class Shares:
+    def __init__(self, keep, send, bits, axis=0):
+        self.keep, self.bits, self.axis = keep, list(bits), axis
+        self.got = swap(send, "seq", 1 << self.bits.pop(0))
+
+    def step(self, chain):
+        half = list(self.got.shape)
+        half[self.axis] //= 2
+        self.keep, send = kernel_call(
+            functools.partial(share_round_kernel, self.axis),
+            (shaped(half, bf16), shaped(half, bf16)),
+            chain, self.keep, self.got, name="share_round",
+        )
+        self.got = swap(send, "seq", 1 << self.bits.pop(0))
+
+    def until(self, chain, left):
+        while len(self.bits) > left:
+            self.step(chain)
+
+    def pair(self, chain):
+        self.until(chain, 0)
+        return self.keep, self.got
+
+
+def head_rounds(chain, value):
+    count = lax.axis_size("head")
+    bit = 1
+    while bit < count:
+        value = added(chain, value, swap(value, "head", bit))
+        bit *= 2
+    return value
 
 
 def body(
@@ -1011,8 +1135,21 @@
     width = 3 * head_width
     chunks = rows // CHUNK
     y_first = list(range(rounds))
-
-    place = Place()
+    y_last = y_first[1:] + y_first[:1]
+    y_next = y_first[1:2] + y_first[:1] + y_first[2:]
+    by_plan = {"first": y_first, "last": y_last, "next": y_next}
+    down_bits, gate_bits, up_bits, early_bits, project_bits = (
+        by_plan[PLANS[key]] for key in ("down", "gate", "up", "early", "project")
+    )
+
+    chain = Chain()
+
+    def ffn_share(chain, pair):
+        return kernel_call(
+            functools.partial(ffn_share_kernel, ffn_axis),
+            (final((ffn_width, share), f32),), chain, *pair, name="ffn_share",
+        )
+
     bias_in = beta_bias[None] if heads > 1 else jnp.broadcast_to(beta_bias[None], (1, 2))
     gain_row, fgain_row, hgain_row = Free(norm_gain[None]), Free(ffn_gain[None]), Free(head_gain[None])
     taps_in = Free(conv_weight)
@@ -1030,7 +1167,7 @@
             Direct((SUB, model), f32),
             Direct(w_out.shape, bf16),
         ),
-        place, Far(block_input), Far(w_query), Far(w_key), Far(w_value), Far(w_gate),
+        chain, Far(block_input), Far(w_query), Far(w_key), Far(w_value), Far(w_gate),
         Far(norm_gain[None]), Far(w_beta.T), Far(bias_in),
         Far(segment_ids.reshape(chunks, LANES)), Far(w_out),
         scratch=(
@@ -1048,7 +1185,6 @@
             pltpu.SemaphoreType.DMA((4,)),
         ),
         name="project",
-        flops=2 * rows * model * (4 * head_width + LANES),
     )
     halo = shift(tail, "seq", 1)
     joined = pltpu.VMEM((rows + SUB, width), f32)
@@ -1062,19 +1198,19 @@
             shaped((rows + SUB, head_width + LANES), f32),
             shaped((2 * SUB, model), bf16),
         ),
-        place, p, halo, Held(conv_weight), seg_cols, beta,
+        chain, p, halo, Held(conv_weight), seg_cols, beta,
         scratch=(joined, joined_ids),
         name="delta",
-        flops=2 * heads * chunks * 128**3 * 30,
     )
     half_maps = heads * HEAD_DIM
-    back, facts, steps, a_before = park(
-        place, (back, None), (facts, None), (mix, 2 * head_width), (a_before, None), name="park_delta"
-    )
     w_out_all = gathered(w_out_copy)
     prefix = pack = maps
     for bit in range(rounds - 1):
         other = swap(maps, "seq", 1 << bit)
+        if bit == 0:
+            back, facts, steps, a_before = park(
+                chain, (back, None), (facts, None), (mix, 2 * head_width), (a_before, None), name="park_delta"
+            )
         maps, prefix, pack = kernel_call(
             functools.partial(scan_round_kernel, bit),
             (
@@ -1082,188 +1218,377 @@
                 shaped((2 * half_maps, HEAD_DIM), bf16),
                 shaped((2 * half_maps * (bit + 1), HEAD_DIM), bf16),
             ),
-            place, maps, other, prefix, pack,
+            chain, maps, other, prefix, pack,
             name="scan_round",
-            flops=2 * heads * 128**3 * 5,
-            deps=(Held(steps),) if bit == 0 else (),
-        )
+            )
     other_a = swap(maps, "seq", 1 << (rounds - 1))
     y, mixed, keep_y = kernel_call(
         functools.partial(mixer_kernel, rounds - 1),
         (shaped(square, bf16), shaped(square, f32), shaped((rows, 2 * head_width), bf16)),
-        place, prefix, other_a, mix, Free(gate_raw), hgain_row,
+        chain, prefix, other_a, mix, Free(gate_raw), hgain_row,
         name="mixer",
-        flops=2 * heads * chunks * 128**3 * 2,
     )
     mixed, keep_y, pack = park(
-        place, (mixed, None), (keep_y, None), (pack, None), name="park_mixer"
+        chain, (mixed, None), (keep_y, None), (pack, None), name="park_mixer"
     )
     y_all = gathered(y)
     half = (rows // 2, model)
     wide = pltpu.VMEM((rows, model), f32)
-    db_send, h, grad_ffn, hidden, db_keep = kernel_call(
-        functools.partial(ffn_kernel, share),
+    ffn_wide = -(-ffn_width // LANES) * LANES
+    ffn_axis = 0 if share % LANES else 1
+    ffn_whole = (ffn_width, model) if ffn_axis else (model, ffn_wide)
+    ffn_half = (ffn_width, model // 2) if ffn_axis else (model // 2, ffn_wide)
+    (
+        db_send, down_send, gate_send, h, hidden, db_keep, down_keep, gate_keep, grad_up,
+    ) = kernel_call(
+        functools.partial(ffn_kernel, ffn_axis, down_bits, gate_bits),
         (
             shaped(half, bf16),
+            shaped(ffn_half, bf16),
+            shaped(ffn_half, bf16),
             Direct((rows, model), f32),
-            Direct((3 * model, ffn_width), bf16),
             Direct((rows, ffn_width), bf16),
             Direct(half, bf16),
+            Direct(ffn_half, bf16),
+            Direct(ffn_half, bf16),
+            Direct(ffn_whole, bf16),
         ),
-        place, Free(block_input), Free(cotangent), fgain_row,
+        chain, Free(block_input), Free(cotangent), fgain_row,
         Free(w_ffn_gate.T), Free(w_ffn_up.T), Free(w_ffn_down),
         *y_all, Free(w_out_all[0]), *w_out_all[1:],
         scratch=(
             wide,
-            pltpu.VMEM((3 * model, ffn_width), bf16),
             pltpu.VMEM((rows, ffn_width), bf16),
             pltpu.VMEM(half, bf16),
+            pltpu.VMEM(ffn_half, bf16),
+            pltpu.VMEM(ffn_half, bf16),
+            pltpu.VMEM(ffn_whole, bf16),
+            pltpu.VMEM(ffn_whole, bf16),
             wide,
-            pltpu.SemaphoreType.DMA((4,)),
+            pltpu.SemaphoreType.DMA((6,)),
         ),
-        deps=(Held(keep_y),),
         name="ffn",
-        flops=2 * rows * model * (model + 8 * ffn_width),
-    )
-    ffn_shares = lax.psum_scatter(grad_ffn, "seq", scatter_dimension=0, tiled=True)
-    out_keep, out_send = kernel_call(
-        out_part_kernel,
-        (shaped(half, bf16), shaped(half, bf16)),
-        place, Held(hidden), Held(w_ffn_down),
-        scratch=(wide,),
-        name="out_part",
-        flops=2 * rows * model * ffn_width,
-    )
-    db_parts = head_sum(place, Held(db_keep), db_send, second=(out_keep,))
-    gh, pull, dh, d_out, d_gate_raw, sums_a = kernel_call(
-        residual_back_kernel,
-        (
-            shaped((rows, model), bf16),
-            shaped((half_maps, HEAD_DIM), bf16),
-            shaped((rows, model), f32),
-            shaped(square, bf16),
-            shaped(square, bf16),
-            shaped((SUB, model), f32),
-        ),
-        place, *db_parts, Free(h), Free(cotangent), fgain_row, Free(w_out), Free(mixed),
-        Free(gate_raw), hgain_row, Free(steps),
-        scratch=(wide,),
-        name="residual_back",
-        flops=2 * rows * model * head_width,
-    )
-    dh, d_out, d_gate_raw, sums_a = park(
-        place, (dh, None), (d_out, None), (d_gate_raw, None), (sums_a, None), name="park_residual"
-    )
-    other_pulls = [swap(pull, "seq", 1)]
-    early_keep, early_send = kernel_call(
-        functools.partial(early_grads_kernel, y_first),
-        (shaped((model // 2, 2 * head_width), bf16), shaped((model // 2, 2 * head_width), bf16)),
-        place, gh, Free(keep_y), Free(a), Free(d_gate_raw),
-        scratch=(pltpu.VMEM((model, 2 * head_width), bf16),),
-        deps=(other_pulls[0],),
-        name="early_grads",
-        flops=2 * rows * model * 2 * head_width,
-    )
-    early_pair, early_got = share_rounds(place, early_keep, early_send, y_first)
-    out_parts = head_sum(place, out_keep, out_send, first=(pull,))
-    after = pull
-    for bit in range(rounds - 1):
+    )
+    down = Shares(Held(down_keep), down_send, down_bits, ffn_axis)
+    gate = Shares(Held(gate_keep), gate_send, gate_bits, ffn_axis)
+    head_bits = [1 << bit for bit in range(1, lax.axis_size("head").bit_length() - 1)]
+    pre = dk_part = gq = q_halo = q_small = q_share = None
+    conv_scratch = (
+        pltpu.VMEM((rows + 2 * SUB, LANES), f32),
+        pltpu.VMEM((taps - 1, rows + 2 * SUB, LANES), f32),
+    )
+    step_bits = list(range(rounds - 1))
+    rest_bits = list(project_bits[1:])
+    _, small_extra = small_places(model, taps, heads, 2 * head_width)
+    mine = out_keep = out_send = gh = pull = dh = d_out = d_gate_raw = sums_a = other = after = up = up_keep = up_send = out_mine = early = early_keep = early_send = gp = gp_halo = grad_small = da = da_edge = head_rows = from_next = keep = send = got = da_keep = da_send = block_output = input_grad = out_share = w_gate_share = down_share = ffn_gate_share = ffn_up_share = None
+
+    def db_core():
+        nonlocal mine
+        mine = added(chain, Held(db_keep), swap(db_send, "head", 1))
+
+    def out_part():
+        nonlocal out_keep, out_send
+        out_keep, out_send = kernel_call(
+            out_part_kernel,
+            (shaped(half, bf16), shaped(half, bf16)),
+            chain, Held(hidden), Held(w_ffn_down),
+            scratch=(wide,),
+            name="out_part",
+        )
+
+    def db_far():
+        nonlocal mine
+        for bit in head_bits:
+            mine = added(chain, mine, swap(mine, "head", bit))
+
+    def residual_back():
+        nonlocal gh, pull, dh, d_out, d_gate_raw, sums_a, other
+        gh, pull, dh, d_out, d_gate_raw, sums_a = kernel_call(
+            residual_back_kernel,
+            (
+                shaped((rows, model), bf16),
+                shaped((half_maps, HEAD_DIM), bf16),
+                shaped((rows, model), f32),
+                shaped(square, bf16),
+                shaped(square, bf16),
+                shaped((SUB, model), f32),
+            ),
+            chain, mine, swap(mine, "head", 1), Free(h), Free(cotangent), fgain_row, Free(w_out), Free(mixed),
+            Free(gate_raw), hgain_row, Free(steps),
+            scratch=(wide,),
+            name="residual_back",
+        )
+        other = swap(pull, "seq", 1)
+
+    def park_back():
+        nonlocal dh, d_out, d_gate_raw, sums_a
+        dh, d_out, d_gate_raw, sums_a = park(
+            chain, (dh, None), (d_out, None), (d_gate_raw, None), (sums_a, None), name="park_residual"
+        )
+
+    def down_one():
+        down.step(chain)
+
+    def gate_one():
+        gate.step(chain)
+
+    def scan_back():
+        nonlocal pull, other, after
+
+        bit = step_bits.pop(0)
         pull, after = kernel_call(
             functools.partial(back_round_kernel, bit),
             (shaped(pull.shape, bf16), shaped(pull.shape, bf16)),
-            place, Free(pack), pull, other_pulls[bit], after,
+            chain, Free(pack), pull, other, pull if after is None else after,
             name="back_round",
-            flops=2 * heads * 128**3 * 2,
-            deps=((Held(dh),), (early_keep,))[min(bit, 1)],
-        )
-        other_pulls.append(swap(pull, "seq", 2 << bit))
-    gp, gp_halo, grad_small = kernel_call(
-        functools.partial(delta_back_kernel, rounds - 1),
-        (
-            shaped((rows, width + LANES), f32),
-            shaped((SUB, width), f32),
-            stored((-(-(3 * taps + 1) // SUB) * SUB, head_width), f32),
-        ),
-        place, taps_in, Free(back), Free(facts), Free(steps), Free(keep_y), Free(d_out),
-        Free(pack), after, other_pulls[-1],
-        deps=(out_parts[0],),
-        scratch=(
-            joined,
-            joined_ids,
-            pltpu.VMEM((rows, width), f32),
-            pltpu.VMEM((rows + 2 * SUB, LANES), f32),
-            pltpu.VMEM((taps - 1, rows + 2 * SUB, LANES), f32),
-        ),
-        name="delta_back",
-        flops=2 * heads * chunks * 128**3 * 20,
-    )
-    from_next = shift(gp_halo, "seq", -1)
-    _, small_extra = small_places(model, taps, heads, width)
-    keep, send = kernel_call(
-        functools.partial(project_grads_kernel, y_first, taps),
-        (
-            shaped((model // 2 + small_extra, width), bf16),
-            shaped((model // 2 + small_extra, width), bf16),
-        ),
-        place, Free(a), Free(a_before), gp, gp_halo, Free(sums_a), Free(grad_small),
-        scratch=(pltpu.VMEM((model, width), bf16), pltpu.VMEM((small_extra, width), f32)),
-        name="project_grads",
-    )
-    (block_output,) = kernel_call(
-        output_kernel,
-        (final((rows, model), bf16),),
-        place, *out_parts, Free(h),
-        scratch=(wide,),
-        name="output",
-    )
-    da_keep, da_send = kernel_call(
-        input_back_kernel,
-        (
-            shaped((rows // 2 + 2 * SUB, model), bf16),
-            shaped((rows // 2 + 2 * SUB, model), bf16),
-        ),
-        place, gp, from_next, Free(d_gate_raw),
-        Free(w_query), Free(w_key), Free(w_value), Free(w_gate), Free(w_beta8), Free(block_input),
-        Free(sums_a),
-        deps=(early_got[0], keep),
-        scratch=(wide, pltpu.VMEM((rows, width + LANES), bf16)),
-        name="input_back",
-    )
-    da_parts = head_sum(place, da_keep, da_send, second=(Held(block_output), early_got[1]))
-    (head_small,) = kernel_call(
-        head_rows_kernel, (shaped((SUB, model), f32),), place, da_parts[0], name="head_rows"
-    )
-    head_got = swap(head_small, "seq", 1)
-    (input_grad,) = kernel_call(
-        input_grad_kernel,
-        (final((rows, model), f32),),
-        place, *da_parts, Free(block_input), gain_row, Free(dh),
-        scratch=(wide,),
-        name="input_grad",
-    )
-    for bit in range(rounds):
-        got = swap(send, "seq", 1 << bit)
-        if bit < rounds - 1:
-            shape = ((keep.shape[0] - small_extra) // 2 + small_extra, width)
-            keep, send = kernel_call(
-                functools.partial(share_small_kernel, taps),
-                (shaped(shape, bf16), shaped(shape, bf16)),
-                place, keep, got, *((head_small, head_got) if bit == 0 else ()),
-                scratch=(pltpu.VMEM((small_extra, width), f32),),
-                name="share_small",
-            )
-    out_share, w_gate_share = kernel_call(
-        early_sum_kernel,
-        (final((head_width, share), f32), final((share, head_width), f32)),
-        place, *early_pair, name="early_sum",
-    )
+        )
+        other = swap(pull, "seq", 2 << bit)
+
+    def scan_rest():
+        while step_bits:
+            scan_back()
+
+    def up_blocks():
+        nonlocal up, up_keep, up_send
+        up_keep, up_send = kernel_call(
+            functools.partial(emit_kernel, ffn_axis, up_bits),
+            (shaped(ffn_half, bf16), shaped(ffn_half, bf16)),
+            chain, Held(grad_up),
+            name="up_blocks",
+        )
+        up = Shares(up_keep, up_send, up_bits, ffn_axis)
+
+    def out_core():
+        nonlocal out_mine
+        out_mine = added(chain, out_keep, swap(out_send, "head", 1))
+
+    def delta_query():
+        nonlocal pre, dk_part, gq, q_halo, q_small
+        pre, dk_part, gq, q_halo, q_small = kernel_call(
+            delta_query_kernel,
+            (
+                shaped((rows, 2 * head_width), bf16),
+                shaped(square, f32),
+                stored(square, f32),
+                stored((SUB, head_width), f32),
+                stored((-(-taps // SUB) * SUB, head_width), f32),
+            ),
+            chain, taps_in, Free(back), Free(facts), Free(keep_y), Free(d_out),
+            scratch=(joined, joined_ids, pltpu.VMEM(square, f32)) + conv_scratch,
+            name="delta_query",
+        )
+
+    def early_grads():
+        nonlocal early
+        early_keep, early_send = kernel_call(
+            functools.partial(early_grads_kernel, early_bits),
+            (shaped((model // 2, width), bf16), shaped((model // 2, width), bf16)),
+            chain, gh, Free(keep_y), Free(a), Free(d_gate_raw), Held(gq), Held(q_halo), Held(a_before),
+            scratch=(pltpu.VMEM((model, width), bf16),),
+            name="early_grads",
+        )
+        early = Shares(early_keep, early_send, early_bits)
+
+    def down_two():
+        down.until(chain, 0)
+
+    def gate_two():
+        gate.until(chain, 0)
+
+    def out_far():
+        nonlocal out_mine
+        for bit in head_bits:
+            out_mine = added(chain, out_mine, swap(out_mine, "head", bit))
+
+    def delta_back():
+        nonlocal gp, gp_halo, grad_small
+        gp, gp_halo, grad_small = kernel_call(
+            functools.partial(delta_back_kernel, rounds - 1),
+            (
+                shaped((rows, 2 * head_width + LANES), f32),
+                shaped((SUB, 2 * head_width), f32),
+                stored((-(-(2 * taps + 1) // SUB) * SUB, head_width), f32),
+            ),
+            chain, taps_in, Free(back), Free(facts), Free(steps), Free(keep_y), Free(d_out),
+            pre, dk_part, Free(pack), after, other,
+            scratch=(joined, joined_ids, pltpu.VMEM((rows, 2 * head_width), f32)) + conv_scratch,
+            name="delta_back",
+        )
+
+    def input_back():
+        nonlocal da, da_edge, head_rows, from_next
+        da, da_edge, head_rows = kernel_call(
+            input_back_kernel,
+            (shaped((rows, model), f32), shaped((SUB, model), f32), shaped((SUB, model), f32)),
+            chain, gp, gp_halo, Held(gq), Held(q_halo), Free(d_gate_raw),
+            Free(w_query), Free(w_key), Free(w_value), Free(w_gate), Free(w_beta8), Free(block_input),
+            gain_row, Free(a_before), Free(sums_a),
+            name="input_back",
+        )
+        from_next = shift(da_edge, "seq", -1)
+
+    def up_one():
+        up.step(chain)
+
+    def rows_core():
+        nonlocal head_rows
+        head_rows = added(chain, head_rows, swap(head_rows, "head", 1))
+
+    def rows_far():
+        nonlocal head_rows
+        for bit in head_bits:
+            head_rows = added(chain, head_rows, swap(head_rows, "head", bit))
+
+    def project_grads():
+        nonlocal keep, send, got
+        keep, send = kernel_call(
+            functools.partial(project_grads_kernel, project_bits, taps),
+            (
+                shaped((model // 2 + small_extra, 2 * head_width), bf16),
+                shaped((model // 2 + small_extra, 2 * head_width), bf16),
+            ),
+            chain, Free(a), Free(a_before), gp, gp_halo, Free(sums_a), Held(q_small), Free(grad_small), head_rows,
+            scratch=(pltpu.VMEM((model, 2 * head_width), bf16), pltpu.VMEM((small_extra, 2 * head_width), f32)),
+            name="project_grads",
+        )
+        got = swap(send, "seq", 1 << project_bits[0])
+
+    def input_split():
+        nonlocal da_keep, da_send
+        da_keep, da_send = kernel_call(
+            input_split_kernel,
+            (shaped(half, bf16), shaped(half, bf16)),
+            chain, da, from_next,
+            scratch=(wide,),
+            name="input_split",
+        )
+
+    def early_one():
+        early.step(chain)
+
+    def up_two():
+        up.until(chain, 0)
+
+    def da_core():
+        nonlocal mine
+        mine = added(chain, da_keep, swap(da_send, "head", 1))
+
+    def da_far():
+        nonlocal mine
+        for bit in head_bits:
+            mine = added(chain, mine, swap(mine, "head", bit))
+
+    def output():
+        nonlocal block_output
+        (block_output,) = kernel_call(
+            output_kernel,
+            (final((rows, model), bf16),),
+            chain, out_mine, swap(out_mine, "head", 1), Free(h),
+            scratch=(wide,),
+            name="output",
+        )
+
+    def input_grad():
+        nonlocal input_grad
+        (input_grad,) = kernel_call(
+            input_grad_kernel,
+            (final((rows, model), f32),),
+            chain, mine, swap(mine, "head", 1), Free(block_input), gain_row, Free(dh),
+            scratch=(wide,),
+            name="input_grad",
+        )
+
+    def share_one():
+        nonlocal keep, send, got
+
+        shape = ((keep.shape[0] - small_extra) // 2 + small_extra, 2 * head_width)
+        keep, send = kernel_call(
+            share_small_kernel,
+            (shaped(shape, bf16), shaped(shape, bf16)),
+            chain, keep, got,
+            name="share_small",
+        )
+        got = swap(send, "seq", 1 << rest_bits.pop(0))
+
+    def share_two():
+        while rest_bits:
+            share_one()
+
+    def early_two():
+        early.until(chain, 0)
+
+    def down_out():
+        nonlocal down_share
+        (down_share,) = ffn_share(chain, down.pair(chain))
+
+    def up_out():
+        nonlocal ffn_up_share
+        (ffn_up_share,) = ffn_share(chain, up.pair(chain))
+
+    def gate_out():
+        nonlocal ffn_gate_share
+        (ffn_gate_share,) = ffn_share(chain, gate.pair(chain))
+
+    def early_out():
+        nonlocal out_share, w_gate_share, q_share
+        out_share, w_gate_share, q_share = kernel_call(
+            early_sum_kernel,
+            (
+                final((head_width, share), f32),
+                final((share, head_width), f32),
+                final((share, head_width), f32),
+            ),
+            chain, *early.pair(chain), name="early_sum",
+        )
+
+    parts = (
+        db_core,
+        out_part,
+        db_far,
+        residual_back,
+        park_back,
+        down_one,
+        gate_one,
+        scan_back,
+        up_blocks,
+        out_core,
+        scan_rest,
+        delta_query,
+        early_grads,
+        down_two,
+        gate_two,
+        out_far,
+        delta_back,
+        input_back,
+        up_one,
+        rows_core,
+        input_split,
+        rows_far,
+        project_grads,
+        up_two,
+        early_one,
+        da_core,
+        output,
+        down_out,
+        share_one,
+        early_two,
+        up_out,
+        da_far,
+        input_grad,
+        share_two,
+        early_out,
+        gate_out,
+    )
+    by_name = {part.__name__: part for part in parts}
+    for name in ORDER:
+        by_name[name]()
     beta_shape = (heads, model if share % LANES else share)
     (
-        q_share, k_share, v_share, norm_total, head_gain_total, ffn_gain_total, conv_total, beta_rows,
+        k_share, v_share, norm_total, head_gain_total, ffn_gain_total, conv_total, beta_rows,
         bias_total,
     ) = kernel_call(
         functools.partial(project_sum_kernel, taps),
-        tuple(final((share, head_width), f32) for _ in range(3))
+        tuple(final((share, head_width), f32) for _ in range(2))
         + (
             final((1, model), f32),
             final((1, LANES), f32),
@@ -1272,10 +1597,9 @@
             final(beta_shape, f32),
             final((1, heads), f32),
         ),
-        place, keep, got,
-        deps=(Held(input_grad), Held(out_share)),
+        chain, keep, got,
         scratch=(
-            pltpu.VMEM((small_extra, width), f32),
+            pltpu.VMEM((small_extra, 2 * head_width), f32),
             pltpu.VMEM((-(-heads * model // LANES // SUB) * SUB, LANES), f32),
         ),
         name="project_sum",
@@ -1283,11 +1607,6 @@
     if share % LANES:
         beta_rows = lax.dynamic_slice(beta_rows, (0, lax.axis_index("seq") * share), (heads, share))
     beta_share = beta_rows.T
-    down_share, ffn_gate_share, ffn_up_share = kernel_call(
-        ffn_shares_kernel,
-        tuple(final((ffn_width, share), f32) for _ in range(3)),
-        place, Free(ffn_shares), name="ffn_shares",
-    )
     return (
         block_output,
         input_grad,

time: 204 us -> 176 us (0.86)
  waiting for transfers between devices: 103 us -> 66.9 us
  starting transfers between devices: 34.5 us -> 48.9 us
  between operations: 14.6 us -> 1.33 us
  Pallas kernels: 47.5 us -> 57.8 us
  local copies, waits for them, and re-layouts: 4.56 us -> 0.16 us
    ppermute x28 -> x38, waiting for transfers between devices: 99 us -> 60.7 us  [swap(): return lax.ppermute(value, axis, [(s, s ^ bit) for s in range(count)])]
    ppermute x28 -> x38, starting transfers between devices: 29.4 us -> 43.9 us  [swap(): return lax.ppermute(value, axis, [(s, s ^ bit) for s in range(count)])]
    pallas_call x33 -> x45, Pallas kernels: 47.5 us -> 57.8 us  [kernel_call(): pl.pallas_call(run, out_shape=tuple(results), in_specs=specs, out_specs=t...]
    unnamed x70 -> x62, local copies, waits for them, and re-layouts: 4.56 us -> 0.16 us
    ppermute x2, waiting for transfers between devices: 3.61 us -> 6.2 us  [shift(): lax.ppermute(value, axis, [(s, s + step) for s in range(count) if 0 <= s...]
  transfers between devices with their start and end apart: 31 -> 40, of which waited for: 20 -> 20; matrix products, arithmetic and copies ran while one was open for 0% -> 0% of each run, Pallas kernels for 16% -> 24%
where the time goes in v3:
time: 176 us; the launch traced here: 175 us
  waiting for transfers between devices  66.9 us (38%)
  Pallas kernels  57.8 us (33%)
  starting transfers between devices  48.9 us (28%)
    ppermute x38, waiting for transfers between devices, swap(): return lax.ppermute(value, axis, [(s, s ^ bit) for s in range(count)])  60.7 us
    pallas_call x45, Pallas kernels, kernel_call(): pl.pallas_call(run, out_shape=tuple(results), in_specs=specs, out_specs=t...  57.8 us
    ppermute x38, starting transfers between devices, swap(): return lax.ppermute(value, axis, [(s, s ^ bit) for s in range(count)])  43.9 us
    ppermute x2, waiting for transfers between devices, shift(): lax.ppermute(value, axis, [(s, s + step) for s in range(count) if 0 <= s...  6.2 us
    ppermute x2, starting transfers between devices, shift(): lax.ppermute(value, axis, [(s, s + step) for s in range(count) if 0 <= s...  4.93 us
  transfers between devices with their start and end apart: 40, of which 20 were waited for; matrix products, arithmetic and copies ran while one was open for 0% of the time, Pallas kernels for 24%

profile of v3, /device:TPU:0, one launch (start us, length us, event | category | flops | bytes accessed | tf_op | source)
XLA Modules:
  0.0 175.1 jit_solution(9480214722732514260)
XLA Ops:
  0.6 4.2 %project.1 = (bf16[384,768]{1,0:T(8,128)(2,1)S(1)}, f32[384,256]{1,0:T(8,128)S(1)}, f32[384,128]{1,0:T(8,128)S(1)}, f32[8,1920]{1,0:T(8,128)S(1)}, bf16[384,1024...) custom-call(bf16[384,1024]{1,0:T(8,128)(2,1)} %refs_2_.5, ...), custom_call_target="tpu_custom_call" | custom-call | tf_op jit(solution)/shard_map/project/pallas_call | solution.py:146
  4.8 3.0 %collective-permute-start.7 = (bf16[256,1024]{1,0:T(8,128)(2,1)}, bf16[256,1024]{1,0:T(8,128)(2,1)S(1)}, u32[]{:S(2)}, u32[]{:S(2)}) collective-permute-start(bf16[256,1024]{1,0:T(8,128)(2,1)} %get-tuple-element.198.refs_10_), channel_id=1, source_target_pairs={{0,2},{1,3},{2,0},{3,1},{4,6},{5,7},{6,4},{7,5},{8,10},{9,11},{10,... | collective-permute-start | bytes 1572872 | tf_op jit(solution)/shard_map/ppermute | solution.py:185
  7.8 3.4 %collective-permute-start = (f32[8,1920]{1,0:T(8,128)S(1)}, f32[8,1920]{1,0:T(8,128)S(1)}, u32[]{:S(2)}, u32[]{:S(2)}) collective-permute-start(f32[8,1920]{1,0:T(8,128)S(1)} %get-tuple-element.178), channel_id=1, source_target_pairs={{0,4},{4,8},{8,12},{12,16},{16,20},{20,24},{24,28},{1,5},{5,9},{9,... | collective-permute-start | bytes 184328 | tf_op jit(solution)/shard_map/ppermute | solution.py:190
  13.1 4.6 %delta.1 = (bf16[512,128]{1,0:T(8,128)(2,1)S(1)}, bf16[400,1024]{1,0:T(8,128)(2,1)S(1)}, bf16[400,2560]{1,0:T(8,128)(2,1)S(1)}, f32[392,384]{1,0:T(8,128)S(1)}, ...) custom-call(bf16[384,768]{1,0:T(8,128)(2,1)S(1)} %get-tuple-element.177.refs_0_, ...), custom_call_target="tpu_custom_call" | custom-call | tf_op jit(solution)/shard_map/delta/pallas_call | solution.py:146
  17.7 2.4 %collective-permute-start.1 = (bf16[512,128]{1,0:T(8,128)(2,1)S(1)}, bf16[512,128]{1,0:T(8,128)(2,1)S(1)}, u32[]{:S(2)}, u32[]{:S(2)}) collective-permute-start(bf16[512,128]{1,0:T(8,128)(2,1)S(1)} %get-tuple-element.182.refs_0_.refs_2_.refs_3_), channel_id=1, source_target_pairs={{0,4},{4,0},{8,12},{12,8},{16,20},{20,16},{24,28},{28,24},{1,5},{5... | collective-permute-start | bytes 393224 | tf_op jit(solution)/shard_map/ppermute | solution.py:185
  23.3 3.0 %collective-permute-start.2 = (bf16[512,128]{1,0:T(8,128)(2,1)S(1)}, bf16[512,128]{1,0:T(8,128)(2,1)S(1)}, u32[]{:S(2)}, u32[]{:S(2)}) collective-permute-start(bf16[512,128]{1,0:T(8,128)(2,1)S(1)} %get-tuple-element.189.refs_0_), channel_id=1, source_target_pairs={{0,8},{4,12},{8,0},{12,4},{16,24},{20,28},{24,16},{28,20},{1,9},{5... | collective-permute-start | bytes 393224 | tf_op jit(solution)/shard_map/ppermute | solution.py:185
  29.6 3.8 %collective-permute-start.3 = (bf16[256,128]{1,0:T(8,128)(2,1)S(1)}, bf16[256,128]{1,0:T(8,128)(2,1)S(1)}, u32[]{:S(2)}, u32[]{:S(2)}) collective-permute-start(bf16[256,128]{1,0:T(8,128)(2,1)S(1)} %get-tuple-element.194), channel_id=1, source_target_pairs={{0,16},{4,20},{8,24},{12,28},{16,0},{20,4},{24,8},{28,12},{1,17},{... | collective-permute-start | bytes 196616 | tf_op jit(solution)/shard_map/ppermute | solution.py:185
  37.2 5.1 %collective-permute-done.4.refs_7_ = bf16[384,256]{1,0:T(8,128)(2,1)S(1)} collective-permute-done((bf16[384,256]{1,0:T(8,128)(2,1)S(1)}, bf16[384,256]{1,0:T(8,128)(2,1)S(1)}, u32[]{:S(2)}, u32[]{:S(2)}) %collective-permute-start.4) | collective-permute-done | bytes 196640 | tf_op jit(solution)/shard_map/ppermute | solution.py:185
  43.9 9.7 %ffn.1 = (bf16[192,1024]{1,0:T(8,128)(2,1)S(1)}, bf16[704,512]{1,0:T(8,128)(2,1)S(1)}, bf16[704,512]{1,0:T(8,128)(2,1)S(1)}, f32[384,1024]{1,0:T(8,128)}, bf16[3...) custom-call(bf16[384,1024]{1,0:T(8,128)(2,1)S(1)} %copy-done, ...), custom_call_target="tpu_custom_call" | custom-call | tf_op jit(solution)/shard_map/ffn/pallas_call | solution.py:146
  58.9 2.5 %out_part.1 = (bf16[192,1024]{1,0:T(8,128)(2,1)S(1)}, bf16[192,1024]{1,0:T(8,128)(2,1)S(1)}, f32[8,128]{1,0:T(8,128)S(1)}) custom-call(bf16[384,704]{1,0:T(8,128)(2,1)} %get-tuple-element.204.refs_0_, bf16[704,1024]{1,0:T(8,128)(2,1)} %refs_1_.5, f32[8,128]{1,0:T(8,128)S(1)} %get-tuple-element.208.refs_2_), custom_call_target="tpu_custom_call" | custom-call | tf_op jit(solution)/shard_map/out_part/pallas_call | solution.py:146
  61.5 6.3 %collective-permute-done.12.refs_1_ = bf16[192,1024]{1,0:T(8,128)(2,1)S(1)} collective-permute-done((bf16[192,1024]{1,0:T(8,128)(2,1)S(1)}, bf16[192,1024]{1,0:T(8,128)(2,1)S(1)}, u32[]{:S(2)}, u32[]{:S(2)}) %collective-permute-start.12) | collective-permute-done | bytes 393248 | tf_op jit(solution)/shard_map/ppermute | solution.py:185
  84.7 3.0 %collective-permute-start.18 = (bf16[704,256]{1,0:T(8,128)(2,1)S(1)}, bf16[704,256]{1,0:T(8,128)(2,1)S(1)}, u32[]{:S(2)}, u32[]{:S(2)}) collective-permute-start(bf16[704,256]{1,0:T(8,128)(2,1)S(1)} %get-tuple-element.237), channel_id=1, source_target_pairs={{0,16},{4,20},{8,24},{12,28},{16,0},{20,4},{24,8},{28,12},{1,17},{... | collective-permute-start | bytes 1081352 | tf_op jit(solution)/shard_map/ppermute | solution.py:185
  88.0 3.1 %delta_query.1 = (bf16[384,512]{1,0:T(8,128)(2,1)S(1)}, f32[384,256]{1,0:T(8,128)S(1)}, f32[384,256]{1,0:T(8,128)}, f32[8,256]{1,0:T(8,128)}, f32[8,256]{1,0:T(8,128)}, /*index=5*/f32[8,128]{1,0:T(8,128)S(1)}) custom-call(f32[3,4,256]{2,1,0:T(4,128)S(1)} %copy-done.25, bf16[400,2560]{1,0:T(8,128)(2,1)S(1)} %copy-done.1, f32[392,384]{1,0:T(8,128)S(1)} %copy-done.7, ...), custom_call_target="tpu_custom_call" | custom-call | tf_op jit(solution)/shard_map/delta_query/pallas_call | solution.py:146
  93.4 5.2 %collective-permute-start.27 = (bf16[512,768]{1,0:T(8,128)(2,1)S(1)}, bf16[512,768]{1,0:T(8,128)(2,1)S(1)}, u32[]{:S(2)}, u32[]{:S(2)}) collective-permute-start(bf16[512,768]{1,0:T(8,128)(2,1)S(1)} %get-tuple-element.280), channel_id=1, source_target_pairs={{0,4},{4,0},{8,12},{12,8},{16,20},{20,16},{24,28},{28,24},{1,5},{5... | collective-permute-start | bytes 2359304 | tf_op jit(solution)/shard_map/ppermute | solution.py:185
  99.5 5.1 %collective-permute-done.22.refs_10_ = bf16[256,128]{1,0:T(8,128)(2,1)S(1)} collective-permute-done((bf16[256,128]{1,0:T(8,128)(2,1)S(1)}, bf16[256,128]{1,0:T(8,128)(2,1)S(1)}, u32[]{:S(2)}, u32[]{:S(2)}) %collective-permute-start.22) | collective-permute-done | bytes 65568 | tf_op jit(solution)/shard_map/ppermute | solution.py:185
  104.7 5.3 %delta_back.1 = (f32[384,640]{1,0:T(8,128)S(1)}, f32[8,512]{1,0:T(8,128)S(1)}, f32[16,256]{1,0:T(8,128)}, f32[8,128]{1,0:T(8,128)S(1)}) custom-call(f32[3,4,256]{2,1,0:T(4,128)S(1)} %copy-done.25, bf16[400,2560]{1,0:T(8,128)(2,1)S(1)} %copy-done.1, f32[392,384]{1,0:T(8,128)S(1)} %copy-done.7, bf16[400,512]{1,0:T(8,128)(2,1)S(1)} %copy-done.14, ...), custom_call_target="tpu_custom_call" | custom-call | tf_op jit(solution)/shard_map/delta_back/pallas_call | solution.py:146
  110.0 2.6 %input_back.1 = (f32[384,1024]{1,0:T(8,128)S(1)}, f32[8,1024]{1,0:T(8,128)S(1)}, f32[8,1024]{1,0:T(8,128)S(1)}, f32[8,128]{1,0:T(8,128)S(1)}) custom-call(f32[384,640]{1,0:T(8,128)S(1)} %get-tuple-element.264.refs_0_.refs_2_, f32[8,512]{1,0:T(8,128)S(1)} %get-tuple-element.265.refs_1_.refs_3_, f32[384,256]{1,0:T(8,128)} %get-tuple-element.251.refs_4_.refs_2_, ...), custom_call_target="tpu_custom_call" | custom-call | tf_op jit(solution)/shard_map/input_back/pallas_call | solution.py:146
  114.4 4.4 %collective-permute-done.23.refs_1_ = f32[8,1024]{1,0:T(8,128)S(1)} collective-permute-done((f32[8,1024]{1,0:T(8,128)S(1)}, f32[8,1024]{1,0:T(8,128)S(1)}, u32[]{:S(2)}, u32[]{:S(2)}) %collective-permute-start.23) | collective-permute-done | bytes 32800 | tf_op jit(solution)/shard_map/ppermute | solution.py:190
  119.3 2.7 %collective-permute-start.29 = (f32[8,1024]{1,0:T(8,128)S(1)}, f32[8,1024]{1,0:T(8,128)S(1)}, u32[]{:S(2)}, u32[]{:S(2)}) collective-permute-start(f32[8,1024]{1,0:T(8,128)S(1)} %get-tuple-element.285.refs_0_), channel_id=1, source_target_pairs={{0,2},{1,3},{2,0},{3,1},{4,6},{5,7},{6,4},{7,5},{8,10},{9,11},{10,... | collective-permute-start | bytes 98312 | tf_op jit(solution)/shard_map/ppermute | solution.py:185
  130.4 2.9 %collective-permute-start.30 = (bf16[192,1024]{1,0:T(8,128)(2,1)S(1)}, bf16[192,1024]{1,0:T(8,128)(2,1)S(1)}, u32[]{:S(2)}, u32[]{:S(2)}) collective-permute-start(bf16[192,1024]{1,0:T(8,128)(2,1)S(1)} %get-tuple-element.294.refs_0_), channel_id=1, source_target_pairs={{0,2},{1,3},{2,0},{3,1},{4,6},{5,7},{6,4},{7,5},{8,10},{9,11},{10,... | collective-permute-start | bytes 1179656 | tf_op jit(solution)/shard_map/ppermute | solution.py:185
  137.4 6.4 %collective-permute-done.34.refs_1_ = bf16[704,128]{1,0:T(8,128)(2,1)S(1)} collective-permute-done((bf16[704,128]{1,0:T(8,128)(2,1)S(1)}, bf16[704,128]{1,0:T(8,128)(2,1)S(1)}, u32[]{:S(2)}, u32[]{:S(2)}) %collective-permute-start.34) | collective-permute-done | bytes 180256 | tf_op jit(solution)/shard_map/ppermute | solution.py:185
  147.0 4.6 %collective-permute-done.31.refs_1_ = bf16[704,128]{1,0:T(8,128)(2,1)S(1)} collective-permute-done((bf16[704,128]{1,0:T(8,128)(2,1)S(1)}, bf16[704,128]{1,0:T(8,128)(2,1)S(1)}, u32[]{:S(2)}, u32[]{:S(2)}) %collective-permute-start.31) | collective-permute-done | bytes 180256 | tf_op jit(solution)/shard_map/ppermute | solution.py:185
  157.5 8.3 %collective-permute-done.36.refs_1_ = bf16[272,512]{1,0:T(8,128)(2,1)S(1)} collective-permute-done((bf16[272,512]{1,0:T(8,128)(2,1)S(1)}, bf16[272,512]{1,0:T(8,128)(2,1)S(1)}, u32[]{:S(2)}, u32[]{:S(2)}) %collective-permute-start.36) | collective-permute-done | bytes 278560 | tf_op jit(solution)/shard_map/ppermute | solution.py:185
  167.5 6.9 %collective-permute-done.37.refs_1_ = bf16[144,512]{1,0:T(8,128)(2,1)S(1)} collective-permute-done((bf16[144,512]{1,0:T(8,128)(2,1)S(1)}, bf16[144,512]{1,0:T(8,128)(2,1)S(1)}, u32[]{:S(2)}, u32[]{:S(2)}) %collective-permute-start.37) | collective-permute-done | bytes 147488 | tf_op jit(solution)/shard_map/ppermute | solution.py:185
  (163 shorter events, 65.3 us)
Async XLA Ops:
  4.8 21.5 %collective-permute-start.7 = (bf16[256,1024]{1,0:T(8,128)(2,1)}, bf16[256,1024]{1,0:T(8,128)(2,1)S(1)}, u32[]{:S(2)}, u32[]{:S(2)}) collective-permute-start(bf16[256,1024]{1,0:T(8,128)(2,1)} %get-tuple-element.198.refs_10_), channel_id=1, source_target_pairs={{0,2},{1,3},{2,0},{3,1},{4,6},{5,7},{6,4},{7,5},{8,10},{9,11},{10,... | collective-permute-start | bytes 1572872 | tf_op jit(solution)/shard_map/ppermute | solution.py:185
  26.4 17.0 %collective-permute-start.8 = (bf16[256,1024]{1,0:T(8,128)(2,1)S(1)}, bf16[256,1024]{1,0:T(8,128)(2,1)S(1)}, u32[]{:S(2)}, u32[]{:S(2)}) collective-permute-start(bf16[256,1024]{1,0:T(8,128)(2,1)S(1)} %copy-done.21), channel_id=1, source_target_pairs={{0,1},{1,0},{2,3},{3,2},{4,5},{5,4},{6,7},{7,6},{8,9},{9,8},{10,11... | collective-permute-start | bytes 1572872 | tf_op jit(solution)/shard_map/ppermute | solution.py:185
  26.4 17.4 %collective-permute-start.9 = (bf16[256,1024]{1,0:T(8,128)(2,1)S(1)}, bf16[256,1024]{1,0:T(8,128)(2,1)S(1)}, u32[]{:S(2)}, u32[]{:S(2)}) collective-permute-start(bf16[256,1024]{1,0:T(8,128)(2,1)S(1)} %collective-permute-done.7.refs_11_), channel_id=1, source_target_pairs={{0,1},{1,0},{2,3},{3,2},{4,5},{5,4},{6,7},{7,6},{8,9},{9,8},{10,11... | collective-permute-start | bytes 1572872 | tf_op jit(solution)/shard_map/ppermute | solution.py:185
  56.5 11.2 %collective-permute-start.12 = (bf16[192,1024]{1,0:T(8,128)(2,1)S(1)}, bf16[192,1024]{1,0:T(8,128)(2,1)S(1)}, u32[]{:S(2)}, u32[]{:S(2)}) collective-permute-start(bf16[192,1024]{1,0:T(8,128)(2,1)S(1)} %get-tuple-element.213.refs_0_), channel_id=1, source_target_pairs={{0,2},{1,3},{2,0},{3,1},{4,6},{5,7},{6,4},{7,5},{8,10},{9,11},{10,... | collective-permute-start | bytes 1179656 | tf_op jit(solution)/shard_map/ppermute | solution.py:185
  57.1 18.4 %collective-permute-start.16 = (bf16[704,512]{1,0:T(8,128)(2,1)S(1)}, bf16[704,512]{1,0:T(8,128)(2,1)S(1)}, u32[]{:S(2)}, u32[]{:S(2)}) collective-permute-start(bf16[704,512]{1,0:T(8,128)(2,1)S(1)} %get-tuple-element.224), channel_id=1, source_target_pairs={{0,4},{4,0},{8,12},{12,8},{16,20},{20,16},{24,28},{28,24},{1,5},{5... | collective-permute-start | bytes 2162696 | tf_op jit(solution)/shard_map/ppermute | solution.py:185
  57.7 19.1 %collective-permute-start.15 = (bf16[704,512]{1,0:T(8,128)(2,1)S(1)}, bf16[704,512]{1,0:T(8,128)(2,1)S(1)}, u32[]{:S(2)}, u32[]{:S(2)}) collective-permute-start(bf16[704,512]{1,0:T(8,128)(2,1)S(1)} %get-tuple-element.222), channel_id=1, source_target_pairs={{0,8},{4,12},{8,0},{12,4},{16,24},{20,28},{24,16},{28,20},{1,9},{5... | collective-permute-start | bytes 2162696 | tf_op jit(solution)/shard_map/ppermute | solution.py:185
  67.9 14.8 %collective-permute-start.11 = (bf16[192,1024]{1,0:T(8,128)(2,1)S(1)}, bf16[192,1024]{1,0:T(8,128)(2,1)S(1)}, u32[]{:S(2)}, u32[]{:S(2)}) collective-permute-start(bf16[192,1024]{1,0:T(8,128)(2,1)S(1)} %get-tuple-element.210), channel_id=1, source_target_pairs={{0,1},{1,0},{2,3},{3,2},{4,5},{5,4},{6,7},{7,6},{8,9},{9,8},{10,11... | collective-permute-start | bytes 1179656 | tf_op jit(solution)/shard_map/ppermute | solution.py:185
  80.1 34.1 %collective-permute-start.25 = (bf16[704,512]{1,0:T(8,128)(2,1)S(1)}, bf16[704,512]{1,0:T(8,128)(2,1)S(1)}, u32[]{:S(2)}, u32[]{:S(2)}) collective-permute-start(bf16[704,512]{1,0:T(8,128)(2,1)S(1)} %get-tuple-element.273), channel_id=1, source_target_pairs={{0,4},{4,0},{8,12},{12,8},{16,20},{20,16},{24,28},{28,24},{1,5},{5... | collective-permute-start | bytes 2162696 | tf_op jit(solution)/shard_map/ppermute | solution.py:185
  81.9 17.2 %collective-permute-start.19 = (bf16[704,256]{1,0:T(8,128)(2,1)S(1)}, bf16[704,256]{1,0:T(8,128)(2,1)S(1)}, u32[]{:S(2)}, u32[]{:S(2)}) collective-permute-start(bf16[704,256]{1,0:T(8,128)(2,1)S(1)} %get-tuple-element.239), channel_id=1, source_target_pairs={{0,8},{4,12},{8,0},{12,4},{16,24},{20,28},{24,16},{28,20},{1,9},{5... | collective-permute-start | bytes 1081352 | tf_op jit(solution)/shard_map/ppermute | solution.py:185
  82.8 16.6 %collective-permute-start.17 = (bf16[192,1024]{1,0:T(8,128)(2,1)S(1)}, bf16[192,1024]{1,0:T(8,128)(2,1)S(1)}, u32[]{:S(2)}, u32[]{:S(2)}) collective-permute-start(bf16[192,1024]{1,0:T(8,128)(2,1)S(1)} %get-tuple-element.235.refs_0_), channel_id=1, source_target_pairs={{0,2},{1,3},{2,0},{3,1},{4,6},{5,7},{6,4},{7,5},{8,10},{9,11},{10,... | collective-permute-start | bytes 1179656 | tf_op jit(solution)/shard_map/ppermute | solution.py:185
  84.7 14.5 %collective-permute-start.18 = (bf16[704,256]{1,0:T(8,128)(2,1)S(1)}, bf16[704,256]{1,0:T(8,128)(2,1)S(1)}, u32[]{:S(2)}, u32[]{:S(2)}) collective-permute-start(bf16[704,256]{1,0:T(8,128)(2,1)S(1)} %get-tuple-element.237), channel_id=1, source_target_pairs={{0,16},{4,20},{8,24},{12,28},{16,0},{20,4},{24,8},{28,12},{1,17},{... | collective-permute-start | bytes 1081352 | tf_op jit(solution)/shard_map/ppermute | solution.py:185
  93.4 36.5 %collective-permute-start.27 = (bf16[512,768]{1,0:T(8,128)(2,1)S(1)}, bf16[512,768]{1,0:T(8,128)(2,1)S(1)}, u32[]{:S(2)}, u32[]{:S(2)}) collective-permute-start(bf16[512,768]{1,0:T(8,128)(2,1)S(1)} %get-tuple-element.280), channel_id=1, source_target_pairs={{0,4},{4,0},{8,12},{12,8},{16,20},{20,16},{24,28},{28,24},{1,5},{5... | collective-permute-start | bytes 2359304 | tf_op jit(solution)/shard_map/ppermute | solution.py:185
  118.9 11.4 %collective-permute-start.26 = (bf16[192,1024]{1,0:T(8,128)(2,1)S(1)}, bf16[192,1024]{1,0:T(8,128)(2,1)S(1)}, u32[]{:S(2)}, u32[]{:S(2)}) collective-permute-start(bf16[192,1024]{1,0:T(8,128)(2,1)S(1)} %get-tuple-element.278), channel_id=1, source_target_pairs={{0,1},{1,0},{2,3},{3,2},{4,5},{5,4},{6,7},{7,6},{8,9},{9,8},{10,11... | collective-permute-start | bytes 1179656 | tf_op jit(solution)/shard_map/ppermute | solution.py:185
  119.0 10.8 %collective-permute-start.28 = (bf16[704,256]{1,0:T(8,128)(2,1)S(1)}, bf16[704,256]{1,0:T(8,128)(2,1)S(1)}, u32[]{:S(2)}, u32[]{:S(2)}) collective-permute-start(bf16[704,256]{1,0:T(8,128)(2,1)S(1)} %get-tuple-element.282), channel_id=1, source_target_pairs={{0,8},{4,12},{8,0},{12,4},{16,24},{20,28},{24,16},{28,20},{1,9},{5... | collective-permute-start | bytes 1081352 | tf_op jit(solution)/shard_map/ppermute | solution.py:185
  121.9 12.8 %collective-permute-start.21 = (bf16[192,1024]{1,0:T(8,128)(2,1)S(1)}, bf16[192,1024]{1,0:T(8,128)(2,1)S(1)}, u32[]{:S(2)}, u32[]{:S(2)}) collective-permute-start(bf16[192,1024]{1,0:T(8,128)(2,1)S(1)} %get-tuple-element.258.refs_0_), channel_id=1, source_target_pairs={{0,1},{1,0},{2,3},{3,2},{4,5},{5,4},{6,7},{7,6},{8,9},{9,8},{10,11... | collective-permute-start | bytes 1179656 | tf_op jit(solution)/shard_map/ppermute | solution.py:185
  125.8 18.8 %collective-permute-start.33 = (bf16[528,512]{1,0:T(8,128)(2,1)S(1)}, bf16[528,512]{1,0:T(8,128)(2,1)S(1)}, u32[]{:S(2)}, u32[]{:S(2)}) collective-permute-start(bf16[528,512]{1,0:T(8,128)(2,1)S(1)} %get-tuple-element.300), channel_id=1, source_target_pairs={{0,4},{4,0},{8,12},{12,8},{16,20},{20,16},{24,28},{28,24},{1,5},{5... | collective-permute-start | bytes 1622024 | tf_op jit(solution)/shard_map/ppermute | solution.py:185
  130.0 16.9 %collective-permute-start.32 = (bf16[256,768]{1,0:T(8,128)(2,1)S(1)}, bf16[256,768]{1,0:T(8,128)(2,1)S(1)}, u32[]{:S(2)}, u32[]{:S(2)}) collective-permute-start(bf16[256,768]{1,0:T(8,128)(2,1)S(1)} %get-tuple-element.298), channel_id=1, source_target_pairs={{0,8},{4,12},{8,0},{12,4},{16,24},{20,28},{24,16},{28,20},{1,9},{5... | collective-permute-start | bytes 1179656 | tf_op jit(solution)/shard_map/ppermute | solution.py:185
  130.4 21.9 %collective-permute-start.30 = (bf16[192,1024]{1,0:T(8,128)(2,1)S(1)}, bf16[192,1024]{1,0:T(8,128)(2,1)S(1)}, u32[]{:S(2)}, u32[]{:S(2)}) collective-permute-start(bf16[192,1024]{1,0:T(8,128)(2,1)S(1)} %get-tuple-element.294.refs_0_), channel_id=1, source_target_pairs={{0,2},{1,3},{2,0},{3,1},{4,6},{5,7},{6,4},{7,5},{8,10},{9,11},{10,... | collective-permute-start | bytes 1179656 | tf_op jit(solution)/shard_map/ppermute | solution.py:185
  133.3 10.5 %collective-permute-start.34 = (bf16[704,128]{1,0:T(8,128)(2,1)S(1)}, bf16[704,128]{1,0:T(8,128)(2,1)S(1)}, u32[]{:S(2)}, u32[]{:S(2)}) collective-permute-start(bf16[704,128]{1,0:T(8,128)(2,1)S(1)} %get-tuple-element.302), channel_id=1, source_target_pairs={{0,16},{4,20},{8,24},{12,28},{16,0},{20,4},{24,8},{28,12},{1,17},{... | collective-permute-start | bytes 540680 | tf_op jit(solution)/shard_map/ppermute | solution.py:185
  134.7 16.9 %collective-permute-start.31 = (bf16[704,128]{1,0:T(8,128)(2,1)S(1)}, bf16[704,128]{1,0:T(8,128)(2,1)S(1)}, u32[]{:S(2)}, u32[]{:S(2)}) collective-permute-start(bf16[704,128]{1,0:T(8,128)(2,1)S(1)} %get-tuple-element.296), channel_id=1, source_target_pairs={{0,16},{4,20},{8,24},{12,28},{16,0},{20,4},{24,8},{28,12},{1,17},{... | collective-permute-start | bytes 540680 | tf_op jit(solution)/shard_map/ppermute | solution.py:185
  152.5 13.3 %collective-permute-start.36 = (bf16[272,512]{1,0:T(8,128)(2,1)S(1)}, bf16[272,512]{1,0:T(8,128)(2,1)S(1)}, u32[]{:S(2)}, u32[]{:S(2)}) collective-permute-start(bf16[272,512]{1,0:T(8,128)(2,1)S(1)} %get-tuple-element.313), channel_id=1, source_target_pairs={{0,8},{4,12},{8,0},{12,4},{16,24},{20,28},{24,16},{28,20},{1,9},{5... | collective-permute-start | bytes 835592 | tf_op jit(solution)/shard_map/ppermute | solution.py:185
  152.6 13.3 %collective-permute-start.39 = (bf16[128,768]{1,0:T(8,128)(2,1)S(1)}, bf16[128,768]{1,0:T(8,128)(2,1)S(1)}, u32[]{:S(2)}, u32[]{:S(2)}) collective-permute-start(bf16[128,768]{1,0:T(8,128)(2,1)S(1)} %get-tuple-element.320), channel_id=1, source_target_pairs={{0,16},{4,20},{8,24},{12,28},{16,0},{20,4},{24,8},{28,12},{1,17},{... | collective-permute-start | bytes 589832 | tf_op jit(solution)/shard_map/ppermute | solution.py:185
  154.5 12.3 %collective-permute-start.38 = (bf16[704,128]{1,0:T(8,128)(2,1)S(1)}, bf16[704,128]{1,0:T(8,128)(2,1)S(1)}, u32[]{:S(2)}, u32[]{:S(2)}) collective-permute-start(bf16[704,128]{1,0:T(8,128)(2,1)S(1)} %get-tuple-element.318), channel_id=1, source_target_pairs={{0,4},{4,0},{8,12},{12,8},{16,20},{20,16},{24,28},{28,24},{1,5},{5... | collective-permute-start | bytes 540680 | tf_op jit(solution)/shard_map/ppermute | solution.py:185
  165.9 8.5 %collective-permute-start.37 = (bf16[144,512]{1,0:T(8,128)(2,1)S(1)}, bf16[144,512]{1,0:T(8,128)(2,1)S(1)}, u32[]{:S(2)}, u32[]{:S(2)}) collective-permute-start(bf16[144,512]{1,0:T(8,128)(2,1)S(1)} %get-tuple-element.316), channel_id=1, source_target_pairs={{0,16},{4,20},{8,24},{12,28},{16,0},{20,4},{24,8},{28,12},{1,17},{... | collective-permute-start | bytes 442376 | tf_op jit(solution)/shard_map/ppermute | solution.py:185
  (47 other events, 419.5 us)

commit v4 on v3

--- a/solution.py
+++ b/solution.py
@@ -17,26 +17,26 @@
 
 ORDER = (
     "db_core",
-    "out_part",
     "db_far",
     "residual_back",
+    "out_part",
+    "gate_one",
+    "down_one",
     "park_back",
-    "down_one",
-    "gate_one",
     "scan_back",
     "up_blocks",
+    "down_two",
     "out_core",
     "scan_rest",
     "delta_query",
     "early_grads",
-    "down_two",
     "gate_two",
-    "out_far",
     "delta_back",
     "input_back",
-    "up_one",
     "rows_core",
     "input_split",
+    "out_far",
+    "up_one",
     "rows_far",
     "project_grads",
     "up_two",
@@ -48,10 +48,10 @@
     "early_two",
     "up_out",
     "da_far",
+    "share_two",
+    "gate_out",
+    "early_out",
     "input_grad",
-    "share_two",
-    "early_out",
-    "gate_out",
 )
 PLANS = {"down": "first", "gate": "last", "up": "first", "early": "first", "project": "first"}
 
@@ -1269,8 +1269,8 @@
         ),
         name="ffn",
     )
-    down = Shares(Held(down_keep), down_send, down_bits, ffn_axis)
-    gate = Shares(Held(gate_keep), gate_send, gate_bits, ffn_axis)
+    down = Shares(Free(down_keep), down_send, down_bits, ffn_axis)
+    gate = Shares(Free(gate_keep), gate_send, gate_bits, ffn_axis)
     head_bits = [1 << bit for bit in range(1, lax.axis_size("head").bit_length() - 1)]
     pre = dk_part = gq = q_halo = q_small = q_share = None
     conv_scratch = (
@@ -1353,7 +1353,7 @@
         up_keep, up_send = kernel_call(
             functools.partial(emit_kernel, ffn_axis, up_bits),
             (shaped(ffn_half, bf16), shaped(ffn_half, bf16)),
-            chain, Held(grad_up),
+            chain, Free(grad_up),
             name="up_blocks",
         )
         up = Shares(up_keep, up_send, up_bits, ffn_axis)
@@ -1420,7 +1420,7 @@
         da, da_edge, head_rows = kernel_call(
             input_back_kernel,
             (shaped((rows, model), f32), shaped((SUB, model), f32), shaped((SUB, model), f32)),
-            chain, gp, gp_halo, Held(gq), Held(q_halo), Free(d_gate_raw),
+            chain, gp, gp_halo, Free(gq), Free(q_halo), Free(d_gate_raw),
             Free(w_query), Free(w_key), Free(w_value), Free(w_gate), Free(w_beta8), Free(block_input),
             gain_row, Free(a_before), Free(sums_a),
             name="input_back",

time: 176 us -> 169 us (0.960)
  Pallas kernels: 57.8 us -> 53.1 us
  waiting for transfers between devices: 66.9 us -> 63.5 us
    pallas_call x45, Pallas kernels: 57.8 us -> 53.1 us  [kernel_call(): pl.pallas_call(run, out_shape=tuple(results), in_specs=specs, out_specs=t...]
    ppermute x38, waiting for transfers between devices: 60.7 us -> 57.1 us  [swap(): return lax.ppermute(value, axis, [(s, s ^ bit) for s in range(count)])]
  transfers between devices with their start and end apart: 40 -> 40, of which waited for: 20 -> 24; matrix products, arithmetic and copies ran while one was open for 0% -> 0% of each run, Pallas kernels for 24% -> 22%
where the time goes in v4:
time: 169 us; the launch traced here: 168 us
  waiting for transfers between devices  63.5 us (38%)
  Pallas kernels  53.1 us (31%)
  starting transfers between devices  50.1 us (30%)
    ppermute x38, waiting for transfers between devices, swap(): return lax.ppermute(value, axis, [(s, s ^ bit) for s in range(count)])  57.1 us
    pallas_call x45, Pallas kernels, kernel_call(): pl.pallas_call(run, out_shape=tuple(results), in_specs=specs, out_specs=t...  53.1 us
    ppermute x38, starting transfers between devices, swap(): return lax.ppermute(value, axis, [(s, s ^ bit) for s in range(count)])  45.4 us
    ppermute x2, waiting for transfers between devices, shift(): lax.ppermute(value, axis, [(s, s + step) for s in range(count) if 0 <= s...  6.41 us
    ppermute x2, starting transfers between devices, shift(): lax.ppermute(value, axis, [(s, s + step) for s in range(count) if 0 <= s...  4.71 us
  transfers between devices with their start and end apart: 40, of which 24 were waited for; matrix products, arithmetic and copies ran while one was open for 0% of the time, Pallas kernels for 22%

profile of v4, /device:TPU:0, one launch (start us, length us, event | category | flops | bytes accessed | tf_op | source)
XLA Modules:
  0.0 168.2 jit_solution(7447235251118426791)
XLA Ops:
  0.6 4.2 %project.1 = (bf16[384,768]{1,0:T(8,128)(2,1)S(1)}, f32[384,256]{1,0:T(8,128)S(1)}, f32[384,128]{1,0:T(8,128)S(1)}, f32[8,1920]{1,0:T(8,128)S(1)}, bf16[384,1024...) custom-call(bf16[384,1024]{1,0:T(8,128)(2,1)} %refs_2_.5, ...), custom_call_target="tpu_custom_call" | custom-call | tf_op jit(solution)/shard_map/project/pallas_call | solution.py:146
  4.8 3.0 %collective-permute-start.7 = (bf16[256,1024]{1,0:T(8,128)(2,1)}, bf16[256,1024]{1,0:T(8,128)(2,1)S(1)}, u32[]{:S(2)}, u32[]{:S(2)}) collective-permute-start(bf16[256,1024]{1,0:T(8,128)(2,1)} %get-tuple-element.198.refs_10_), channel_id=1, source_target_pairs={{0,2},{1,3},{2,0},{3,1},{4,6},{5,7},{6,4},{7,5},{8,10},{9,11},{10,... | collective-permute-start | bytes 1572872 | tf_op jit(solution)/shard_map/ppermute | solution.py:185
  7.8 3.4 %collective-permute-start = (f32[8,1920]{1,0:T(8,128)S(1)}, f32[8,1920]{1,0:T(8,128)S(1)}, u32[]{:S(2)}, u32[]{:S(2)}) collective-permute-start(f32[8,1920]{1,0:T(8,128)S(1)} %get-tuple-element.178), channel_id=1, source_target_pairs={{0,4},{4,8},{8,12},{12,16},{16,20},{20,24},{24,28},{1,5},{5,9},{9,... | collective-permute-start | bytes 184328 | tf_op jit(solution)/shard_map/ppermute | solution.py:190
  13.1 4.6 %delta.1 = (bf16[512,128]{1,0:T(8,128)(2,1)S(1)}, bf16[400,1024]{1,0:T(8,128)(2,1)S(1)}, bf16[400,2560]{1,0:T(8,128)(2,1)S(1)}, f32[392,384]{1,0:T(8,128)S(1)}, ...) custom-call(bf16[384,768]{1,0:T(8,128)(2,1)S(1)} %get-tuple-element.177.refs_0_, ...), custom_call_target="tpu_custom_call" | custom-call | tf_op jit(solution)/shard_map/delta/pallas_call | solution.py:146
  17.7 2.4 %collective-permute-start.1 = (bf16[512,128]{1,0:T(8,128)(2,1)S(1)}, bf16[512,128]{1,0:T(8,128)(2,1)S(1)}, u32[]{:S(2)}, u32[]{:S(2)}) collective-permute-start(bf16[512,128]{1,0:T(8,128)(2,1)S(1)} %get-tuple-element.182.refs_0_.refs_2_.refs_3_), channel_id=1, source_target_pairs={{0,4},{4,0},{8,12},{12,8},{16,20},{20,16},{24,28},{28,24},{1,5},{5... | collective-permute-start | bytes 393224 | tf_op jit(solution)/shard_map/ppermute | solution.py:185
  23.3 3.0 %collective-permute-start.2 = (bf16[512,128]{1,0:T(8,128)(2,1)S(1)}, bf16[512,128]{1,0:T(8,128)(2,1)S(1)}, u32[]{:S(2)}, u32[]{:S(2)}) collective-permute-start(bf16[512,128]{1,0:T(8,128)(2,1)S(1)} %get-tuple-element.189.refs_0_), channel_id=1, source_target_pairs={{0,8},{4,12},{8,0},{12,4},{16,24},{20,28},{24,16},{28,20},{1,9},{5... | collective-permute-start | bytes 393224 | tf_op jit(solution)/shard_map/ppermute | solution.py:185
  26.9 2.4 %collective-permute-done.2.refs_1_ = bf16[512,128]{1,0:T(8,128)(2,1)S(1)} collective-permute-done((bf16[512,128]{1,0:T(8,128)(2,1)S(1)}, bf16[512,128]{1,0:T(8,128)(2,1)S(1)}, u32[]{:S(2)}, u32[]{:S(2)}) %collective-permute-start.2) | collective-permute-done | bytes 131104 | tf_op jit(solution)/shard_map/ppermute | solution.py:185
  29.6 3.8 %collective-permute-start.3 = (bf16[256,128]{1,0:T(8,128)(2,1)S(1)}, bf16[256,128]{1,0:T(8,128)(2,1)S(1)}, u32[]{:S(2)}, u32[]{:S(2)}) collective-permute-start(bf16[256,128]{1,0:T(8,128)(2,1)S(1)} %get-tuple-element.194), channel_id=1, source_target_pairs={{0,16},{4,20},{8,24},{12,28},{16,0},{20,4},{24,8},{28,12},{1,17},{... | collective-permute-start | bytes 196616 | tf_op jit(solution)/shard_map/ppermute | solution.py:185
  37.2 5.1 %collective-permute-done.4.refs_7_ = bf16[384,256]{1,0:T(8,128)(2,1)S(1)} collective-permute-done((bf16[384,256]{1,0:T(8,128)(2,1)S(1)}, bf16[384,256]{1,0:T(8,128)(2,1)S(1)}, u32[]{:S(2)}, u32[]{:S(2)}) %collective-permute-start.4) | collective-permute-done | bytes 196640 | tf_op jit(solution)/shard_map/ppermute | solution.py:185
  43.9 9.7 %ffn.1 = (bf16[192,1024]{1,0:T(8,128)(2,1)S(1)}, bf16[704,512]{1,0:T(8,128)(2,1)S(1)}, bf16[704,512]{1,0:T(8,128)(2,1)S(1)}, f32[384,1024]{1,0:T(8,128)}, bf16[3...) custom-call(bf16[384,1024]{1,0:T(8,128)(2,1)S(1)} %copy-done, ...), custom_call_target="tpu_custom_call" | custom-call | tf_op jit(solution)/shard_map/ffn/pallas_call | solution.py:146
  58.9 8.8 %collective-permute-done.11.refs_1_ = bf16[192,1024]{1,0:T(8,128)(2,1)S(1)} collective-permute-done((bf16[192,1024]{1,0:T(8,128)(2,1)S(1)}, bf16[192,1024]{1,0:T(8,128)(2,1)S(1)}, u32[]{:S(2)}, u32[]{:S(2)}) %collective-permute-start.11) | collective-permute-done | bytes 393248 | tf_op jit(solution)/shard_map/ppermute | solution.py:185
  71.6 2.6 %out_part.1 = (bf16[192,1024]{1,0:T(8,128)(2,1)S(1)}, bf16[192,1024]{1,0:T(8,128)(2,1)S(1)}, f32[8,128]{1,0:T(8,128)S(1)}) custom-call(bf16[384,704]{1,0:T(8,128)(2,1)} %get-tuple-element.204.refs_0_, bf16[704,1024]{1,0:T(8,128)(2,1)} %refs_1_.5, f32[8,128]{1,0:T(8,128)S(1)} %get-tuple-element.215.refs_2_), custom_call_target="tpu_custom_call" | custom-call | tf_op jit(solution)/shard_map/out_part/pallas_call | solution.py:146
  78.7 2.4 %collective-permute-done.17.refs_2_ = bf16[256,128]{1,0:T(8,128)(2,1)S(1)} collective-permute-done((bf16[256,128]{1,0:T(8,128)(2,1)S(1)}, bf16[256,128]{1,0:T(8,128)(2,1)S(1)}, u32[]{:S(2)}, u32[]{:S(2)}) %collective-permute-start.17) | collective-permute-done | bytes 65568 | tf_op jit(solution)/shard_map/ppermute | solution.py:185
  83.7 3.3 %collective-permute-start.21 = (bf16[704,256]{1,0:T(8,128)(2,1)S(1)}, bf16[704,256]{1,0:T(8,128)(2,1)S(1)}, u32[]{:S(2)}, u32[]{:S(2)}) collective-permute-start(bf16[704,256]{1,0:T(8,128)(2,1)S(1)} %get-tuple-element.252), channel_id=1, source_target_pairs={{0,16},{4,20},{8,24},{12,28},{16,0},{20,4},{24,8},{28,12},{1,17},{... | collective-permute-start | bytes 1081352 | tf_op jit(solution)/shard_map/ppermute | solution.py:185
  87.0 3.0 %collective-permute-done.16.refs_1_ = bf16[704,256]{1,0:T(8,128)(2,1)S(1)} collective-permute-done((bf16[704,256]{1,0:T(8,128)(2,1)S(1)}, bf16[704,256]{1,0:T(8,128)(2,1)S(1)}, u32[]{:S(2)}, u32[]{:S(2)}) %collective-permute-start.16) | collective-permute-done | bytes 360480 | tf_op jit(solution)/shard_map/ppermute | solution.py:185
  91.6 3.2 %delta_query.1 = (bf16[384,512]{1,0:T(8,128)(2,1)S(1)}, f32[384,256]{1,0:T(8,128)S(1)}, f32[384,256]{1,0:T(8,128)}, f32[8,256]{1,0:T(8,128)}, f32[8,256]{1,0:T(8,128)}, /*index=5*/f32[8,128]{1,0:T(8,128)S(1)}) custom-call(f32[3,4,256]{2,1,0:T(4,128)S(1)} %copy-done.29, bf16[400,2560]{1,0:T(8,128)(2,1)S(1)} %copy-done.1, f32[392,384]{1,0:T(8,128)S(1)} %copy-done.7, ...), custom_call_target="tpu_custom_call" | custom-call | tf_op jit(solution)/shard_map/delta_query/pallas_call | solution.py:146
  103.3 5.3 %delta_back.1 = (f32[384,640]{1,0:T(8,128)S(1)}, f32[8,512]{1,0:T(8,128)S(1)}, f32[16,256]{1,0:T(8,128)}, f32[8,128]{1,0:T(8,128)S(1)}) custom-call(f32[3,4,256]{2,1,0:T(4,128)S(1)} %copy-done.29, bf16[400,2560]{1,0:T(8,128)(2,1)S(1)} %copy-done.1, f32[392,384]{1,0:T(8,128)S(1)} %copy-done.7, bf16[400,512]{1,0:T(8,128)(2,1)S(1)} %copy-done.14, ...), custom_call_target="tpu_custom_call" | custom-call | tf_op jit(solution)/shard_map/delta_back/pallas_call | solution.py:146
  112.0 4.6 %collective-permute-done.22.refs_1_ = f32[8,1024]{1,0:T(8,128)S(1)} collective-permute-done((f32[8,1024]{1,0:T(8,128)S(1)}, f32[8,1024]{1,0:T(8,128)S(1)}, u32[]{:S(2)}, u32[]{:S(2)}) %collective-permute-start.22) | collective-permute-done | bytes 32800 | tf_op jit(solution)/shard_map/ppermute | solution.py:190
  119.3 2.7 %collective-permute-done.29.refs_1_ = f32[8,1024]{1,0:T(8,128)S(1)} collective-permute-done((f32[8,1024]{1,0:T(8,128)S(1)}, f32[8,1024]{1,0:T(8,128)S(1)}, u32[]{:S(2)}, u32[]{:S(2)}) %collective-permute-start.29) | collective-permute-done | bytes 32800 | tf_op jit(solution)/shard_map/ppermute | solution.py:185
  134.6 8.0 %collective-permute-done.34.refs_1_ = bf16[704,128]{1,0:T(8,128)(2,1)S(1)} collective-permute-done((bf16[704,128]{1,0:T(8,128)(2,1)S(1)}, bf16[704,128]{1,0:T(8,128)(2,1)S(1)}, u32[]{:S(2)}, u32[]{:S(2)}) %collective-permute-start.34) | collective-permute-done | bytes 180256 | tf_op jit(solution)/shard_map/ppermute | solution.py:185
  143.4 3.9 %collective-permute-start.38 = (bf16[272,512]{1,0:T(8,128)(2,1)S(1)}, bf16[272,512]{1,0:T(8,128)(2,1)S(1)}, u32[]{:S(2)}, u32[]{:S(2)}) collective-permute-start(bf16[272,512]{1,0:T(8,128)(2,1)S(1)} %get-tuple-element.315), channel_id=1, source_target_pairs={{0,8},{4,12},{8,0},{12,4},{16,24},{20,28},{24,16},{28,20},{1,9},{5... | collective-permute-start | bytes 835592 | tf_op jit(solution)/shard_map/ppermute | solution.py:185
  149.8 2.5 %collective-permute-start.37 = (bf16[704,128]{1,0:T(8,128)(2,1)S(1)}, bf16[704,128]{1,0:T(8,128)(2,1)S(1)}, u32[]{:S(2)}, u32[]{:S(2)}) collective-permute-start(bf16[704,128]{1,0:T(8,128)(2,1)S(1)} %get-tuple-element.313), channel_id=1, source_target_pairs={{0,4},{4,0},{8,12},{12,8},{16,20},{20,16},{24,28},{28,24},{1,5},{5... | collective-permute-start | bytes 540680 | tf_op jit(solution)/shard_map/ppermute | solution.py:185
  152.6 2.4 %collective-permute-start.39 = (bf16[144,512]{1,0:T(8,128)(2,1)S(1)}, bf16[144,512]{1,0:T(8,128)(2,1)S(1)}, u32[]{:S(2)}, u32[]{:S(2)}) collective-permute-start(bf16[144,512]{1,0:T(8,128)(2,1)S(1)} %get-tuple-element.322), channel_id=1, source_target_pairs={{0,16},{4,20},{8,24},{12,28},{16,0},{20,4},{24,8},{28,12},{1,17},{... | collective-permute-start | bytes 442376 | tf_op jit(solution)/shard_map/ppermute | solution.py:185
  157.9 6.6 %collective-permute-done.36.refs_1_ = bf16[128,768]{1,0:T(8,128)(2,1)S(1)} collective-permute-done((bf16[128,768]{1,0:T(8,128)(2,1)S(1)}, bf16[128,768]{1,0:T(8,128)(2,1)S(1)}, u32[]{:S(2)}, u32[]{:S(2)}) %collective-permute-start.36) | collective-permute-done | bytes 196640 | tf_op jit(solution)/shard_map/ppermute | solution.py:185
  (173 shorter events, 65.9 us)
Async XLA Ops:
  4.8 21.5 %collective-permute-start.7 = (bf16[256,1024]{1,0:T(8,128)(2,1)}, bf16[256,1024]{1,0:T(8,128)(2,1)S(1)}, u32[]{:S(2)}, u32[]{:S(2)}) collective-permute-start(bf16[256,1024]{1,0:T(8,128)(2,1)} %get-tuple-element.198.refs_10_), channel_id=1, source_target_pairs={{0,2},{1,3},{2,0},{3,1},{4,6},{5,7},{6,4},{7,5},{8,10},{9,11},{10,... | collective-permute-start | bytes 1572872 | tf_op jit(solution)/shard_map/ppermute | solution.py:185
  26.4 17.0 %collective-permute-start.8 = (bf16[256,1024]{1,0:T(8,128)(2,1)S(1)}, bf16[256,1024]{1,0:T(8,128)(2,1)S(1)}, u32[]{:S(2)}, u32[]{:S(2)}) collective-permute-start(bf16[256,1024]{1,0:T(8,128)(2,1)S(1)} %copy-done.25), channel_id=1, source_target_pairs={{0,1},{1,0},{2,3},{3,2},{4,5},{5,4},{6,7},{7,6},{8,9},{9,8},{10,11... | collective-permute-start | bytes 1572872 | tf_op jit(solution)/shard_map/ppermute | solution.py:185
  26.4 17.4 %collective-permute-start.9 = (bf16[256,1024]{1,0:T(8,128)(2,1)S(1)}, bf16[256,1024]{1,0:T(8,128)(2,1)S(1)}, u32[]{:S(2)}, u32[]{:S(2)}) collective-permute-start(bf16[256,1024]{1,0:T(8,128)(2,1)S(1)} %collective-permute-done.7.refs_11_), channel_id=1, source_target_pairs={{0,1},{1,0},{2,3},{3,2},{4,5},{5,4},{6,7},{7,6},{8,9},{9,8},{10,11... | collective-permute-start | bytes 1572872 | tf_op jit(solution)/shard_map/ppermute | solution.py:185
  56.4 11.2 %collective-permute-start.11 = (bf16[192,1024]{1,0:T(8,128)(2,1)S(1)}, bf16[192,1024]{1,0:T(8,128)(2,1)S(1)}, u32[]{:S(2)}, u32[]{:S(2)}) collective-permute-start(bf16[192,1024]{1,0:T(8,128)(2,1)S(1)} %get-tuple-element.208.refs_0_), channel_id=1, source_target_pairs={{0,2},{1,3},{2,0},{3,1},{4,6},{5,7},{6,4},{7,5},{8,10},{9,11},{10,... | collective-permute-start | bytes 1179656 | tf_op jit(solution)/shard_map/ppermute | solution.py:185
  57.1 17.9 %collective-permute-start.15 = (bf16[704,512]{1,0:T(8,128)(2,1)S(1)}, bf16[704,512]{1,0:T(8,128)(2,1)S(1)}, u32[]{:S(2)}, u32[]{:S(2)}) collective-permute-start(bf16[704,512]{1,0:T(8,128)(2,1)S(1)} %get-tuple-element.221), channel_id=1, source_target_pairs={{0,8},{4,12},{8,0},{12,4},{16,24},{20,28},{24,16},{28,20},{1,9},{5... | collective-permute-start | bytes 2162696 | tf_op jit(solution)/shard_map/ppermute | solution.py:185
  58.3 17.6 %collective-permute-start.14 = (bf16[704,512]{1,0:T(8,128)(2,1)S(1)}, bf16[704,512]{1,0:T(8,128)(2,1)S(1)}, u32[]{:S(2)}, u32[]{:S(2)}) collective-permute-start(bf16[704,512]{1,0:T(8,128)(2,1)S(1)} %get-tuple-element.219), channel_id=1, source_target_pairs={{0,4},{4,0},{8,12},{12,8},{16,20},{20,16},{24,28},{28,24},{1,5},{5... | collective-permute-start | bytes 2162696 | tf_op jit(solution)/shard_map/ppermute | solution.py:185
  74.2 15.8 %collective-permute-start.13 = (bf16[192,1024]{1,0:T(8,128)(2,1)S(1)}, bf16[192,1024]{1,0:T(8,128)(2,1)S(1)}, u32[]{:S(2)}, u32[]{:S(2)}) collective-permute-start(bf16[192,1024]{1,0:T(8,128)(2,1)S(1)} %get-tuple-element.217), channel_id=1, source_target_pairs={{0,1},{1,0},{2,3},{3,2},{4,5},{5,4},{6,7},{7,6},{8,9},{9,8},{10,11... | collective-permute-start | bytes 1179656 | tf_op jit(solution)/shard_map/ppermute | solution.py:185
  76.0 13.9 %collective-permute-start.16 = (bf16[704,256]{1,0:T(8,128)(2,1)S(1)}, bf16[704,256]{1,0:T(8,128)(2,1)S(1)}, u32[]{:S(2)}, u32[]{:S(2)}) collective-permute-start(bf16[704,256]{1,0:T(8,128)(2,1)S(1)} %get-tuple-element.225), channel_id=1, source_target_pairs={{0,8},{4,12},{8,0},{12,4},{16,24},{20,28},{24,16},{28,20},{1,9},{5... | collective-permute-start | bytes 1081352 | tf_op jit(solution)/shard_map/ppermute | solution.py:185
  81.8 35.1 %collective-permute-start.27 = (bf16[704,512]{1,0:T(8,128)(2,1)S(1)}, bf16[704,512]{1,0:T(8,128)(2,1)S(1)}, u32[]{:S(2)}, u32[]{:S(2)}) collective-permute-start(bf16[704,512]{1,0:T(8,128)(2,1)S(1)} %get-tuple-element.279), channel_id=1, source_target_pairs={{0,4},{4,0},{8,12},{12,8},{16,20},{20,16},{24,28},{28,24},{1,5},{5... | collective-permute-start | bytes 2162696 | tf_op jit(solution)/shard_map/ppermute | solution.py:185
  83.7 18.6 %collective-permute-start.21 = (bf16[704,256]{1,0:T(8,128)(2,1)S(1)}, bf16[704,256]{1,0:T(8,128)(2,1)S(1)}, u32[]{:S(2)}, u32[]{:S(2)}) collective-permute-start(bf16[704,256]{1,0:T(8,128)(2,1)S(1)} %get-tuple-element.252), channel_id=1, source_target_pairs={{0,16},{4,20},{8,24},{12,28},{16,0},{20,4},{24,8},{28,12},{1,17},{... | collective-permute-start | bytes 1081352 | tf_op jit(solution)/shard_map/ppermute | solution.py:185
  97.1 30.9 %collective-permute-start.26 = (bf16[512,768]{1,0:T(8,128)(2,1)S(1)}, bf16[512,768]{1,0:T(8,128)(2,1)S(1)}, u32[]{:S(2)}, u32[]{:S(2)}) collective-permute-start(bf16[512,768]{1,0:T(8,128)(2,1)S(1)} %get-tuple-element.277), channel_id=1, source_target_pairs={{0,4},{4,0},{8,12},{12,8},{16,20},{20,16},{24,28},{28,24},{1,5},{5... | collective-permute-start | bytes 2359304 | tf_op jit(solution)/shard_map/ppermute | solution.py:185
  97.2 19.6 %collective-permute-start.18 = (bf16[192,1024]{1,0:T(8,128)(2,1)S(1)}, bf16[192,1024]{1,0:T(8,128)(2,1)S(1)}, u32[]{:S(2)}, u32[]{:S(2)}) collective-permute-start(bf16[192,1024]{1,0:T(8,128)(2,1)S(1)} %get-tuple-element.238.refs_0_), channel_id=1, source_target_pairs={{0,2},{1,3},{2,0},{3,1},{4,6},{5,7},{6,4},{7,5},{8,10},{9,11},{10,... | collective-permute-start | bytes 1179656 | tf_op jit(solution)/shard_map/ppermute | solution.py:185
  116.7 12.4 %collective-permute-start.25 = (bf16[192,1024]{1,0:T(8,128)(2,1)S(1)}, bf16[192,1024]{1,0:T(8,128)(2,1)S(1)}, u32[]{:S(2)}, u32[]{:S(2)}) collective-permute-start(bf16[192,1024]{1,0:T(8,128)(2,1)S(1)} %get-tuple-element.275), channel_id=1, source_target_pairs={{0,1},{1,0},{2,3},{3,2},{4,5},{5,4},{6,7},{7,6},{8,9},{9,8},{10,11... | collective-permute-start | bytes 1179656 | tf_op jit(solution)/shard_map/ppermute | solution.py:185
  117.0 10.9 %collective-permute-start.28 = (bf16[704,256]{1,0:T(8,128)(2,1)S(1)}, bf16[704,256]{1,0:T(8,128)(2,1)S(1)}, u32[]{:S(2)}, u32[]{:S(2)}) collective-permute-start(bf16[704,256]{1,0:T(8,128)(2,1)S(1)} %get-tuple-element.282), channel_id=1, source_target_pairs={{0,8},{4,12},{8,0},{12,4},{16,24},{20,28},{24,16},{28,20},{1,9},{5... | collective-permute-start | bytes 1081352 | tf_op jit(solution)/shard_map/ppermute | solution.py:185
  119.3 13.3 %collective-permute-start.24 = (bf16[192,1024]{1,0:T(8,128)(2,1)S(1)}, bf16[192,1024]{1,0:T(8,128)(2,1)S(1)}, u32[]{:S(2)}, u32[]{:S(2)}) collective-permute-start(bf16[192,1024]{1,0:T(8,128)(2,1)S(1)} %get-tuple-element.273.refs_0_), channel_id=1, source_target_pairs={{0,1},{1,0},{2,3},{3,2},{4,5},{5,4},{6,7},{7,6},{8,9},{9,8},{10,11... | collective-permute-start | bytes 1179656 | tf_op jit(solution)/shard_map/ppermute | solution.py:185
  123.9 19.4 %collective-permute-start.33 = (bf16[528,512]{1,0:T(8,128)(2,1)S(1)}, bf16[528,512]{1,0:T(8,128)(2,1)S(1)}, u32[]{:S(2)}, u32[]{:S(2)}) collective-permute-start(bf16[528,512]{1,0:T(8,128)(2,1)S(1)} %get-tuple-element.300), channel_id=1, source_target_pairs={{0,4},{4,0},{8,12},{12,8},{16,20},{20,16},{24,28},{28,24},{1,5},{5... | collective-permute-start | bytes 1622024 | tf_op jit(solution)/shard_map/ppermute | solution.py:185
  128.1 19.2 %collective-permute-start.32 = (bf16[256,768]{1,0:T(8,128)(2,1)S(1)}, bf16[256,768]{1,0:T(8,128)(2,1)S(1)}, u32[]{:S(2)}, u32[]{:S(2)}) collective-permute-start(bf16[256,768]{1,0:T(8,128)(2,1)S(1)} %get-tuple-element.298), channel_id=1, source_target_pairs={{0,8},{4,12},{8,0},{12,4},{16,24},{20,28},{24,16},{28,20},{1,9},{5... | collective-permute-start | bytes 1179656 | tf_op jit(solution)/shard_map/ppermute | solution.py:185
  129.2 19.1 %collective-permute-start.30 = (bf16[192,1024]{1,0:T(8,128)(2,1)S(1)}, bf16[192,1024]{1,0:T(8,128)(2,1)S(1)}, u32[]{:S(2)}, u32[]{:S(2)}) collective-permute-start(bf16[192,1024]{1,0:T(8,128)(2,1)S(1)} %get-tuple-element.294.refs_0_), channel_id=1, source_target_pairs={{0,2},{1,3},{2,0},{3,1},{4,6},{5,7},{6,4},{7,5},{8,10},{9,11},{10,... | collective-permute-start | bytes 1179656 | tf_op jit(solution)/shard_map/ppermute | solution.py:185
  130.5 12.1 %collective-permute-start.34 = (bf16[704,128]{1,0:T(8,128)(2,1)S(1)}, bf16[704,128]{1,0:T(8,128)(2,1)S(1)}, u32[]{:S(2)}, u32[]{:S(2)}) collective-permute-start(bf16[704,128]{1,0:T(8,128)(2,1)S(1)} %get-tuple-element.302), channel_id=1, source_target_pairs={{0,16},{4,20},{8,24},{12,28},{16,0},{20,4},{24,8},{28,12},{1,17},{... | collective-permute-start | bytes 540680 | tf_op jit(solution)/shard_map/ppermute | solution.py:185
  132.6 15.0 %collective-permute-start.31 = (bf16[704,128]{1,0:T(8,128)(2,1)S(1)}, bf16[704,128]{1,0:T(8,128)(2,1)S(1)}, u32[]{:S(2)}, u32[]{:S(2)}) collective-permute-start(bf16[704,128]{1,0:T(8,128)(2,1)S(1)} %get-tuple-element.296), channel_id=1, source_target_pairs={{0,16},{4,20},{8,24},{12,28},{16,0},{20,4},{24,8},{28,12},{1,17},{... | collective-permute-start | bytes 540680 | tf_op jit(solution)/shard_map/ppermute | solution.py:185
  143.4 9.1 %collective-permute-start.38 = (bf16[272,512]{1,0:T(8,128)(2,1)S(1)}, bf16[272,512]{1,0:T(8,128)(2,1)S(1)}, u32[]{:S(2)}, u32[]{:S(2)}) collective-permute-start(bf16[272,512]{1,0:T(8,128)(2,1)S(1)} %get-tuple-element.315), channel_id=1, source_target_pairs={{0,8},{4,12},{8,0},{12,4},{16,24},{20,28},{24,16},{28,20},{1,9},{5... | collective-permute-start | bytes 835592 | tf_op jit(solution)/shard_map/ppermute | solution.py:185
  148.5 16.9 %collective-permute-start.35 = (bf16[192,1024]{1,0:T(8,128)(2,1)S(1)}, bf16[192,1024]{1,0:T(8,128)(2,1)S(1)}, u32[]{:S(2)}, u32[]{:S(2)}) collective-permute-start(bf16[192,1024]{1,0:T(8,128)(2,1)S(1)} %get-tuple-element.308.refs_0_), channel_id=1, source_target_pairs={{0,1},{1,0},{2,3},{3,2},{4,5},{5,4},{6,7},{7,6},{8,9},{9,8},{10,11... | collective-permute-start | bytes 1179656 | tf_op jit(solution)/shard_map/ppermute | solution.py:185
  148.5 16.0 %collective-permute-start.36 = (bf16[128,768]{1,0:T(8,128)(2,1)S(1)}, bf16[128,768]{1,0:T(8,128)(2,1)S(1)}, u32[]{:S(2)}, u32[]{:S(2)}) collective-permute-start(bf16[128,768]{1,0:T(8,128)(2,1)S(1)} %get-tuple-element.311), channel_id=1, source_target_pairs={{0,16},{4,20},{8,24},{12,28},{16,0},{20,4},{24,8},{28,12},{1,17},{... | collective-permute-start | bytes 589832 | tf_op jit(solution)/shard_map/ppermute | solution.py:185
  152.6 14.9 %collective-permute-start.39 = (bf16[144,512]{1,0:T(8,128)(2,1)S(1)}, bf16[144,512]{1,0:T(8,128)(2,1)S(1)}, u32[]{:S(2)}, u32[]{:S(2)}) collective-permute-start(bf16[144,512]{1,0:T(8,128)(2,1)S(1)} %get-tuple-element.322), channel_id=1, source_target_pairs={{0,16},{4,20},{8,24},{12,28},{16,0},{20,4},{24,8},{28,12},{1,17},{... | collective-permute-start | bytes 442376 | tf_op jit(solution)/shard_map/ppermute | solution.py:185
  (52 other events, 490.0 us)

commit v5 on v4

--- a/solution.py
+++ b/solution.py
@@ -13,7 +13,7 @@
 LANES = 128
 SUB = 8
 Q_SCALE = HEAD_DIM ** (-0.5)
-VMEM_SLACK = 14 * 1024 * 1024
+VMEM_SLACK = 7 * 1024 * 1024
 
 ORDER = (
     "db_core",
@@ -34,8 +34,8 @@
     "delta_back",
     "input_back",
     "rows_core",
+    "out_far",
     "input_split",
-    "out_far",
     "up_one",
     "rows_far",
     "project_grads",

time: 169 us -> 168 us (level)
  transfers between devices with their start and end apart: 40 -> 40, of which waited for: 24 -> 23; matrix products, arithmetic and copies ran while one was open for 0% -> 0% of each run, Pallas kernels for 22% -> 22%
where the time goes in v5:
time: 168 us
  waiting for transfers between devices  63.2 us (38%)
  Pallas kernels  53.1 us (32%)
  starting transfers between devices  49.9 us (30%)
    ppermute x38, waiting for transfers between devices, swap(): return lax.ppermute(value, axis, [(s, s ^ bit) for s in range(count)])  57 us
    pallas_call x45, Pallas kernels, kernel_call(): pl.pallas_call(run, out_shape=tuple(results), in_specs=specs, out_specs=t...  53.1 us
    ppermute x38, starting transfers between devices, swap(): return lax.ppermute(value, axis, [(s, s ^ bit) for s in range(count)])  45.2 us
    ppermute x2, waiting for transfers between devices, shift(): lax.ppermute(value, axis, [(s, s + step) for s in range(count) if 0 <= s...  6.22 us
    ppermute x2, starting transfers between devices, shift(): lax.ppermute(value, axis, [(s, s + step) for s in range(count) if 0 <= s...  4.71 us
  transfers between devices with their start and end apart: 40, of which 23 were waited for; matrix products, arithmetic and copies ran while one was open for 0% of the time, Pallas kernels for 22%

profile of v5, /device:TPU:0, one launch (start us, length us, event | category | flops | bytes accessed | tf_op | source)
XLA Modules:
  0.0 167.7 jit_solution(864347189685434175)
XLA Ops:
  0.6 4.2 %project.1 = (bf16[384,768]{1,0:T(8,128)(2,1)S(1)}, f32[384,256]{1,0:T(8,128)S(1)}, f32[384,128]{1,0:T(8,128)S(1)}, f32[8,1920]{1,0:T(8,128)S(1)}, bf16[384,1024...) custom-call(bf16[384,1024]{1,0:T(8,128)(2,1)} %refs_2_.5, ...), custom_call_target="tpu_custom_call" | custom-call | tf_op jit(solution)/shard_map/project/pallas_call | solution.py:146
  4.8 3.0 %collective-permute-start.7 = (bf16[256,1024]{1,0:T(8,128)(2,1)}, bf16[256,1024]{1,0:T(8,128)(2,1)S(1)}, u32[]{:S(2)}, u32[]{:S(2)}) collective-permute-start(bf16[256,1024]{1,0:T(8,128)(2,1)} %get-tuple-element.198.refs_10_), channel_id=1, source_target_pairs={{0,2},{1,3},{2,0},{3,1},{4,6},{5,7},{6,4},{7,5},{8,10},{9,11},{10,... | collective-permute-start | bytes 1572872 | tf_op jit(solution)/shard_map/ppermute | solution.py:185
  7.8 3.4 %collective-permute-start = (f32[8,1920]{1,0:T(8,128)S(1)}, f32[8,1920]{1,0:T(8,128)S(1)}, u32[]{:S(2)}, u32[]{:S(2)}) collective-permute-start(f32[8,1920]{1,0:T(8,128)S(1)} %get-tuple-element.178), channel_id=1, source_target_pairs={{0,4},{4,8},{8,12},{12,16},{16,20},{20,24},{24,28},{1,5},{5,9},{9,... | collective-permute-start | bytes 184328 | tf_op jit(solution)/shard_map/ppermute | solution.py:190
  13.1 4.6 %delta.1 = (bf16[512,128]{1,0:T(8,128)(2,1)S(1)}, bf16[400,1024]{1,0:T(8,128)(2,1)S(1)}, bf16[400,2560]{1,0:T(8,128)(2,1)S(1)}, f32[392,384]{1,0:T(8,128)S(1)}, ...) custom-call(bf16[384,768]{1,0:T(8,128)(2,1)S(1)} %get-tuple-element.177.refs_0_, ...), custom_call_target="tpu_custom_call" | custom-call | tf_op jit(solution)/shard_map/delta/pallas_call | solution.py:146
  17.7 2.4 %collective-permute-start.1 = (bf16[512,128]{1,0:T(8,128)(2,1)S(1)}, bf16[512,128]{1,0:T(8,128)(2,1)S(1)}, u32[]{:S(2)}, u32[]{:S(2)}) collective-permute-start(bf16[512,128]{1,0:T(8,128)(2,1)S(1)} %get-tuple-element.182.refs_0_.refs_2_.refs_3_), channel_id=1, source_target_pairs={{0,4},{4,0},{8,12},{12,8},{16,20},{20,16},{24,28},{28,24},{1,5},{5... | collective-permute-start | bytes 393224 | tf_op jit(solution)/shard_map/ppermute | solution.py:185
  23.3 3.0 %collective-permute-start.2 = (bf16[512,128]{1,0:T(8,128)(2,1)S(1)}, bf16[512,128]{1,0:T(8,128)(2,1)S(1)}, u32[]{:S(2)}, u32[]{:S(2)}) collective-permute-start(bf16[512,128]{1,0:T(8,128)(2,1)S(1)} %get-tuple-element.189.refs_0_), channel_id=1, source_target_pairs={{0,8},{4,12},{8,0},{12,4},{16,24},{20,28},{24,16},{28,20},{1,9},{5... | collective-permute-start | bytes 393224 | tf_op jit(solution)/shard_map/ppermute | solution.py:185
  26.9 2.4 %collective-permute-done.2.refs_1_ = bf16[512,128]{1,0:T(8,128)(2,1)S(1)} collective-permute-done((bf16[512,128]{1,0:T(8,128)(2,1)S(1)}, bf16[512,128]{1,0:T(8,128)(2,1)S(1)}, u32[]{:S(2)}, u32[]{:S(2)}) %collective-permute-start.2) | collective-permute-done | bytes 131104 | tf_op jit(solution)/shard_map/ppermute | solution.py:185
  29.6 3.8 %collective-permute-start.3 = (bf16[256,128]{1,0:T(8,128)(2,1)S(1)}, bf16[256,128]{1,0:T(8,128)(2,1)S(1)}, u32[]{:S(2)}, u32[]{:S(2)}) collective-permute-start(bf16[256,128]{1,0:T(8,128)(2,1)S(1)} %get-tuple-element.194), channel_id=1, source_target_pairs={{0,16},{4,20},{8,24},{12,28},{16,0},{20,4},{24,8},{28,12},{1,17},{... | collective-permute-start | bytes 196616 | tf_op jit(solution)/shard_map/ppermute | solution.py:185
  37.2 5.1 %collective-permute-done.4.refs_7_ = bf16[384,256]{1,0:T(8,128)(2,1)S(1)} collective-permute-done((bf16[384,256]{1,0:T(8,128)(2,1)S(1)}, bf16[384,256]{1,0:T(8,128)(2,1)S(1)}, u32[]{:S(2)}, u32[]{:S(2)}) %collective-permute-start.4) | collective-permute-done | bytes 196640 | tf_op jit(solution)/shard_map/ppermute | solution.py:185
  43.9 9.7 %ffn.1 = (bf16[192,1024]{1,0:T(8,128)(2,1)S(1)}, bf16[704,512]{1,0:T(8,128)(2,1)S(1)}, bf16[704,512]{1,0:T(8,128)(2,1)S(1)}, f32[384,1024]{1,0:T(8,128)}, bf16[3...) custom-call(bf16[384,1024]{1,0:T(8,128)(2,1)S(1)} %copy-done, ...), custom_call_target="tpu_custom_call" | custom-call | tf_op jit(solution)/shard_map/ffn/pallas_call | solution.py:146
  58.9 8.8 %collective-permute-done.11.refs_1_ = bf16[192,1024]{1,0:T(8,128)(2,1)S(1)} collective-permute-done((bf16[192,1024]{1,0:T(8,128)(2,1)S(1)}, bf16[192,1024]{1,0:T(8,128)(2,1)S(1)}, u32[]{:S(2)}, u32[]{:S(2)}) %collective-permute-start.11) | collective-permute-done | bytes 393248 | tf_op jit(solution)/shard_map/ppermute | solution.py:185
  71.6 2.6 %out_part.1 = (bf16[192,1024]{1,0:T(8,128)(2,1)S(1)}, bf16[192,1024]{1,0:T(8,128)(2,1)S(1)}, f32[8,128]{1,0:T(8,128)S(1)}) custom-call(bf16[384,704]{1,0:T(8,128)(2,1)} %get-tuple-element.204.refs_0_, bf16[704,1024]{1,0:T(8,128)(2,1)} %refs_1_.5, f32[8,128]{1,0:T(8,128)S(1)} %get-tuple-element.215.refs_2_), custom_call_target="tpu_custom_call" | custom-call | tf_op jit(solution)/shard_map/out_part/pallas_call | solution.py:146
  83.7 3.3 %collective-permute-start.21 = (bf16[704,256]{1,0:T(8,128)(2,1)S(1)}, bf16[704,256]{1,0:T(8,128)(2,1)S(1)}, u32[]{:S(2)}, u32[]{:S(2)}) collective-permute-start(bf16[704,256]{1,0:T(8,128)(2,1)S(1)} %get-tuple-element.252), channel_id=1, source_target_pairs={{0,16},{4,20},{8,24},{12,28},{16,0},{20,4},{24,8},{28,12},{1,17},{... | collective-permute-start | bytes 1081352 | tf_op jit(solution)/shard_map/ppermute | solution.py:185
  87.0 3.0 %collective-permute-done.16.refs_1_ = bf16[704,256]{1,0:T(8,128)(2,1)S(1)} collective-permute-done((bf16[704,256]{1,0:T(8,128)(2,1)S(1)}, bf16[704,256]{1,0:T(8,128)(2,1)S(1)}, u32[]{:S(2)}, u32[]{:S(2)}) %collective-permute-start.16) | collective-permute-done | bytes 360480 | tf_op jit(solution)/shard_map/ppermute | solution.py:185
  91.6 3.2 %delta_query.1 = (bf16[384,512]{1,0:T(8,128)(2,1)S(1)}, f32[384,256]{1,0:T(8,128)S(1)}, f32[384,256]{1,0:T(8,128)}, f32[8,256]{1,0:T(8,128)}, f32[8,256]{1,0:T(8,128)}, /*index=5*/f32[8,128]{1,0:T(8,128)S(1)}) custom-call(f32[3,4,256]{2,1,0:T(4,128)S(1)} %copy-done.29, bf16[400,2560]{1,0:T(8,128)(2,1)S(1)} %copy-done.1, f32[392,384]{1,0:T(8,128)S(1)} %copy-done.7, ...), custom_call_target="tpu_custom_call" | custom-call | tf_op jit(solution)/shard_map/delta_query/pallas_call | solution.py:146
  98.8 3.5 %collective-permute-done.21.refs_1_ = bf16[704,256]{1,0:T(8,128)(2,1)S(1)} collective-permute-done((bf16[704,256]{1,0:T(8,128)(2,1)S(1)}, bf16[704,256]{1,0:T(8,128)(2,1)S(1)}, u32[]{:S(2)}, u32[]{:S(2)}) %collective-permute-start.21) | collective-permute-done | bytes 360480 | tf_op jit(solution)/shard_map/ppermute | solution.py:185
  103.0 5.3 %delta_back.1 = (f32[384,640]{1,0:T(8,128)S(1)}, f32[8,512]{1,0:T(8,128)S(1)}, f32[16,256]{1,0:T(8,128)}, f32[8,128]{1,0:T(8,128)S(1)}) custom-call(f32[3,4,256]{2,1,0:T(4,128)S(1)} %copy-done.29, bf16[400,2560]{1,0:T(8,128)(2,1)S(1)} %copy-done.1, f32[392,384]{1,0:T(8,128)S(1)} %copy-done.7, bf16[400,512]{1,0:T(8,128)(2,1)S(1)} %copy-done.14, ...), custom_call_target="tpu_custom_call" | custom-call | tf_op jit(solution)/shard_map/delta_back/pallas_call | solution.py:146
  111.7 4.4 %collective-permute-done.24.refs_1_ = f32[8,1024]{1,0:T(8,128)S(1)} collective-permute-done((f32[8,1024]{1,0:T(8,128)S(1)}, f32[8,1024]{1,0:T(8,128)S(1)}, u32[]{:S(2)}, u32[]{:S(2)}) %collective-permute-start.24) | collective-permute-done | bytes 32800 | tf_op jit(solution)/shard_map/ppermute | solution.py:190
  118.5 2.7 %collective-permute-done.29.refs_1_ = f32[8,1024]{1,0:T(8,128)S(1)} collective-permute-done((f32[8,1024]{1,0:T(8,128)S(1)}, f32[8,1024]{1,0:T(8,128)S(1)}, u32[]{:S(2)}, u32[]{:S(2)}) %collective-permute-start.29) | collective-permute-done | bytes 32800 | tf_op jit(solution)/shard_map/ppermute | solution.py:185
  129.7 2.8 %collective-permute-start.34 = (bf16[704,128]{1,0:T(8,128)(2,1)S(1)}, bf16[704,128]{1,0:T(8,128)(2,1)S(1)}, u32[]{:S(2)}, u32[]{:S(2)}) collective-permute-start(bf16[704,128]{1,0:T(8,128)(2,1)S(1)} %get-tuple-element.302), channel_id=1, source_target_pairs={{0,16},{4,20},{8,24},{12,28},{16,0},{20,4},{24,8},{28,12},{1,17},{... | collective-permute-start | bytes 540680 | tf_op jit(solution)/shard_map/ppermute | solution.py:185
  133.8 7.9 %collective-permute-done.34.refs_1_ = bf16[704,128]{1,0:T(8,128)(2,1)S(1)} collective-permute-done((bf16[704,128]{1,0:T(8,128)(2,1)S(1)}, bf16[704,128]{1,0:T(8,128)(2,1)S(1)}, u32[]{:S(2)}, u32[]{:S(2)}) %collective-permute-start.34) | collective-permute-done | bytes 180256 | tf_op jit(solution)/shard_map/ppermute | solution.py:185
  142.6 4.5 %collective-permute-start.38 = (bf16[272,512]{1,0:T(8,128)(2,1)S(1)}, bf16[272,512]{1,0:T(8,128)(2,1)S(1)}, u32[]{:S(2)}, u32[]{:S(2)}) collective-permute-start(bf16[272,512]{1,0:T(8,128)(2,1)S(1)} %get-tuple-element.315), channel_id=1, source_target_pairs={{0,8},{4,12},{8,0},{12,4},{16,24},{20,28},{24,16},{28,20},{1,9},{5... | collective-permute-start | bytes 835592 | tf_op jit(solution)/shard_map/ppermute | solution.py:185
  148.8 3.1 %collective-permute-start.37 = (bf16[704,128]{1,0:T(8,128)(2,1)S(1)}, bf16[704,128]{1,0:T(8,128)(2,1)S(1)}, u32[]{:S(2)}, u32[]{:S(2)}) collective-permute-start(bf16[704,128]{1,0:T(8,128)(2,1)S(1)} %get-tuple-element.313), channel_id=1, source_target_pairs={{0,4},{4,0},{8,12},{12,8},{16,20},{20,16},{24,28},{28,24},{1,5},{5... | collective-permute-start | bytes 540680 | tf_op jit(solution)/shard_map/ppermute | solution.py:185
  157.5 6.6 %collective-permute-done.36.refs_1_ = bf16[128,768]{1,0:T(8,128)(2,1)S(1)} collective-permute-done((bf16[128,768]{1,0:T(8,128)(2,1)S(1)}, bf16[128,768]{1,0:T(8,128)(2,1)S(1)}, u32[]{:S(2)}, u32[]{:S(2)}) %collective-permute-start.36) | collective-permute-done | bytes 196640 | tf_op jit(solution)/shard_map/ppermute | solution.py:185
  (173 shorter events, 63.1 us)
Async XLA Ops:
  4.8 21.5 %collective-permute-start.7 = (bf16[256,1024]{1,0:T(8,128)(2,1)}, bf16[256,1024]{1,0:T(8,128)(2,1)S(1)}, u32[]{:S(2)}, u32[]{:S(2)}) collective-permute-start(bf16[256,1024]{1,0:T(8,128)(2,1)} %get-tuple-element.198.refs_10_), channel_id=1, source_target_pairs={{0,2},{1,3},{2,0},{3,1},{4,6},{5,7},{6,4},{7,5},{8,10},{9,11},{10,... | collective-permute-start | bytes 1572872 | tf_op jit(solution)/shard_map/ppermute | solution.py:185
  26.4 17.0 %collective-permute-start.8 = (bf16[256,1024]{1,0:T(8,128)(2,1)S(1)}, bf16[256,1024]{1,0:T(8,128)(2,1)S(1)}, u32[]{:S(2)}, u32[]{:S(2)}) collective-permute-start(bf16[256,1024]{1,0:T(8,128)(2,1)S(1)} %copy-done.25), channel_id=1, source_target_pairs={{0,1},{1,0},{2,3},{3,2},{4,5},{5,4},{6,7},{7,6},{8,9},{9,8},{10,11... | collective-permute-start | bytes 1572872 | tf_op jit(solution)/shard_map/ppermute | solution.py:185
  26.4 17.4 %collective-permute-start.9 = (bf16[256,1024]{1,0:T(8,128)(2,1)S(1)}, bf16[256,1024]{1,0:T(8,128)(2,1)S(1)}, u32[]{:S(2)}, u32[]{:S(2)}) collective-permute-start(bf16[256,1024]{1,0:T(8,128)(2,1)S(1)} %collective-permute-done.7.refs_11_), channel_id=1, source_target_pairs={{0,1},{1,0},{2,3},{3,2},{4,5},{5,4},{6,7},{7,6},{8,9},{9,8},{10,11... | collective-permute-start | bytes 1572872 | tf_op jit(solution)/shard_map/ppermute | solution.py:185
  56.4 11.2 %collective-permute-start.11 = (bf16[192,1024]{1,0:T(8,128)(2,1)S(1)}, bf16[192,1024]{1,0:T(8,128)(2,1)S(1)}, u32[]{:S(2)}, u32[]{:S(2)}) collective-permute-start(bf16[192,1024]{1,0:T(8,128)(2,1)S(1)} %get-tuple-element.208.refs_0_), channel_id=1, source_target_pairs={{0,2},{1,3},{2,0},{3,1},{4,6},{5,7},{6,4},{7,5},{8,10},{9,11},{10,... | collective-permute-start | bytes 1179656 | tf_op jit(solution)/shard_map/ppermute | solution.py:185
  57.1 17.9 %collective-permute-start.15 = (bf16[704,512]{1,0:T(8,128)(2,1)S(1)}, bf16[704,512]{1,0:T(8,128)(2,1)S(1)}, u32[]{:S(2)}, u32[]{:S(2)}) collective-permute-start(bf16[704,512]{1,0:T(8,128)(2,1)S(1)} %get-tuple-element.221), channel_id=1, source_target_pairs={{0,8},{4,12},{8,0},{12,4},{16,24},{20,28},{24,16},{28,20},{1,9},{5... | collective-permute-start | bytes 2162696 | tf_op jit(solution)/shard_map/ppermute | solution.py:185
  58.3 17.6 %collective-permute-start.14 = (bf16[704,512]{1,0:T(8,128)(2,1)S(1)}, bf16[704,512]{1,0:T(8,128)(2,1)S(1)}, u32[]{:S(2)}, u32[]{:S(2)}) collective-permute-start(bf16[704,512]{1,0:T(8,128)(2,1)S(1)} %get-tuple-element.219), channel_id=1, source_target_pairs={{0,4},{4,0},{8,12},{12,8},{16,20},{20,16},{24,28},{28,24},{1,5},{5... | collective-permute-start | bytes 2162696 | tf_op jit(solution)/shard_map/ppermute | solution.py:185
  74.2 15.8 %collective-permute-start.13 = (bf16[192,1024]{1,0:T(8,128)(2,1)S(1)}, bf16[192,1024]{1,0:T(8,128)(2,1)S(1)}, u32[]{:S(2)}, u32[]{:S(2)}) collective-permute-start(bf16[192,1024]{1,0:T(8,128)(2,1)S(1)} %get-tuple-element.217), channel_id=1, source_target_pairs={{0,1},{1,0},{2,3},{3,2},{4,5},{5,4},{6,7},{7,6},{8,9},{9,8},{10,11... | collective-permute-start | bytes 1179656 | tf_op jit(solution)/shard_map/ppermute | solution.py:185
  76.0 13.9 %collective-permute-start.16 = (bf16[704,256]{1,0:T(8,128)(2,1)S(1)}, bf16[704,256]{1,0:T(8,128)(2,1)S(1)}, u32[]{:S(2)}, u32[]{:S(2)}) collective-permute-start(bf16[704,256]{1,0:T(8,128)(2,1)S(1)} %get-tuple-element.225), channel_id=1, source_target_pairs={{0,8},{4,12},{8,0},{12,4},{16,24},{20,28},{24,16},{28,20},{1,9},{5... | collective-permute-start | bytes 1081352 | tf_op jit(solution)/shard_map/ppermute | solution.py:185
  81.8 34.6 %collective-permute-start.27 = (bf16[704,512]{1,0:T(8,128)(2,1)S(1)}, bf16[704,512]{1,0:T(8,128)(2,1)S(1)}, u32[]{:S(2)}, u32[]{:S(2)}) collective-permute-start(bf16[704,512]{1,0:T(8,128)(2,1)S(1)} %get-tuple-element.279), channel_id=1, source_target_pairs={{0,4},{4,0},{8,12},{12,8},{16,20},{20,16},{24,28},{28,24},{1,5},{5... | collective-permute-start | bytes 2162696 | tf_op jit(solution)/shard_map/ppermute | solution.py:185
  83.7 18.6 %collective-permute-start.21 = (bf16[704,256]{1,0:T(8,128)(2,1)S(1)}, bf16[704,256]{1,0:T(8,128)(2,1)S(1)}, u32[]{:S(2)}, u32[]{:S(2)}) collective-permute-start(bf16[704,256]{1,0:T(8,128)(2,1)S(1)} %get-tuple-element.252), channel_id=1, source_target_pairs={{0,16},{4,20},{8,24},{12,28},{16,0},{20,4},{24,8},{28,12},{1,17},{... | collective-permute-start | bytes 1081352 | tf_op jit(solution)/shard_map/ppermute | solution.py:185
  90.2 21.5 %collective-permute-start.18 = (bf16[192,1024]{1,0:T(8,128)(2,1)S(1)}, bf16[192,1024]{1,0:T(8,128)(2,1)S(1)}, u32[]{:S(2)}, u32[]{:S(2)}) collective-permute-start(bf16[192,1024]{1,0:T(8,128)(2,1)S(1)} %get-tuple-element.238.refs_0_), channel_id=1, source_target_pairs={{0,2},{1,3},{2,0},{3,1},{4,6},{5,7},{6,4},{7,5},{8,10},{9,11},{10,... | collective-permute-start | bytes 1179656 | tf_op jit(solution)/shard_map/ppermute | solution.py:185
  97.1 30.3 %collective-permute-start.26 = (bf16[512,768]{1,0:T(8,128)(2,1)S(1)}, bf16[512,768]{1,0:T(8,128)(2,1)S(1)}, u32[]{:S(2)}, u32[]{:S(2)}) collective-permute-start(bf16[512,768]{1,0:T(8,128)(2,1)S(1)} %get-tuple-element.277), channel_id=1, source_target_pairs={{0,4},{4,0},{8,12},{12,8},{16,20},{20,16},{24,28},{28,24},{1,5},{5... | collective-permute-start | bytes 2359304 | tf_op jit(solution)/shard_map/ppermute | solution.py:185
  116.3 12.0 %collective-permute-start.25 = (bf16[192,1024]{1,0:T(8,128)(2,1)S(1)}, bf16[192,1024]{1,0:T(8,128)(2,1)S(1)}, u32[]{:S(2)}, u32[]{:S(2)}) collective-permute-start(bf16[192,1024]{1,0:T(8,128)(2,1)S(1)} %get-tuple-element.275), channel_id=1, source_target_pairs={{0,1},{1,0},{2,3},{3,2},{4,5},{5,4},{6,7},{7,6},{8,9},{9,8},{10,11... | collective-permute-start | bytes 1179656 | tf_op jit(solution)/shard_map/ppermute | solution.py:185
  116.5 10.9 %collective-permute-start.28 = (bf16[704,256]{1,0:T(8,128)(2,1)S(1)}, bf16[704,256]{1,0:T(8,128)(2,1)S(1)}, u32[]{:S(2)}, u32[]{:S(2)}) collective-permute-start(bf16[704,256]{1,0:T(8,128)(2,1)S(1)} %get-tuple-element.282), channel_id=1, source_target_pairs={{0,8},{4,12},{8,0},{12,4},{16,24},{20,28},{24,16},{28,20},{1,9},{5... | collective-permute-start | bytes 1081352 | tf_op jit(solution)/shard_map/ppermute | solution.py:185
  118.5 14.0 %collective-permute-start.23 = (bf16[192,1024]{1,0:T(8,128)(2,1)S(1)}, bf16[192,1024]{1,0:T(8,128)(2,1)S(1)}, u32[]{:S(2)}, u32[]{:S(2)}) collective-permute-start(bf16[192,1024]{1,0:T(8,128)(2,1)S(1)} %get-tuple-element.270.refs_0_), channel_id=1, source_target_pairs={{0,1},{1,0},{2,3},{3,2},{4,5},{5,4},{6,7},{7,6},{8,9},{9,8},{10,11... | collective-permute-start | bytes 1179656 | tf_op jit(solution)/shard_map/ppermute | solution.py:185
  123.1 19.4 %collective-permute-start.33 = (bf16[528,512]{1,0:T(8,128)(2,1)S(1)}, bf16[528,512]{1,0:T(8,128)(2,1)S(1)}, u32[]{:S(2)}, u32[]{:S(2)}) collective-permute-start(bf16[528,512]{1,0:T(8,128)(2,1)S(1)} %get-tuple-element.300), channel_id=1, source_target_pairs={{0,4},{4,0},{8,12},{12,8},{16,20},{20,16},{24,28},{28,24},{1,5},{5... | collective-permute-start | bytes 1622024 | tf_op jit(solution)/shard_map/ppermute | solution.py:185
  127.5 19.5 %collective-permute-start.32 = (bf16[256,768]{1,0:T(8,128)(2,1)S(1)}, bf16[256,768]{1,0:T(8,128)(2,1)S(1)}, u32[]{:S(2)}, u32[]{:S(2)}) collective-permute-start(bf16[256,768]{1,0:T(8,128)(2,1)S(1)} %get-tuple-element.298), channel_id=1, source_target_pairs={{0,8},{4,12},{8,0},{12,4},{16,24},{20,28},{24,16},{28,20},{1,9},{5... | collective-permute-start | bytes 1179656 | tf_op jit(solution)/shard_map/ppermute | solution.py:185
  128.4 19.5 %collective-permute-start.30 = (bf16[192,1024]{1,0:T(8,128)(2,1)S(1)}, bf16[192,1024]{1,0:T(8,128)(2,1)S(1)}, u32[]{:S(2)}, u32[]{:S(2)}) collective-permute-start(bf16[192,1024]{1,0:T(8,128)(2,1)S(1)} %get-tuple-element.294.refs_0_), channel_id=1, source_target_pairs={{0,2},{1,3},{2,0},{3,1},{4,6},{5,7},{6,4},{7,5},{8,10},{9,11},{10,... | collective-permute-start | bytes 1179656 | tf_op jit(solution)/shard_map/ppermute | solution.py:185
  129.7 12.1 %collective-permute-start.34 = (bf16[704,128]{1,0:T(8,128)(2,1)S(1)}, bf16[704,128]{1,0:T(8,128)(2,1)S(1)}, u32[]{:S(2)}, u32[]{:S(2)}) collective-permute-start(bf16[704,128]{1,0:T(8,128)(2,1)S(1)} %get-tuple-element.302), channel_id=1, source_target_pairs={{0,16},{4,20},{8,24},{12,28},{16,0},{20,4},{24,8},{28,12},{1,17},{... | collective-permute-start | bytes 540680 | tf_op jit(solution)/shard_map/ppermute | solution.py:185
  132.5 14.7 %collective-permute-start.31 = (bf16[704,128]{1,0:T(8,128)(2,1)S(1)}, bf16[704,128]{1,0:T(8,128)(2,1)S(1)}, u32[]{:S(2)}, u32[]{:S(2)}) collective-permute-start(bf16[704,128]{1,0:T(8,128)(2,1)S(1)} %get-tuple-element.296), channel_id=1, source_target_pairs={{0,16},{4,20},{8,24},{12,28},{16,0},{20,4},{24,8},{28,12},{1,17},{... | collective-permute-start | bytes 540680 | tf_op jit(solution)/shard_map/ppermute | solution.py:185
  142.6 10.3 %collective-permute-start.38 = (bf16[272,512]{1,0:T(8,128)(2,1)S(1)}, bf16[272,512]{1,0:T(8,128)(2,1)S(1)}, u32[]{:S(2)}, u32[]{:S(2)}) collective-permute-start(bf16[272,512]{1,0:T(8,128)(2,1)S(1)} %get-tuple-element.315), channel_id=1, source_target_pairs={{0,8},{4,12},{8,0},{12,4},{16,24},{20,28},{24,16},{28,20},{1,9},{5... | collective-permute-start | bytes 835592 | tf_op jit(solution)/shard_map/ppermute | solution.py:185
  148.0 16.9 %collective-permute-start.35 = (bf16[192,1024]{1,0:T(8,128)(2,1)S(1)}, bf16[192,1024]{1,0:T(8,128)(2,1)S(1)}, u32[]{:S(2)}, u32[]{:S(2)}) collective-permute-start(bf16[192,1024]{1,0:T(8,128)(2,1)S(1)} %get-tuple-element.308.refs_0_), channel_id=1, source_target_pairs={{0,1},{1,0},{2,3},{3,2},{4,5},{5,4},{6,7},{7,6},{8,9},{9,8},{10,11... | collective-permute-start | bytes 1179656 | tf_op jit(solution)/shard_map/ppermute | solution.py:185
  148.1 16.0 %collective-permute-start.36 = (bf16[128,768]{1,0:T(8,128)(2,1)S(1)}, bf16[128,768]{1,0:T(8,128)(2,1)S(1)}, u32[]{:S(2)}, u32[]{:S(2)}) collective-permute-start(bf16[128,768]{1,0:T(8,128)(2,1)S(1)} %get-tuple-element.311), channel_id=1, source_target_pairs={{0,16},{4,20},{8,24},{12,28},{16,0},{20,4},{24,8},{28,12},{1,17},{... | collective-permute-start | bytes 589832 | tf_op jit(solution)/shard_map/ppermute | solution.py:185
  153.0 14.0 %collective-permute-start.39 = (bf16[144,512]{1,0:T(8,128)(2,1)S(1)}, bf16[144,512]{1,0:T(8,128)(2,1)S(1)}, u32[]{:S(2)}, u32[]{:S(2)}) collective-permute-start(bf16[144,512]{1,0:T(8,128)(2,1)S(1)} %get-tuple-element.322), channel_id=1, source_target_pairs={{0,16},{4,20},{8,24},{12,28},{16,0},{20,4},{24,8},{28,12},{1,17},{... | collective-permute-start | bytes 442376 | tf_op jit(solution)/shard_map/ppermute | solution.py:185
  (52 other events, 490.4 us)
